TPU v7x, 256 devices: a whole 4x4x8 slice. The times are simulated.
256 devices in a mesh: sx: 8 (over z), sy: 16 (over y, x), dp: 2 (over core).
Axes of the slice: x: 4, y: 4, z: 8, core: 2. Of those that a mesh axis runs over, the one named last changes fastest.
Arguments:
- features: bfloat16 [2, 64, 128, 4, 8, 128], P('dp', 'sx', 'sy'), may hold values from -6 to 6
- cotangent: bfloat16 [2, 64, 128, 4, 8, 128], P('dp', 'sx', 'sy'), may hold values from -6 to 6
- first_weight: bfloat16 [27, 128, 128], replicated, may hold values from -0.109375 to 0.109375
- second_weight: bfloat16 [27, 128, 128], replicated, may hold values from -0.109375 to 0.109375
- neighbours: int32 [2, 8, 16, 4, 26], P('dp', 'sx', 'sy'), may hold values from -1 to 3, as said below
- counts: int32 [2, 8, 16], P('dp', 'sx', 'sy'), may hold values from 1 to 4, as said below
Outputs:
- out_field: bfloat16 [2, 64, 128, 4, 8, 128], P('dp', 'sx', 'sy')
- grad_input: bfloat16 [2, 64, 128, 4, 8, 128], P('dp', 'sx', 'sy')
- grad_first: float32 [27, 128, 128], replicated
- grad_second: float32 [27, 128, 128], replicated
Inputs may be any that keep to these rules, and one draw needn't show every extreme that they name: Entries name only live slots; slots at or above a column's count have no neighbours; the relation is symmetric: if slot s of column (i, j) names slot t in direction d, then slot t of column (i+dx, j+dy) names s in the opposite direction, and the blocks are adjacent in space; columns outside the grid are never named. `counts`: some column of every workpiece has 4 live slots.
All inputs are finite; a program needn't handle non-finite values.
Results may differ from a plain program's by a relative error of at most 0.012.
Values may be sent and summed in bfloat16 or wider, within the bound.
No kernel may reach another device: no remote copies, remote signals or barrier semaphores. Data moves between devices by JAX's collectives and lax.ppermute only.
A program may use at most 192 MiB of HBM per device.

v0:
```python
import jax
import jax.numpy as jnp
from jax import lax
from jax.sharding import PartitionSpec as P


def with_halo(cells, sides, width):
    for axis, dim in sides:
        count = lax.axis_size(axis)
        ends = count - 1
        head = lax.slice_in_dim(cells, 0, width, axis=dim)
        tail = lax.slice_in_dim(cells, cells.shape[dim] - width, cells.shape[dim], axis=dim)
        cells = jnp.concatenate(
            [
                lax.ppermute(tail, axis, [(i, (i + 1) % count) for i in range(ends)]),
                cells,
                lax.ppermute(head, axis, [((i + 1) % count, i) for i in range(ends)]),
            ],
            axis=dim,
        )
    return cells


def padded_blocks(halo_field, neighbour):
    block_edge = halo_field.shape[0] - 2
    ranges_xy = [(0, 1), (1, block_edge + 1), (block_edge + 1, block_edge + 2)]
    ranges_z = [(block_edge - 1, block_edge), (0, block_edge), (0, 1)]
    planes = []
    for shift_x in range(3):
        row_list = []
        for shift_y in range(3):
            slab_list = []
            for shift_z in range(3):
                direction = shift_x * 9 + shift_y * 3 + shift_z
                low_x, high_x = ranges_xy[shift_x]
                low_y, high_y = ranges_xy[shift_y]
                low_z, high_z = ranges_z[shift_z]
                region = halo_field[low_x:high_x, low_y:high_y, :, low_z:high_z]
                if direction == 13:
                    slab_piece = region
                else:
                    entry = direction if direction < 13 else direction - 1
                    target = neighbour[:, entry]
                    valid = (target >= 0).astype(region.dtype)[None, None, :, None, None]
                    slab_piece = jnp.take(region, jnp.maximum(target, 0), axis=2) * valid
                slab_list.append(slab_piece)
            row_list.append(jnp.concatenate(slab_list, axis=3))
        planes.append(jnp.concatenate(row_list, axis=1))
    return jnp.concatenate(planes, axis=0)


def patch_matrix(padded, block_edge):
    pieces = []
    for shift_x in range(3):
        for shift_y in range(3):
            for shift_z in range(3):
                pieces.append(
                    padded[
                        shift_x : shift_x + block_edge,
                        shift_y : shift_y + block_edge,
                        :,
                        shift_z : shift_z + block_edge,
                    ]
                )
    stacked = jnp.concatenate(pieces, axis=-1)
    return stacked.reshape(-1, stacked.shape[-1])


def flipped_weight(weight):
    return jnp.transpose(weight[::-1], (0, 2, 1))


def silu_slope(values):
    logistic = jax.nn.sigmoid(values)
    return logistic * (1.0 + values * (1.0 - logistic))


def exchanged(values, neighbour):
    halo_field = with_halo(values, (("sx", 0), ("sy", 1)), 1)
    return patch_matrix(padded_blocks(halo_field, neighbour), values.shape[0])


def convolve(columns, weight, shape):
    matrix = weight.reshape(-1, weight.shape[2])
    return jnp.dot(columns, matrix, preferred_element_type=jnp.float32).reshape(shape)


def weight_partial(columns, grads):
    channels = grads.shape[-1]
    term = lax.dot_general(
        columns,
        grads.reshape(-1, channels),
        (((0,), (0,)), ((), ())),
        preferred_element_type=jnp.float32,
    )
    return term.reshape(27, channels, channels)


def sum_gradients(first_part, second_part):
    first_total, second_total = lax.psum((first_part, second_part), ("sx", "sy", "dp"))
    return (first_total, second_total)


def shards(features, cotangent, first_weight, second_weight, neighbours, counts):
    voxels_in = features[0]
    upstream = cotangent[0]
    neighbour = neighbours[0, 0, 0]
    block_edge = voxels_in.shape[0]
    slot_count = voxels_in.shape[2]
    shape = voxels_in.shape
    grad_scale = float(
        lax.axis_size("sx") * lax.axis_size("sy") * lax.axis_size("dp") * slot_count * block_edge**3
    ) ** (-0.5)
    live_mask = (jnp.arange(slot_count, dtype=jnp.int32) < counts[0, 0, 0]).astype(jnp.float32)[
        None, None, :, None, None
    ]
    masked = voxels_in * live_mask.astype(voxels_in.dtype)
    input_columns = exchanged(masked, neighbour)
    pre_first = convolve(input_columns, first_weight, shape)
    hidden = (jax.nn.silu(pre_first) * live_mask).astype(jnp.bfloat16)
    hidden_columns = exchanged(hidden, neighbour)
    pre_second = convolve(hidden_columns, second_weight, shape)
    summed = masked.astype(jnp.float32) + pre_second
    out_block = (jax.nn.silu(summed) * live_mask).astype(jnp.bfloat16)
    back_second = (upstream.astype(jnp.float32) * silu_slope(summed) * live_mask).astype(
        jnp.bfloat16
    )
    second_part = weight_partial(hidden_columns, back_second)
    back_hidden = convolve(exchanged(back_second, neighbour), flipped_weight(second_weight), shape)
    back_first = (back_hidden * silu_slope(pre_first) * live_mask).astype(jnp.bfloat16)
    first_part = weight_partial(input_columns, back_first)
    first_total, second_total = sum_gradients(first_part, second_part)
    back_input = convolve(exchanged(back_first, neighbour), flipped_weight(first_weight), shape)
    input_block = ((back_second.astype(jnp.float32) + back_input) * live_mask).astype(jnp.bfloat16)
    return (out_block[None], input_block[None], first_total * grad_scale, second_total * grad_scale)


def solution(mesh):
    in_specs = (
        P("dp", "sx", "sy", None, None, None),
        P("dp", "sx", "sy", None, None, None),
        P(),
        P(),
        P("dp", "sx", "sy", None, None),
        P("dp", "sx", "sy"),
    )
    out_specs = (
        P("dp", "sx", "sy", None, None, None),
        P("dp", "sx", "sy", None, None, None),
        P(),
        P(),
    )
    return jax.shard_map(shards, mesh=mesh, in_specs=in_specs, out_specs=out_specs, check_vma=False)
```

profile of v0, /device:TPU:1, one launch (start us, length us, event | category | flops | bytes accessed | tf_op | source)
XLA Modules:
  0.0 636.8 jit_solution(4533185112222517016)
XLA Ops:
  8.5 1.2 bitcast_multiply_fusion
  10.3 1.3 collective-permute-start.1
  11.6 5.0 collective-permute-start
  16.6 1.9 maximum_reduce_fusion.8
  18.5 2.4 fusion.137
  22.3 1.2 maximum_reduce_fusion.25
  29.2 1.8 fusion.139
  47.5 1.3 copy.114
  49.8 1.3 copy.149
  55.2 1.2 pad_clamp_fusion.8
  56.5 1.3 collective-permute-start.3
  57.8 4.2 collective-permute-start.2
  84.2 1.6 maximum_maximum_fusion.9
  85.9 2.2 maximum_maximum_fusion
  94.9 1.1 slice_dynamic-update-slice_fusion.88
  100.0 1.1 fusion.14
  101.2 1.1 constant_dynamic-update-slice_fusion
  102.3 1.2 fusion.13
  111.1 3.2 maximum_maximum_fusion.1
  118.3 1.1 slice_dynamic-update-slice_fusion.76
  123.4 8.5 %multiply_convert_fusion.1 = (bf16[8,8,4,8,128]{4,3,2,1,0:T(8,128)(2,1)S(1)}, f32[8,8,4,8,128]{4,3,2,1,0:T(8,128)}) fusion(f32[4]{0:T(128)S(1)} %copy-done.57, bf16[8,8,4,8,3456]{4,3,2,1,0:T(8,128)(2,1)} %slice_dynamic-update-slice_fusion.72, bf16[3456,128,1,1,1]{1,0,4,3,2:T(8,128)(2,1)S(1)} %bitcast.657), kind=kOutput, calls=%fused_computation.133 | convolution fusion | flops 1813512192 | bytes 16613392 | tf_op jit(solution)/shard_map/dot_general | solution.py:85
  132.2 1.3 collective-permute-start.5
  133.5 4.2 collective-permute-start.4
  139.7 17.9 %copy.150 = bf16[3456,2048]{1,0:T(8,128)(2,1)} copy(bf16[3456,2048]{0,1:T(8,128)(2,1)} %bitcast.253) | data formatting | bytes 28311552 | tf_op jit(solution)/shard_map/dot_general | solution.py:90
  157.8 1.3 collective-permute-start.7
  159.1 4.0 collective-permute-start.6
  177.6 2.0 maximum_maximum_fusion.11
  179.6 2.2 maximum_maximum_fusion.2
  188.7 1.1 slice_dynamic-update-slice_fusion.64
  193.7 1.1 fusion.12
  195.7 1.2 fusion.11
  204.5 3.2 maximum_maximum_fusion.3
  211.8 1.1 slice_dynamic-update-slice_fusion.52
  216.9 10.1 %fusion.6 = (bf16[8,8,4,8,128]{4,3,2,1,0:T(8,128)(2,1)S(1)}, bf16[1,8,8,4,8,128]{5,4,3,2,1,0:T(8,128)(2,1)}) fusion(bf16[1,8,8,4,8,128]{5,4,3,2,1,0:T(8,128)(2,1)S(1)} %copy-done.60, f32[4]{0:T(128)S(1)} %copy-done.57, bf16[8,8,4,8,3456]{4,3,2,1,0:T(8,128)(2,1)} %slice_dynamic-update-slice_fusion.48, bf16[3456,128,1,1,1]{1,0,4,3,2:T(8,128)(2,1)S(1)} %bitcast.658, ...), kind=kOutput, calls=%fused_computation.130 | convolution fusion | flops 1816133632 | bytes 17137680 | tf_op jit(solution)/shard_map/dot_general | solution.py:85
  227.2 1.5 collective-permute-start.9
  228.7 4.2 collective-permute-start.8
  234.5 18.8 %copy.151 = bf16[3456,2048]{1,0:T(8,128)(2,1)} copy(bf16[3456,2048]{0,1:T(8,128)(2,1)} %bitcast.258) | data formatting | bytes 28311552 | tf_op jit(solution)/shard_map/dot_general | solution.py:90
  253.3 8.2 %fusion.180 = f32[27,128,128]{2,1,0:T(8,128)} fusion(bf16[27,128,2048]{2,1,0:T(8,128)(2,1)} %bitcast.651, bf16[2048,128,1]{1,0,2:T(8,128)(2,1)S(1)} %bitcast.648), kind=kOutput, calls=%fused_computation.762 | convolution fusion | flops 1811939328 | bytes 16449536 | tf_op jit(solution)/shard_map/dot_general | solution.py:90
  261.8 1.3 collective-permute-start.11
  263.1 4.0 collective-permute-start.10
  281.4 1.6 maximum_maximum_fusion.13
  283.0 2.2 maximum_maximum_fusion.4
  292.1 1.1 slice_dynamic-update-slice_fusion.40
  297.1 1.1 fusion.10
  299.1 1.2 fusion.9
  307.9 3.2 maximum_maximum_fusion.5
  315.1 1.1 slice_dynamic-update-slice_fusion.28
  320.2 9.1 %fusion.3 = bf16[8,8,4,8,128]{4,3,2,1,0:T(8,128)(2,1)S(1)} fusion(bf16[8,8,4,8,3456]{4,3,2,1,0:T(8,128)(2,1)} %slice_dynamic-update-slice_fusion.24, bf16[3456,128,1,1,1]{1,0,4,3,2:T(8,128)(2,1)S(1)} %bitcast.659, f32[8,8,4,8,128]{4,3,2,1,0:T(8,128)S(1)} %copy-done.61, f32[4]{0:T(128)S(1)} %copy-done.57), kind=kOutput, calls=%fused_computation.118 | convolution fusion | flops 1814560768 | bytes 16613392 | tf_op jit(solution)/shard_map/dot_general | solution.py:85
  329.6 1.3 collective-permute-start.13
  330.9 5.6 collective-permute-start.12
  338.1 8.2 %fusion.179 = f32[27,128,128]{2,1,0:T(8,128)} fusion(bf16[27,128,2048]{2,1,0:T(8,128)(2,1)} %bitcast.650, bf16[2048,128,1]{1,0,2:T(8,128)(2,1)S(1)} %bitcast.649), kind=kOutput, calls=%fused_computation.761 | convolution fusion | flops 1811939328 | bytes 16449536 | tf_op jit(solution)/shard_map/dot_general | solution.py:90
  346.6 1.3 collective-permute-start.15
  347.9 5.1 collective-permute-start.14
  367.3 1.6 maximum_maximum_fusion.15
  368.9 2.2 maximum_maximum_fusion.6
  381.9 1.1 slice_dynamic-update-slice_fusion.12
  385.0 1.1 fusion.7
  388.1 1.1 slice_dynamic-update-slice_fusion.9
  393.8 3.2 maximum_maximum_fusion.7
  399.0 1.1 slice_dynamic-update-slice_fusion.6
  406.1 8.3 %fusion.4 = bf16[1,8,8,4,8,128]{5,4,3,2,1,0:T(8,128)(2,1)} fusion(bf16[8,8,4,8,3456]{4,3,2,1,0:T(8,128)(2,1)} %slice_dynamic-update-slice_fusion, bf16[3456,128,1,1,1]{1,0,4,3,2:T(8,128)(2,1)S(1)} %bitcast.656, bf16[8,8,4,8,128]{4,3,2,1,0:T(8,128)(2,1)S(1)} %get-tuple-element.65, f32[4]{0:T(128)S(1)} %copy-done.57), kind=kOutput, calls=%fused_computation.119 | convolution fusion | flops 1812987904 | bytes 16089104 | tf_op jit(solution)/shard_map/dot_general | solution.py:85
  414.4 210.9 %all-reduce.3.cloned.1.call-done = (f32[27,128,128]{2,1,0:T(8,128)}, f32[27,128,128]{2,1,0:T(8,128)}) async-done(((f32[27,128,128]{2,1,0:T(8,128)}, f32[27,128,128]{2,1,0:T(8,128)}), (f32[27,128,128]{2,1,0:T(8,128)}, f32[27,128,128]{2,1,0:T(8,128)})) %all-reduce.3.cloned.1.call-update) | async-done | bytes 3538960 | tf_op jit(solution)/shard_map/psum | solution.py:100
  625.3 3.1 broadcast_multiply_fusion.1
  628.4 1.4 broadcast_multiply_fusion
  (621 shorter events, 208.9 us)
Async XLA Ops:
  7.2 40.3 %copy-start.3 = (bf16[27,128,128]{2,1,0:T(8,128)(2,1)S(1)}, bf16[27,128,128]{2,1,0:T(8,128)(2,1)}, u32[]{:S(2)}) copy-start(bf16[27,128,128]{2,1,0:T(8,128)(2,1)} %param.23) | copy-start | bytes 2654212
  7.2 618.1 %all-reduce.3.cloned.1.call-start = ((), (), s32[]{:S(2)}) async-start(), calls=%async_computation | async-start | bytes 7077888 | tf_op jit(solution)/shard_map/psum | solution.py:100
  8.5 41.3 %copy-start.2 = (bf16[27,128,128]{2,1,0:T(8,128)(2,1)S(1)}, bf16[27,128,128]{2,1,0:T(8,128)(2,1)}, u32[]{:S(2)}) copy-start(bf16[27,128,128]{2,1,0:T(8,128)(2,1)} %param.22) | copy-start | bytes 2654212
  10.3 46.1 %collective-permute-start.1 = (bf16[1,8,4,8,128]{4,3,2,1,0:T(8,128)(2,1)}, bf16[1,8,4,8,128]{4,3,2,1,0:T(8,128)(2,1)S(1)}, u32[]{:S(2)}, u32[]{:S(2)}) collective-permute-start(bf16[1,8,4,8,128]{4,3,2,1,0:T(8,128)(2,1)} %get-tuple-element.98), channel_id=1, source_target_pairs={{32,0},{64,32},{96,64},{128,96},{160,128},{192,160},{224,192},{33,... | collective-permute-start | bytes 196616 | tf_op jit(solution)/shard_map/ppermute | solution.py:17
  11.6 44.8 %collective-permute-start = (bf16[1,8,4,8,128]{4,3,2,1,0:T(8,128)(2,1)S(1)}, bf16[1,8,4,8,128]{4,3,2,1,0:T(8,128)(2,1)S(1)}, u32[]{:S(2)}, u32[]{:S(2)}) collective-permute-start(bf16[1,8,4,8,128]{4,3,2,1,0:T(8,128)(2,1)S(1)} %get-tuple-element.97), channel_id=1, source_target_pairs={{0,32},{32,64},{64,96},{96,128},{128,160},{160,192},{192,224},{1,3... | collective-permute-start | bytes 196616 | tf_op jit(solution)/shard_map/ppermute | solution.py:15
  51.2 26.0 %copy-start.12 = (bf16[4]{0:T(256)(128)(2,1)S(1)}, bf16[4]{0:T(256)(128)(2,1)}, u32[]{:S(2)}) copy-start(bf16[4]{0:T(256)(128)(2,1)} %get-tuple-element.28) | copy-start | bytes 28
  51.2 26.0 %copy-start.32 = (pred[4]{0:T(512)(128)(4,1)S(1)}, pred[4]{0:T(512)(128)(4,1)}, u32[]{:S(2)}) copy-start(pred[4]{0:T(512)(128)(4,1)} %get-tuple-element.209) | copy-start | bytes 16
  53.4 21.9 %copy-start.50 = (s32[1024]{0:T(1024)}, s32[1024]{0:T(1024)S(1)}, u32[]{:S(2)}) copy-start(s32[1024]{0:T(1024)S(1)} %get-tuple-element.220) | copy-start | bytes 12292
  53.4 32.4 %copy-start.51 = (s32[1024]{0:T(1024)}, s32[1024]{0:T(1024)S(1)}, u32[]{:S(2)}) copy-start(s32[1024]{0:T(1024)S(1)} %get-tuple-element.219) | copy-start | bytes 12292
  54.1 31.7 %copy-start.52 = (s32[1024]{0:T(1024)}, s32[1024]{0:T(1024)S(1)}, u32[]{:S(2)}) copy-start(s32[1024]{0:T(1024)S(1)} %get-tuple-element.222) | copy-start | bytes 12292
  54.1 31.7 %copy-start.53 = (s32[1024]{0:T(1024)}, s32[1024]{0:T(1024)S(1)}, u32[]{:S(2)}) copy-start(s32[1024]{0:T(1024)S(1)} %get-tuple-element.221) | copy-start | bytes 12292
  54.8 20.5 %copy-start.49 = (s32[1024]{0:T(1024)}, s32[1024]{0:T(1024)S(1)}, u32[]{:S(2)}) copy-start(s32[1024]{0:T(1024)S(1)} %get-tuple-element.223) | copy-start | bytes 12292
  54.8 31.0 %copy-start.48 = (s32[1024]{0:T(1024)}, s32[1024]{0:T(1024)S(1)}, u32[]{:S(2)}) copy-start(s32[1024]{0:T(1024)S(1)} %get-tuple-element.224) | copy-start | bytes 12292
  56.5 12.6 %collective-permute-start.3 = (bf16[10,1,4,8,128]{4,3,2,1,0:T(8,128)(2,1)S(1)}, bf16[10,1,4,8,128]{4,3,2,1,0:T(8,128)(2,1)S(1)}, u32[]{:S(2)}, u32[]{:S(2)}) collective-permute-start(bf16[10,1,4,8,128]{4,3,2,1,0:T(8,128)(2,1)S(1)} %get-tuple-element.82), channel_id=1, source_target_pairs={{2,0},{4,2},{6,4},{8,6},{10,8},{12,10},{14,12},{16,14},{18,16},{20... | collective-permute-start | bytes 245768 | tf_op jit(solution)/shard_map/ppermute | solution.py:17
  57.8 11.3 %collective-permute-start.2 = (bf16[10,1,4,8,128]{4,3,2,1,0:T(8,128)(2,1)S(1)}, bf16[10,1,4,8,128]{4,3,2,1,0:T(8,128)(2,1)S(1)}, u32[]{:S(2)}, u32[]{:S(2)}) collective-permute-start(bf16[10,1,4,8,128]{4,3,2,1,0:T(8,128)(2,1)S(1)} %get-tuple-element.81), channel_id=1, source_target_pairs={{0,2},{2,4},{4,6},{6,8},{8,10},{10,12},{12,14},{14,16},{16,18},{18... | collective-permute-start | bytes 245768 | tf_op jit(solution)/shard_map/ppermute | solution.py:15
  101.1 9.6 %copy-start.37 = (bf16[4]{0:T(256)(128)(2,1)S(1)}, bf16[4]{0:T(256)(128)(2,1)}, u32[]{:S(2)}) copy-start(bf16[4]{0:T(256)(128)(2,1)} %get-tuple-element.53) | copy-start | bytes 28
  101.1 9.6 %copy-start.42 = (pred[4]{0:T(512)(128)(4,1)S(1)}, pred[4]{0:T(512)(128)(4,1)}, u32[]{:S(2)}) copy-start(pred[4]{0:T(512)(128)(4,1)} %get-tuple-element.203) | copy-start | bytes 16
  101.1 9.7 %copy-start.36 = (bf16[4]{0:T(256)(128)(2,1)S(1)}, bf16[4]{0:T(256)(128)(2,1)}, u32[]{:S(2)}) copy-start(bf16[4]{0:T(256)(128)(2,1)} %get-tuple-element.49) | copy-start | bytes 28
  101.1 9.7 %copy-start.39 = (pred[4]{0:T(512)(128)(4,1)S(1)}, pred[4]{0:T(512)(128)(4,1)}, u32[]{:S(2)}) copy-start(pred[4]{0:T(512)(128)(4,1)} %get-tuple-element.207) | copy-start | bytes 16
  101.2 9.7 %copy-start.6 = (bf16[4]{0:T(256)(128)(2,1)S(1)}, bf16[4]{0:T(256)(128)(2,1)}, u32[]{:S(2)}) copy-start(bf16[4]{0:T(256)(128)(2,1)} %get-tuple-element.29) | copy-start | bytes 28
  101.2 9.7 %copy-start.24 = (pred[4]{0:T(512)(128)(4,1)S(1)}, pred[4]{0:T(512)(128)(4,1)}, u32[]{:S(2)}) copy-start(pred[4]{0:T(512)(128)(4,1)} %get-tuple-element.208) | copy-start | bytes 16
  101.2 9.8 %copy-start.16 = (bf16[4]{0:T(256)(128)(2,1)S(1)}, bf16[4]{0:T(256)(128)(2,1)}, u32[]{:S(2)}) copy-start(bf16[4]{0:T(256)(128)(2,1)} %get-tuple-element.8) | copy-start | bytes 28
  101.2 9.8 %copy-start.55 = (pred[4]{0:T(512)(128)(4,1)S(1)}, pred[4]{0:T(512)(128)(4,1)}, u32[]{:S(2)}) copy-start(pred[4]{0:T(512)(128)(4,1)} %compare_and_fusion.9) | copy-start | bytes 16
  132.2 25.5 %collective-permute-start.5 = (bf16[1,8,4,8,128]{4,3,2,1,0:T(8,128)(2,1)S(1)}, bf16[1,8,4,8,128]{4,3,2,1,0:T(8,128)(2,1)S(1)}, u32[]{:S(2)}, u32[]{:S(2)}) collective-permute-start(bf16[1,8,4,8,128]{4,3,2,1,0:T(8,128)(2,1)S(1)} %get-tuple-element.94), channel_id=1, source_target_pairs={{32,0},{64,32},{96,64},{128,96},{160,128},{192,160},{224,192},{33,... | collective-permute-start | bytes 196616 | tf_op jit(solution)/shard_map/ppermute | solution.py:17
  133.5 24.2 %collective-permute-start.4 = (bf16[1,8,4,8,128]{4,3,2,1,0:T(8,128)(2,1)S(1)}, bf16[1,8,4,8,128]{4,3,2,1,0:T(8,128)(2,1)S(1)}, u32[]{:S(2)}, u32[]{:S(2)}) collective-permute-start(bf16[1,8,4,8,128]{4,3,2,1,0:T(8,128)(2,1)S(1)} %get-tuple-element.93), channel_id=1, source_target_pairs={{0,32},{32,64},{64,96},{96,128},{128,160},{160,192},{192,224},{1,3... | collective-permute-start | bytes 196616 | tf_op jit(solution)/shard_map/ppermute | solution.py:15
  139.5 24.3 %copy-start.15 = (bf16[4]{0:T(256)(128)(2,1)S(1)}, bf16[4]{0:T(256)(128)(2,1)}, u32[]{:S(2)}) copy-start(bf16[4]{0:T(256)(128)(2,1)} %get-tuple-element.17) | copy-start | bytes 28
  139.5 24.3 %copy-start.31 = (pred[4]{0:T(512)(128)(4,1)S(1)}, pred[4]{0:T(512)(128)(4,1)}, u32[]{:S(2)}) copy-start(pred[4]{0:T(512)(128)(4,1)} %get-tuple-element.227) | copy-start | bytes 16
  139.5 25.8 %copy-start.14 = (bf16[4]{0:T(256)(128)(2,1)S(1)}, bf16[4]{0:T(256)(128)(2,1)}, u32[]{:S(2)}) copy-start(bf16[4]{0:T(256)(128)(2,1)} %get-tuple-element.15) | copy-start | bytes 28
  139.5 25.8 %copy-start.29 = (pred[4]{0:T(512)(128)(4,1)S(1)}, pred[4]{0:T(512)(128)(4,1)}, u32[]{:S(2)}) copy-start(pred[4]{0:T(512)(128)(4,1)} %get-tuple-element.229) | copy-start | bytes 16
  139.6 26.7 %copy-start.23 = (bf16[4]{0:T(256)(128)(2,1)S(1)}, bf16[4]{0:T(256)(128)(2,1)}, u32[]{:S(2)}) copy-start(bf16[4]{0:T(256)(128)(2,1)} %get-tuple-element.52) | copy-start | bytes 28
  139.6 26.7 %copy-start.35 = (pred[4]{0:T(512)(128)(4,1)S(1)}, pred[4]{0:T(512)(128)(4,1)}, u32[]{:S(2)}) copy-start(pred[4]{0:T(512)(128)(4,1)} %get-tuple-element.204) | copy-start | bytes 16
  139.6 28.2 %copy-start.22 = (bf16[4]{0:T(256)(128)(2,1)S(1)}, bf16[4]{0:T(256)(128)(2,1)}, u32[]{:S(2)}) copy-start(bf16[4]{0:T(256)(128)(2,1)} %get-tuple-element.50) | copy-start | bytes 28
  139.6 28.2 %copy-start.34 = (pred[4]{0:T(512)(128)(4,1)S(1)}, pred[4]{0:T(512)(128)(4,1)}, u32[]{:S(2)}) copy-start(pred[4]{0:T(512)(128)(4,1)} %get-tuple-element.206) | copy-start | bytes 16
  139.6 29.1 %copy-start.13 = (bf16[4]{0:T(256)(128)(2,1)S(1)}, bf16[4]{0:T(256)(128)(2,1)}, u32[]{:S(2)}) copy-start(bf16[4]{0:T(256)(128)(2,1)} %get-tuple-element.28) | copy-start | bytes 28
  139.6 29.1 %copy-start.33 = (pred[4]{0:T(512)(128)(4,1)S(1)}, pred[4]{0:T(512)(128)(4,1)}, u32[]{:S(2)}) copy-start(pred[4]{0:T(512)(128)(4,1)} %get-tuple-element.209) | copy-start | bytes 16
  139.6 30.7 %copy-start.11 = (bf16[4]{0:T(256)(128)(2,1)S(1)}, bf16[4]{0:T(256)(128)(2,1)}, u32[]{:S(2)}) copy-start(bf16[4]{0:T(256)(128)(2,1)} %get-tuple-element.26) | copy-start | bytes 28
  139.6 30.7 %copy-start.30 = (pred[4]{0:T(512)(128)(4,1)S(1)}, pred[4]{0:T(512)(128)(4,1)}, u32[]{:S(2)}) copy-start(pred[4]{0:T(512)(128)(4,1)} %get-tuple-element.211) | copy-start | bytes 16
  139.6 31.5 %copy-start.10 = (bf16[4]{0:T(256)(128)(2,1)S(1)}, bf16[4]{0:T(256)(128)(2,1)}, u32[]{:S(2)}) copy-start(bf16[4]{0:T(256)(128)(2,1)} %get-tuple-element.23) | copy-start | bytes 28
  139.7 31.5 %copy-start.28 = (pred[4]{0:T(512)(128)(4,1)S(1)}, pred[4]{0:T(512)(128)(4,1)}, u32[]{:S(2)}) copy-start(pred[4]{0:T(512)(128)(4,1)} %get-tuple-element.214) | copy-start | bytes 16
  157.6 15.1 %copy-start.9 = (bf16[4]{0:T(256)(128)(2,1)S(1)}, bf16[4]{0:T(256)(128)(2,1)}, u32[]{:S(2)}) copy-start(bf16[4]{0:T(256)(128)(2,1)} %get-tuple-element.21) | copy-start | bytes 28
  157.6 15.2 %copy-start.27 = (pred[4]{0:T(512)(128)(4,1)S(1)}, pred[4]{0:T(512)(128)(4,1)}, u32[]{:S(2)}) copy-start(pred[4]{0:T(512)(128)(4,1)} %get-tuple-element.216) | copy-start | bytes 16
  157.6 16.0 %copy-start.21 = (bf16[4]{0:T(256)(128)(2,1)S(1)}, bf16[4]{0:T(256)(128)(2,1)}, u32[]{:S(2)}) copy-start(bf16[4]{0:T(256)(128)(2,1)} %get-tuple-element.20) | copy-start | bytes 28
  157.6 16.0 %copy-start.46 = (pred[4]{0:T(512)(128)(4,1)S(1)}, pred[4]{0:T(512)(128)(4,1)}, u32[]{:S(2)}) copy-start(pred[4]{0:T(512)(128)(4,1)} %get-tuple-element.217) | copy-start | bytes 16
  157.6 16.7 %copy-start.8 = (bf16[4]{0:T(256)(128)(2,1)S(1)}, bf16[4]{0:T(256)(128)(2,1)}, u32[]{:S(2)}) copy-start(bf16[4]{0:T(256)(128)(2,1)} %get-tuple-element.19) | copy-start | bytes 28
  157.6 16.7 %copy-start.26 = (pred[4]{0:T(512)(128)(4,1)S(1)}, pred[4]{0:T(512)(128)(4,1)}, u32[]{:S(2)}) copy-start(pred[4]{0:T(512)(128)(4,1)} %get-tuple-element.218) | copy-start | bytes 16
  157.6 17.5 %copy-start.20 = (bf16[4]{0:T(256)(128)(2,1)S(1)}, bf16[4]{0:T(256)(128)(2,1)}, u32[]{:S(2)}) copy-start(bf16[4]{0:T(256)(128)(2,1)} %get-tuple-element.18) | copy-start | bytes 28
  157.6 17.5 %copy-start.47 = (pred[4]{0:T(512)(128)(4,1)S(1)}, pred[4]{0:T(512)(128)(4,1)}, u32[]{:S(2)}) copy-start(pred[4]{0:T(512)(128)(4,1)} %get-tuple-element.226) | copy-start | bytes 16
  157.6 18.3 %copy-start.19 = (bf16[4]{0:T(256)(128)(2,1)S(1)}, bf16[4]{0:T(256)(128)(2,1)}, u32[]{:S(2)}) copy-start(bf16[4]{0:T(256)(128)(2,1)} %get-tuple-element.14) | copy-start | bytes 28
  157.7 18.3 %copy-start.45 = (pred[4]{0:T(512)(128)(4,1)S(1)}, pred[4]{0:T(512)(128)(4,1)}, u32[]{:S(2)}) copy-start(pred[4]{0:T(512)(128)(4,1)} %get-tuple-element.230) | copy-start | bytes 16
  157.7 19.1 %copy-start.7 = (bf16[4]{0:T(256)(128)(2,1)S(1)}, bf16[4]{0:T(256)(128)(2,1)}, u32[]{:S(2)}) copy-start(bf16[4]{0:T(256)(128)(2,1)} %get-tuple-element.12) | copy-start | bytes 28
  157.7 19.1 %copy-start.54 = (pred[4]{0:T(512)(128)(4,1)S(1)}, pred[4]{0:T(512)(128)(4,1)}, u32[]{:S(2)}) copy-start(pred[4]{0:T(512)(128)(4,1)} %compare_and_fusion.25) | copy-start | bytes 16
  157.7 19.8 %copy-start.18 = (bf16[4]{0:T(256)(128)(2,1)S(1)}, bf16[4]{0:T(256)(128)(2,1)}, u32[]{:S(2)}) copy-start(bf16[4]{0:T(256)(128)(2,1)} %get-tuple-element.10) | copy-start | bytes 28
  157.7 19.8 %copy-start.44 = (pred[4]{0:T(512)(128)(4,1)S(1)}, pred[4]{0:T(512)(128)(4,1)}, u32[]{:S(2)}) copy-start(pred[4]{0:T(512)(128)(4,1)} %get-tuple-element.225) | copy-start | bytes 16
  157.8 10.2 %collective-permute-start.7 = (bf16[10,1,4,8,128]{4,3,2,1,0:T(8,128)(2,1)S(1)}, bf16[10,1,4,8,128]{4,3,2,1,0:T(8,128)(2,1)S(1)}, u32[]{:S(2)}, u32[]{:S(2)}) collective-permute-start(bf16[10,1,4,8,128]{4,3,2,1,0:T(8,128)(2,1)S(1)} %get-tuple-element.80), channel_id=1, source_target_pairs={{2,0},{4,2},{6,4},{8,6},{10,8},{12,10},{14,12},{16,14},{18,16},{20... | collective-permute-start | bytes 245768 | tf_op jit(solution)/shard_map/ppermute | solution.py:17
  159.1 11.3 %collective-permute-start.6 = (bf16[10,1,4,8,128]{4,3,2,1,0:T(8,128)(2,1)S(1)}, bf16[10,1,4,8,128]{4,3,2,1,0:T(8,128)(2,1)S(1)}, u32[]{:S(2)}, u32[]{:S(2)}) collective-permute-start(bf16[10,1,4,8,128]{4,3,2,1,0:T(8,128)(2,1)S(1)} %get-tuple-element.79), channel_id=1, source_target_pairs={{0,2},{2,4},{4,6},{6,8},{8,10},{10,12},{12,14},{14,16},{16,18},{18... | collective-permute-start | bytes 245768 | tf_op jit(solution)/shard_map/ppermute | solution.py:15
  194.8 9.6 %copy-start.56 = (pred[4]{0:T(512)(128)(4,1)S(1)}, pred[4]{0:T(512)(128)(4,1)}, u32[]{:S(2)}) copy-start(pred[4]{0:T(512)(128)(4,1)} %compare_and_fusion.9) | copy-start | bytes 16
  227.2 34.5 %collective-permute-start.9 = (bf16[1,8,4,8,128]{4,3,2,1,0:T(8,128)(2,1)S(1)}, bf16[1,8,4,8,128]{4,3,2,1,0:T(8,128)(2,1)S(1)}, u32[]{:S(2)}, u32[]{:S(2)}) collective-permute-start(bf16[1,8,4,8,128]{4,3,2,1,0:T(8,128)(2,1)S(1)} %get-tuple-element.90), channel_id=1, source_target_pairs={{32,0},{64,32},{96,64},{128,96},{160,128},{192,160},{224,192},{33,... | collective-permute-start | bytes 196616 | tf_op jit(solution)/shard_map/ppermute | solution.py:17
  228.7 33.0 %collective-permute-start.8 = (bf16[1,8,4,8,128]{4,3,2,1,0:T(8,128)(2,1)S(1)}, bf16[1,8,4,8,128]{4,3,2,1,0:T(8,128)(2,1)S(1)}, u32[]{:S(2)}, u32[]{:S(2)}) collective-permute-start(bf16[1,8,4,8,128]{4,3,2,1,0:T(8,128)(2,1)S(1)} %get-tuple-element.89), channel_id=1, source_target_pairs={{0,32},{32,64},{64,96},{96,128},{128,160},{160,192},{192,224},{1,3... | collective-permute-start | bytes 196616 | tf_op jit(solution)/shard_map/ppermute | solution.py:15
  261.8 10.1 %collective-permute-start.11 = (bf16[10,1,4,8,128]{4,3,2,1,0:T(8,128)(2,1)S(1)}, bf16[10,1,4,8,128]{4,3,2,1,0:T(8,128)(2,1)S(1)}, u32[]{:S(2)}, u32[]{:S(2)}) collective-permute-start(bf16[10,1,4,8,128]{4,3,2,1,0:T(8,128)(2,1)S(1)} %get-tuple-element.78), channel_id=1, source_target_pairs={{2,0},{4,2},{6,4},{8,6},{10,8},{12,10},{14,12},{16,14},{18,16},{20... | collective-permute-start | bytes 245768 | tf_op jit(solution)/shard_map/ppermute | solution.py:17
  263.1 11.2 %collective-permute-start.10 = (bf16[10,1,4,8,128]{4,3,2,1,0:T(8,128)(2,1)S(1)}, bf16[10,1,4,8,128]{4,3,2,1,0:T(8,128)(2,1)S(1)}, u32[]{:S(2)}, u32[]{:S(2)}) collective-permute-start(bf16[10,1,4,8,128]{4,3,2,1,0:T(8,128)(2,1)S(1)} %get-tuple-element.77), channel_id=1, source_target_pairs={{0,2},{2,4},{4,6},{6,8},{8,10},{10,12},{12,14},{14,16},{16,18},{18... | collective-permute-start | bytes 245768 | tf_op jit(solution)/shard_map/ppermute | solution.py:15
  329.6 17.0 %collective-permute-start.13 = (bf16[1,8,4,8,128]{4,3,2,1,0:T(8,128)(2,1)S(1)}, bf16[1,8,4,8,128]{4,3,2,1,0:T(8,128)(2,1)S(1)}, u32[]{:S(2)}, u32[]{:S(2)}) collective-permute-start(bf16[1,8,4,8,128]{4,3,2,1,0:T(8,128)(2,1)S(1)} %get-tuple-element.86), channel_id=1, source_target_pairs={{32,0},{64,32},{96,64},{128,96},{160,128},{192,160},{224,192},{33,... | collective-permute-start | bytes 196616 | tf_op jit(solution)/shard_map/ppermute | solution.py:17
  330.9 15.7 %collective-permute-start.12 = (bf16[1,8,4,8,128]{4,3,2,1,0:T(8,128)(2,1)S(1)}, bf16[1,8,4,8,128]{4,3,2,1,0:T(8,128)(2,1)S(1)}, u32[]{:S(2)}, u32[]{:S(2)}) collective-permute-start(bf16[1,8,4,8,128]{4,3,2,1,0:T(8,128)(2,1)S(1)} %get-tuple-element.85), channel_id=1, source_target_pairs={{0,32},{32,64},{64,96},{96,128},{128,160},{160,192},{192,224},{1,3... | collective-permute-start | bytes 196616 | tf_op jit(solution)/shard_map/ppermute | solution.py:15
  346.6 11.2 %collective-permute-start.15 = (bf16[10,1,4,8,128]{4,3,2,1,0:T(8,128)(2,1)S(1)}, bf16[10,1,4,8,128]{4,3,2,1,0:T(8,128)(2,1)S(1)}, u32[]{:S(2)}, u32[]{:S(2)}) collective-permute-start(bf16[10,1,4,8,128]{4,3,2,1,0:T(8,128)(2,1)S(1)} %get-tuple-element.76), channel_id=1, source_target_pairs={{2,0},{4,2},{6,4},{8,6},{10,8},{12,10},{14,12},{16,14},{18,16},{20... | collective-permute-start | bytes 245768 | tf_op jit(solution)/shard_map/ppermute | solution.py:17
  347.9 12.3 %collective-permute-start.14 = (bf16[10,1,4,8,128]{4,3,2,1,0:T(8,128)(2,1)S(1)}, bf16[10,1,4,8,128]{4,3,2,1,0:T(8,128)(2,1)S(1)}, u32[]{:S(2)}, u32[]{:S(2)}) collective-permute-start(bf16[10,1,4,8,128]{4,3,2,1,0:T(8,128)(2,1)S(1)} %get-tuple-element.75), channel_id=1, source_target_pairs={{0,2},{2,4},{4,6},{6,8},{8,10},{10,12},{12,14},{14,16},{16,18},{18... | collective-permute-start | bytes 245768 | tf_op jit(solution)/shard_map/ppermute | solution.py:15
  (15 other events, 96.6 us)
Sparse Core Ops, SparseCore 0:
  346.7 278.5 all-reduce.2
where the time goes:
time: 643 us; the launch traced here: 637 us
  local copies, waits for them, and re-layouts  213 us (33%)
  waiting for transfers between devices  211 us (33%)
  other arithmetic  96.8 us (15%)
  matrix products  52.5 us (8%)
  starting transfers between devices  46.7 us (7%)
  between operations  17.3 us (3%)
    psum x1, waiting for transfers between devices, sum_gradients(): lax.psum((first_part, second_part), ('sx', 'sy', 'dp'))  211 us
    unnamed x253, local copies, waits for them, and re-layouts  97.8 us
    gather x104, local copies, waits for them, and re-layouts, padded_blocks(): slab_piece = jnp.take(region, jnp.maximum(target, 0), axis=2) * valid  70.7 us
    dot_general x2, local copies, waits for them, and re-layouts, weight_partial(): lax.dot_general(columns, grads.reshape(-1, channels), (((0,), (0,)), ((),...  36.7 us
    ppermute x8, starting transfers between devices, with_halo(): lax.ppermute(tail, axis, [(i, (i + 1) % count) for i in range(ends)])  36.2 us
    dot_general x4, matrix products, convolve(): jnp.dot(columns, matrix, preferred_element_type=jnp.float32).reshape(shape)  36 us
    concatenate x8, other arithmetic, padded_blocks(): return jnp.concatenate(planes, axis=0)  21.7 us
    mul x104, other arithmetic, padded_blocks(): slab_piece = jnp.take(region, jnp.maximum(target, 0), axis=2) * valid  18.3 us
  transfers between devices with their start and end apart: 17, of which 1 were waited for; matrix products, arithmetic and copies ran while one was open for 28% of the time, Pallas kernels for 0%

commit v1 on v0

v1 whole, which is shorter than its diff:
```python
import functools

import jax
import jax.numpy as jnp
from jax import lax
from jax.experimental import pallas as pl
from jax.experimental.pallas import tpu as pltpu
from jax.sharding import PartitionSpec as P

C = 128
BE = 8
NB = 4
ROWS = NB * BE
ZERO = ROWS
F32 = jnp.float32
BF16 = jnp.bfloat16
COLUMNS = [(cx, cy) for cx in (-1, 0, 1) for cy in (-1, 0, 1)]
OWN = 4


def shift_pair(low, high, axis):
    ends = lax.axis_size(axis) - 1
    from_low = lax.ppermute(high, axis, [(i, i + 1) for i in range(ends)])
    from_high = lax.ppermute(low, axis, [(i + 1, i) for i in range(ends)])
    return from_low, from_high


def spans(halo):
    return {-1: (0, halo), 0: (halo, halo + BE), 1: (halo + BE, 2 * halo + BE)}


def build_patches(tab, field, put, halo, column, xs, ys):
    cx, cy = COLUMNS[column]
    row = lax.broadcasted_iota(jnp.int32, (1, BE, C), 1)
    for sx, (x0, x1) in spans(halo).items():
        xa, xb = max(x0, xs[0]), min(x1, xs[1] + 2)
        if xa >= xb:
            continue
        for sy, (y0, y1) in spans(halo).items():
            ya, yb = max(y0, ys[0]), min(y1, ys[1] + 2)
            if ya >= yb:
                continue
            first = (sx - cx + 1) * 9 + (sy - cy + 1) * 3
            offsets = [
                [pl.multiple_of(tab[column * C + s * 27 + first + j], BE) for j in range(3)]
                for s in range(NB)
            ]

            def line(x):
                parts = [[], [], []]
                for below, here, above in offsets:
                    v = field[x, ya:yb, pl.ds(here, BE), :]
                    lo = field[x, ya:yb, pl.ds(below, BE), :]
                    hi = field[x, ya:yb, pl.ds(above, BE), :]
                    parts[0].append(pltpu.roll(jnp.where(row == BE - 1, lo, v), 1, 1))
                    parts[1].append(v)
                    parts[2].append(pltpu.roll(jnp.where(row == 0, hi, v), BE - 1, 1))
                for j in range(3):
                    value = jnp.concatenate(parts[j], axis=1).astype(BF16)
                    put(x - xs[0], ya - ys[0], yb - ys[0], j * C, value)

            if xb - xa > 3:

                def body(x, unused):
                    line(x)
                    return unused

                lax.fori_loop(xa, xb, body, 0)
            else:
                for x in range(xa, xb):
                    line(x)


def into(ref, lead=None):
    def put(x, ya, yb, lane, value):
        if lead is None:
            ref[x, ya:yb, :, lane : lane + C] = value
        else:
            ref[lead, x, ya:yb, :, lane : lane + C] = value

    return put


def product(get, weight):
    parts = []
    for a in range(3):
        for b in range(3):
            piece = get(a, b)
            parts.append(piece.reshape(-1, piece.shape[-1]))
    return jnp.dot(jnp.concatenate(parts, axis=1), weight[...], preferred_element_type=F32)


def rounded(value):
    return value.astype(BF16).astype(F32)


def slope_of(value):
    sig = jax.nn.sigmoid(value)
    return sig * (1.0 + value * (1.0 - sig))


def live_rows(tab):
    parts = [
        jnp.where(tab[OWN * C + s * 27 + 13] < ZERO, jnp.ones((BE, C), F32), jnp.zeros((BE, C), F32))
        for s in range(NB)
    ]
    return jnp.concatenate(parts, axis=0)


def zero_slot(field):
    def body(x, unused):
        field[x, :, ZERO : ZERO + BE, :] = jnp.zeros((field.shape[1], BE, C), F32)
        return unused

    lax.fori_loop(0, field.shape[0], body, 0)


def rows_at(field, x, y, value):
    n, m = value.shape[:2]
    field[x : x + n, y : y + m, 0:ROWS, :] = value


def weight_grad(patch, grads, turned, out, base, scale):
    for x in range(BE):
        block = grads[x].reshape(BE * ROWS, C).astype(F32)
        turned[:, x * BE * ROWS : (x + 1) * BE * ROWS] = block.T.astype(BF16)

    def body(i, unused):
        a, b = i // 3, i % 3
        right = patch[pl.ds(a, BE), pl.ds(b, BE)].reshape(BE * BE * ROWS, 3 * C)
        term = jnp.dot(turned[...], right, preferred_element_type=F32) * scale
        for j in range(3):
            at = pl.multiple_of(base + (i * 3 + j) * C, C)
            out[pl.ds(at, C), :] = term[:, j * C : (j + 1) * C].T.astype(BF16)
        return unused

    lax.fori_loop(0, 9, body, 0)


def main_kernel(scale, tab, x, cot, xm, xp, ym, yp, w1, w2, w2f, out, b2o, b1o, gr,
                field, hid, back, p1, p2, px, py, pc, slope1, turned):
    live = live_rows(tab)
    for ref in (field, hid, back):
        zero_slot(ref)

    def fill(i, unused):
        field[3 + i, 3:11, 0:ROWS, :] = x[i].astype(F32)
        return unused

    lax.fori_loop(0, BE, fill, 0)
    for i in range(3):
        rows_at(field, i, 3, xm[8 * i : 8 * i + 8].astype(F32)[None])
        rows_at(field, 11 + i, 3, xp[8 * i : 8 * i + 8].astype(F32)[None])

    def fill_sides(i, unused):
        field[i, 0:3, 0:ROWS, :] = ym[pl.ds(3 * i, 3)].astype(F32)
        field[i, 11:14, 0:ROWS, :] = yp[pl.ds(3 * i, 3)].astype(F32)
        return unused

    lax.fori_loop(0, 14, fill_sides, 0)

    ends = spans(2)
    corners = [0, 2, 6, 8]
    build_patches(tab, field, into(p1), 3, OWN, ends[0], ends[0])
    for j, cx in enumerate((-1, 1)):
        build_patches(tab, field, into(px, j), 3, COLUMNS.index((cx, 0)), ends[cx], ends[0])
        build_patches(tab, field, into(py, j), 3, COLUMNS.index((0, cx)), ends[0], ends[cx])
    for j, c in enumerate(corners):
        build_patches(tab, field, into(pc, j), 3, c, ends[COLUMNS[c][0]], ends[COLUMNS[c][1]])

    def first_own(i, unused):
        pre = product(lambda a, b: p1[pl.ds(2 * i + a, 2), b : b + BE], w1)
        slope1[pl.ds(2 * i, 2)] = slope_of(pre).reshape(2, BE, ROWS, C)
        hid[pl.ds(2 + 2 * i, 2), 2:10, 0:ROWS, :] = rounded(pre * jax.nn.sigmoid(pre)).reshape(2, BE, ROWS, C)
        return unused

    lax.fori_loop(0, 4, first_own, 0)
    for j, at in enumerate((0, 10)):
        pre = product(lambda a, b: px[j, a : a + 2, b : b + BE], w1)
        rows_at(hid, at, 2, rounded(pre * jax.nn.sigmoid(pre)).reshape(2, BE, ROWS, C))
        pre = product(lambda a, b: py[j, a : a + BE, b : b + 2], w1)
        rows_at(hid, 2, at, rounded(pre * jax.nn.sigmoid(pre)).reshape(BE, 2, ROWS, C))
    pre = product(lambda a, b: pc[:, a : a + 2, b : b + 2], w1)
    value = rounded(pre * jax.nn.sigmoid(pre)).reshape(4, 2, 2, ROWS, C)
    for j, (ax, ay) in enumerate(((0, 0), (0, 10), (10, 0), (10, 10))):
        rows_at(hid, ax, ay, value[j])

    ends = spans(1)
    build_patches(tab, hid, into(p2), 2, OWN, ends[0], ends[0])
    for j, cx in enumerate((-1, 1)):
        build_patches(tab, hid, into(px, j), 2, COLUMNS.index((cx, 0)), ends[cx], ends[0])
        build_patches(tab, hid, into(py, j), 2, COLUMNS.index((0, cx)), ends[0], ends[cx])
    for j, c in enumerate(corners):
        build_patches(tab, hid, into(pc, j), 2, c, ends[COLUMNS[c][0]], ends[COLUMNS[c][1]])

    def second_own(i, unused):
        pre = product(lambda a, b: p2[pl.ds(2 * i + a, 2), b : b + BE], w2).reshape(2, BE, ROWS, C)
        total = field[pl.ds(3 + 2 * i, 2), 3:11, 0:ROWS, :] * live + pre
        sig = jax.nn.sigmoid(total)
        out[pl.ds(2 * i, 2)] = (total * sig * live).astype(BF16)
        slope = sig * (1.0 + total * (1.0 - sig))
        grad = (cot[pl.ds(2 * i, 2)].astype(F32) * slope * live).astype(BF16)
        b2o[pl.ds(2 * i, 2)] = grad
        back[pl.ds(1 + 2 * i, 2), 1:9, 0:ROWS, :] = grad.astype(F32)
        return unused

    lax.fori_loop(0, 4, second_own, 0)
    pre = product(lambda a, b: px[:, a : a + 1, b : b + BE], w2).reshape(2, BE, ROWS, C)
    for j, (at, cx, near) in enumerate(((2, 0, xm), (11, 9, xp))):
        total = field[at, 3:11, 0:ROWS, :] + pre[j]
        grad = near[24:32].astype(F32) * slope_of(total)
        rows_at(back, cx, 1, rounded(grad)[None])
    pre = product(lambda a, b: py[:, a : a + BE, b : b + 1], w2).reshape(2, BE, ROWS, C)
    for j, (at, cy, near) in enumerate(((2, 0, ym), (11, 9, yp))):
        total = field[3:11, at, 0:ROWS, :] + pre[j]
        grad = near[43:51].astype(F32) * slope_of(total)
        back[1:9, cy, 0:ROWS, :] = rounded(grad)
    pre = product(lambda a, b: pc[:, a : a + 1, b : b + 1], w2).reshape(4, ROWS, C)
    for j, (ax, ay, cx, cy, near, at) in enumerate(
        ((2, 2, 0, 0, ym, 42), (2, 11, 0, 9, yp, 42), (11, 2, 9, 0, ym, 51), (11, 11, 9, 9, yp, 51))
    ):
        total = field[ax, ay, 0:ROWS, :] + pre[j]
        grad = near[at].astype(F32) * slope_of(total)
        back[cx, cy, 0:ROWS, :] = rounded(grad)
    weight_grad(p2, b2o, turned, gr, 27 * C, scale)

    build_patches(tab, back, into(p2), 1, OWN, (0, BE), (0, BE))

    def third(i, unused):
        pre = product(lambda a, b: p2[pl.ds(2 * i + a, 2), b : b + BE], w2f).reshape(2, BE, ROWS, C)
        b1o[pl.ds(2 * i, 2)] = (pre * slope1[pl.ds(2 * i, 2)] * live).astype(BF16)
        return unused

    lax.fori_loop(0, 4, third, 0)
    weight_grad(p1, b1o, turned, gr, 0, scale)


def last_kernel(tab, b1, b2, xm, xp, ym, yp, w1f, out, field, patch):
    live = live_rows(tab)
    zero_slot(field)

    def fill(i, unused):
        field[1 + i, 1:9, 0:ROWS, :] = b1[i].astype(F32)
        return unused

    lax.fori_loop(0, BE, fill, 0)
    rows_at(field, 0, 1, xm[...].astype(F32)[None])
    rows_at(field, 9, 1, xp[...].astype(F32)[None])
    field[:, 0, 0:ROWS, :] = ym[...].astype(F32)
    field[:, 9, 0:ROWS, :] = yp[...].astype(F32)
    build_patches(tab, field, into(patch), 1, OWN, (0, BE), (0, BE))

    def step(i, unused):
        pre = product(lambda a, b: patch[pl.ds(2 * i + a, 2), b : b + BE], w1f).reshape(2, BE, ROWS, C)
        out[pl.ds(2 * i, 2)] = ((b2[pl.ds(2 * i, 2)].astype(F32) + pre) * live).astype(BF16)
        return unused

    lax.fori_loop(0, 4, step, 0)


def call(kernel, outs, scratch, cost, *args):
    smem = pl.BlockSpec(memory_space=pltpu.SMEM)
    vmem = pl.BlockSpec(memory_space=pltpu.VMEM)
    return pl.pallas_call(
        kernel,
        out_shape=outs,
        in_specs=[smem] + [vmem] * (len(args) - 1),
        out_specs=jax.tree.map(lambda o: vmem, outs),
        scratch_shapes=scratch,
        compiler_params=pltpu.CompilerParams(vmem_limit_bytes=48 * 2**20),
        cost_estimate=cost,
    )(*args)


def reduce_axis(part, axis):
    n = lax.axis_size(axis)
    swapped = lax.all_to_all(part.reshape(n, part.shape[0] // n, C), axis, 0, 0, tiled=True)
    return jnp.sum(swapped.astype(F32), axis=0).astype(BF16)


def gather_axis(part, axis):
    n = lax.axis_size(axis)
    copies = jnp.broadcast_to(part[None], (n,) + part.shape)
    return lax.all_to_all(copies, axis, 0, 0, tiled=True).reshape(n * part.shape[0], C)


def flipped_weight(weight):
    return jnp.transpose(weight[::-1], (0, 2, 1)).reshape(27 * C, C)


def shards(features, cotangent, first_weight, second_weight, neighbours, counts):
    x = features.reshape(BE, BE, ROWS, C)
    cot = cotangent.reshape(BE, BE, ROWS, C)
    n_devices = lax.axis_size("sx") * lax.axis_size("sy") * lax.axis_size("dp")
    scale = float(n_devices * NB * BE**3) ** -0.5

    links = neighbours.reshape(NB, 26)
    slots = jnp.arange(NB, dtype=jnp.int32)
    centre = jnp.where(slots < counts.reshape(()), slots, -1)[:, None]
    named = jnp.concatenate([links[:, :13], centre, links[:, 13:]], axis=1)
    starts = jnp.where(named < 0, NB, named) * BE
    table = jnp.pad(starts.reshape(NB * 27), (0, C - NB * 27))
    tline = jnp.broadcast_to(table.astype(BF16)[None, None], (1, ROWS, C))

    def lines(value):
        return value.reshape(-1, ROWS, C)

    low = jnp.concatenate([lines(x[0:3]), cot[0], tline], axis=0)
    high = jnp.concatenate([lines(x[5:8]), cot[7], tline], axis=0)
    xm, xp = shift_pair(low, high, "sx")
    xmf, xpf = (v[:24].reshape(3, BE, ROWS, C) for v in (xm, xp))

    def side(ys, y):
        return jnp.concatenate(
            [lines(xmf[:, ys]), lines(x[:, ys]), lines(xpf[:, ys]), xm[24 + y : 25 + y], cot[:, y], xp[24 + y : 25 + y],
             xm[32:33], tline, xp[32:33]],
            axis=0,
        )

    ym, yp = shift_pair(side(slice(0, 3), 0), side(slice(5, 8), 7), "sy")
    tabs = jnp.stack(
        [ym[52, 0], xm[32, 0], yp[52, 0], ym[53, 0], tline[0, 0], yp[53, 0], ym[54, 0], xp[32, 0], yp[54, 0]]
    ).astype(jnp.int32).reshape(9 * C)

    block = jax.ShapeDtypeStruct((BE, BE, ROWS, C), BF16)
    lanes = 3 * C
    unit = 2 * BE * BE * ROWS * 27 * C * C
    out, b2, b1, grads = call(
        functools.partial(main_kernel, scale),
        [block, block, block, jax.ShapeDtypeStruct((54 * C, C), BF16)],
        [
            pltpu.VMEM((14, 14, ROWS + BE, C), F32),
            pltpu.VMEM((12, 12, ROWS + BE, C), F32),
            pltpu.VMEM((10, 10, ROWS + BE, C), F32),
            pltpu.VMEM((10, 10, ROWS, lanes), BF16),
            pltpu.VMEM((10, 10, ROWS, lanes), BF16),
            pltpu.VMEM((2, 4, 10, ROWS, lanes), BF16),
            pltpu.VMEM((2, 10, 4, ROWS, lanes), BF16),
            pltpu.VMEM((4, 4, 4, ROWS, lanes), BF16),
            pltpu.VMEM((BE, BE, ROWS, C), F32),
            pltpu.VMEM((C, BE * BE * ROWS), BF16),
        ],
        pl.CostEstimate(flops=7 * unit, bytes_accessed=10 * 2**20, transcendentals=2**20),
        tabs, x, cot, xm, xp, ym, yp,
        first_weight.reshape(27 * C, C), second_weight.reshape(27 * C, C), flipped_weight(second_weight),
    )

    bxm, bxp = shift_pair(b1[0], b1[7], "sx")
    bym, byp = shift_pair(
        jnp.concatenate([bxm[0:1], b1[:, 0], bxp[0:1]], axis=0),
        jnp.concatenate([bxm[7:8], b1[:, 7], bxp[7:8]], axis=0),
        "sy",
    )
    grad_input = call(
        last_kernel,
        block,
        [pltpu.VMEM((10, 10, ROWS + BE, C), F32), pltpu.VMEM((10, 10, ROWS, lanes), BF16)],
        pl.CostEstimate(flops=unit, bytes_accessed=4 * 2**20, transcendentals=0),
        tabs, b1, b2, bxm, bxp, bym, byp, flipped_weight(first_weight),
    )

    for axis in ("dp", "sy", "sx"):
        grads = reduce_axis(grads, axis)
    for axis in ("sx", "sy", "dp"):
        grads = gather_axis(grads, axis)
    grads = grads.reshape(2, 27, C, C).astype(F32)
    shape = features.shape
    return out.reshape(shape), grad_input.reshape(shape), grads[0], grads[1]


def solution(mesh):
    column = P("dp", "sx", "sy", None, None, None)
    return jax.shard_map(
        shards,
        mesh=mesh,
        in_specs=(column, column, P(), P(), P("dp", "sx", "sy", None, None), P("dp", "sx", "sy")),
        out_specs=(column, column, P(), P()),
        check_vma=False,
    )
```

time: 643 us -> 185 us (0.29)
  local copies, waits for them, and re-layouts: 213 us -> 26.3 us
  waiting for transfers between devices: 211 us -> 30.5 us
  other arithmetic: 96.8 us -> 3.34 us
  matrix products: 52.5 us -> 0 us
  Pallas kernels: 0 us -> 43.6 us
  blocking collectives: 0 us -> 42.2 us
  between operations: 17.3 us -> 1.62 us
  starting transfers between devices: 46.7 us -> 35.4 us
    psum x1 -> x0, waiting for transfers between devices: 211 us -> none  [sum_gradients(): lax.psum((first_part, second_part), ('sx', 'sy', 'dp'))]
    unnamed x253 -> x39, local copies, waits for them, and re-layouts: 97.8 us -> 11.3 us
    gather x104 -> x0, local copies, waits for them, and re-layouts: 70.7 us -> none  [padded_blocks(): slab_piece = jnp.take(region, jnp.maximum(target, 0), axis=2) * valid]
    dot_general x6 -> x0, matrix products: 52.5 us -> none  [the longest x4 36 us: convolve(): jnp.dot(columns, matrix, preferred_element_type=jnp.float32).reshape(shape)]
    pallas_call x0 -> x2, Pallas kernels: none -> 43.6 us  [call(): pl.pallas_call(kernel, out_shape=outs, in_specs=[smem] + [vmem] * (len(ar...]
    all_to_all x0 -> x3, blocking collectives: none -> 42.2 us  [the longest x2 33.2 us: reduce_axis(): lax.all_to_all(part.reshape(n, part.shape[0] // n, C), axis, 0, 0, tiled=...]
    dot_general x2 -> x0, local copies, waits for them, and re-layouts: 36.7 us -> none  [weight_partial(): lax.dot_general(columns, grads.reshape(-1, channels), (((0,), (0,)), ((),...]
    concatenate x12 -> x4, other arithmetic: 28.3 us -> 0.81 us  [the longest x1 0.65 us: shards(): jnp.concatenate([bxm[0:1], b1[:, 0], bxp[0:1]], axis=0)]
  transfers between devices with their start and end apart: 17 -> 11, of which waited for: 1 -> 8; matrix products, arithmetic and copies ran while one was open for 28% -> 5% of each run, Pallas kernels for 0% -> 4%
where the time goes in v1:
time: 185 us; the launch traced here: 183 us
  Pallas kernels  43.6 us (24%)
  blocking collectives  42.2 us (23%)
  starting transfers between devices  35.4 us (19%)
  waiting for transfers between devices  30.5 us (16%)
  local copies, waits for them, and re-layouts  26.3 us (14%)
  other arithmetic  3.34 us (2%)
    pallas_call x2, Pallas kernels, call(): pl.pallas_call(kernel, out_shape=outs, in_specs=[smem] + [vmem] * (len(ar...  43.6 us
    all_to_all x2, blocking collectives, reduce_axis(): lax.all_to_all(part.reshape(n, part.shape[0] // n, C), axis, 0, 0, tiled=...  33.2 us
    ppermute x4, starting transfers between devices, shift_pair(): from_low = lax.ppermute(high, axis, [(i, i + 1) for i in range(ends)])  14.8 us
    ppermute x4, waiting for transfers between devices, shift_pair(): from_high = lax.ppermute(low, axis, [(i + 1, i) for i in range(ends)])  13 us
    unnamed x39, local copies, waits for them, and re-layouts  11.3 us
    all_to_all x1, blocking collectives, gather_axis(): lax.all_to_all(copies, axis, 0, 0, tiled=True).reshape(n * part.shape[0], C)  8.99 us
    all_to_all x2, starting transfers between devices, gather_axis(): lax.all_to_all(copies, axis, 0, 0, tiled=True).reshape(n * part.shape[0], C)  7.66 us
    all_to_all x1, starting transfers between devices, reduce_axis(): lax.all_to_all(part.reshape(n, part.shape[0] // n, C), axis, 0, 0, tiled=...  7.65 us
  transfers between devices with their start and end apart: 11, of which 8 were waited for; matrix products, arithmetic and copies ran while one was open for 5% of the time, Pallas kernels for 4%

profile of v1, /device:TPU:1, one launch (start us, length us, event | category | flops | bytes accessed | tf_op | source)
XLA Modules:
  0.0 183.0 jit_solution(1687478166679192235)
XLA Ops:
  0.6 0.0 copy-start.3
  0.6 0.0 copy-start
  0.7 0.9 fusion.11
  2.2 0.1 pad_add_fusion
  2.2 0.1 concatenate.24
  2.4 0.9 slice_bitcast_fusion.6
  3.2 1.1 fusion.6
  4.3 0.1 pad_maximum_fusion
  4.4 4.4 %collective-permute-start = (bf16[33,32,128]{2,1,0:T(8,128)(2,1)S(1)}, bf16[33,32,128]{2,1,0:T(8,128)(2,1)S(1)}, u32[]{:S(2)}, u32[]{:S(2)}) collective-permute-start(bf16[33,32,128]{2,1,0:T(8,128)(2,1)S(1)} %get-tuple-element.49), channel_id=1, source_target_pairs={{0,32},{32,64},{64,96},{96,128},{128,160},{160,192},{192,224},{1,3... | collective-permute-start | bytes 811016 | tf_op jit(solution)/shard_map/ppermute | solution.py:23
  8.8 1.3 collective-permute-start.1
  10.2 3.7 %collective-permute-done.xm = bf16[33,32,128]{2,1,0:T(8,128)(2,1)S(1)} collective-permute-done((bf16[33,32,128]{2,1,0:T(8,128)(2,1)S(1)}, bf16[33,32,128]{2,1,0:T(8,128)(2,1)S(1)}, u32[]{:S(2)}, u32[]{:S(2)}) %collective-permute-start) | collective-permute-done | bytes 270368 | tf_op jit(solution)/shard_map/ppermute | solution.py:23
  13.9 0.6 constant_dynamic-update-slice_fusion.7
  14.6 3.5 %collective-permute-done.1.xp = bf16[33,32,128]{2,1,0:T(8,128)(2,1)S(1)} collective-permute-done((bf16[33,32,128]{2,1,0:T(8,128)(2,1)S(1)}, bf16[33,32,128]{2,1,0:T(8,128)(2,1)S(1)}, u32[]{:S(2)}, u32[]{:S(2)}) %collective-permute-start.1) | collective-permute-done | bytes 270368 | tf_op jit(solution)/shard_map/ppermute | solution.py:24
  18.1 0.7 constant_dynamic-update-slice_fusion.6
  18.9 0.7 constant_dynamic-update-slice_fusion.5
  19.5 0.6 constant_dynamic-update-slice_fusion.12
  20.1 0.6 fusion
  20.8 0.6 constant_dynamic-update-slice_fusion.11
  21.4 0.6 constant_dynamic-update-slice_fusion.10
  22.0 0.6 constant_dynamic-update-slice_fusion.9
  22.6 0.6 constant_dynamic-update-slice_fusion.8
  23.2 0.8 copy-done.13
  23.9 4.0 %collective-permute-start.2 = (bf16[55,32,128]{2,1,0:T(8,128)(2,1)}, bf16[55,32,128]{2,1,0:T(8,128)(2,1)}, u32[]{:S(2)}, u32[]{:S(2)}) collective-permute-start(bf16[55,32,128]{2,1,0:T(8,128)(2,1)} %get-tuple-element.33), channel_id=1, source_target_pairs={{0,2},{2,4},{4,6},{6,8},{8,10},{10,12},{12,14},{14,16},{16,18},{18... | collective-permute-start | bytes 1351688 | tf_op jit(solution)/shard_map/ppermute | solution.py:23
  28.0 1.0 reverse_bitcast_fusion.1
  28.9 1.9 %copy.23 = bf16[27,128,128]{2,1,0:T(8,128)(2,1)S(1)} copy(bf16[27,128,128]{1,2,0:T(8,128)(2,1)} %reverse_bitcast_fusion.1) | data formatting | bytes 1769472 | tf_op jit(solution)/shard_map/transpose | solution.py:288
  30.8 1.3 collective-permute-start.3
  32.1 0.7 slice_bitcast_fusion.9
  32.8 2.6 %collective-permute-done.2.ym = bf16[55,32,128]{2,1,0:T(8,128)(2,1)} collective-permute-done((bf16[55,32,128]{2,1,0:T(8,128)(2,1)}, bf16[55,32,128]{2,1,0:T(8,128)(2,1)}, u32[]{:S(2)}, u32[]{:S(2)}) %collective-permute-start.2) | collective-permute-done | bytes 450592 | tf_op jit(solution)/shard_map/ppermute | solution.py:23
  35.4 0.7 slice_bitcast_fusion.10
  36.1 6.7 %collective-permute-done.3.yp = bf16[55,32,128]{2,1,0:T(8,128)(2,1)S(1)} collective-permute-done((bf16[55,32,128]{2,1,0:T(8,128)(2,1)}, bf16[55,32,128]{2,1,0:T(8,128)(2,1)S(1)}, u32[]{:S(2)}, u32[]{:S(2)}) %collective-permute-start.3) | collective-permute-done | bytes 450592 | tf_op jit(solution)/shard_map/ppermute | solution.py:24
  42.8 0.8 copy-done.9
  43.6 0.1 stack.3
  43.6 1.0 copy-done.4
  44.7 1.0 copy-done.6
  45.6 1.0 copy-done.10
  46.6 37.1 %shard_map.93 = (bf16[8,8,32,128]{3,2,1,0:T(8,128)(2,1)}, bf16[8,8,32,128]{3,2,1,0:T(8,128)(2,1)S(1)}, bf16[8,8,32,128]{3,2,1,0:T(8,128)(2,1)S(1)}, bf16[6912,128]{1,0:T(8,128)(2,1)}) custom-call(s32[1152]{0:T(1024)S(1)} %bitcast_convert_fusion.tab, bf16[8,8,32,128]{3,2,1,0:T(8,128)(2,1)S(1)} %bitcast.75, bf16[8,8,32,128]{3,2,1,0:T(8,128)(2,1)S(1)} %bitcast.80, ...), custom_call_target="tpu_custom_call" | custom-call | flops 12683575296 | bytes 10485760 | tf_op jit(solution)/shard_map/pallas_call | solution.py:264
  83.7 0.8 copy-done.7
  84.5 0.8 copy-done.11
  85.3 10.9 %all_to_all.30 = bf16[2,3456,128]{2,1,0:T(8,128)(2,1)} all-to-all(bf16[2,3456,128]{2,1,0:T(8,128)(2,1)} %bitcast.84), channel_id=1, replica_groups=mesh['sx'=8,'sy'=16,'dp'=2] {'dp'}, dimensions={0} | all-to-all | bytes 3538944 | tf_op jit(solution)/shard_map/all_to_all | solution.py:277
  96.2 2.4 %reduce_sum.36 = bf16[3456,128]{1,0:T(8,128)(2,1)S(1)} reduce(bf16[2,3456,128]{2,1,0:T(8,128)(2,1)} %all_to_all.30, bf16[]{:T(256)} %constant.14.clone.1), dimensions={0}, to_apply=%region_0.1 | reduce | flops 442368 | bytes 2654210 | tf_op jit(solution)/shard_map/reduce_sum | solution.py:278
  98.5 0.0 copy-start.8
  98.5 22.3 %all_to_all.31 = bf16[16,216,128]{2,1,0:T(8,128)(2,1)S(1)} all-to-all(bf16[16,216,128]{2,1,0:T(8,128)(2,1)S(1)} %bitcast.81), channel_id=1, replica_groups=mesh['sx'=8,'sy'=16,'dp'=2] {'sy'}, dimensions={0} | all-to-all | bytes 1769472 | tf_op jit(solution)/shard_map/all_to_all | solution.py:277
  120.9 0.1 reduce_sum.37
  121.0 0.7 reshape.138
  121.6 7.6 %all-to-all-start.2 = ((bf16[8,27,128]{2,1,0:T(8,128)(2,1)}), bf16[8,27,128]{2,1,0:T(8,128)(2,1)S(1)}, u32[]{:S(2)}, u32[]{:S(2)}) async-start(bf16[8,27,128]{2,1,0:T(8,128)(2,1)} %reshape.138), calls=%async_computation.2 | async-start | bytes 131072 | tf_op jit(solution)/shard_map/all_to_all | solution.py:277
  129.3 1.3 collective-permute-start.5
  130.6 6.0 %all-to-all-done.2 = bf16[8,27,128]{2,1,0:T(8,128)(2,1)S(1)} async-done(((bf16[8,27,128]{2,1,0:T(8,128)(2,1)}), bf16[8,27,128]{2,1,0:T(8,128)(2,1)S(1)}, u32[]{:S(2)}, u32[]{:S(2)}) %all-to-all-start.2) | async-done | bytes 55328 | tf_op jit(solution)/shard_map/all_to_all | solution.py:277
  136.6 0.6 broadcast_in_dim.38
  137.3 3.4 %all-to-all-start.3 = ((bf16[8,27,128]{2,1,0:T(8,128)(2,1)}), bf16[8,27,128]{2,1,0:T(8,128)(2,1)S(1)}, u32[]{:S(2)}, u32[]{:S(2)}) async-start(bf16[8,27,128]{2,1,0:T(8,128)(2,1)} %broadcast_in_dim.38), calls=%async_computation.3 | async-start | bytes 131072 | tf_op jit(solution)/shard_map/all_to_all | solution.py:284
  140.7 3.3 %collective-permute-start.4 = (bf16[8,32,128]{2,1,0:T(8,128)(2,1)S(1)}, bf16[8,32,128]{2,1,0:T(8,128)(2,1)S(1)}, u32[]{:S(2)}, u32[]{:S(2)}) collective-permute-start(bf16[8,32,128]{2,1,0:T(8,128)(2,1)S(1)} %get-tuple-element.17), channel_id=1, source_target_pairs={{0,32},{32,64},{64,96},{96,128},{128,160},{160,192},{192,224},{1,3... | collective-permute-start | bytes 196616 | tf_op jit(solution)/shard_map/ppermute | solution.py:23
  143.9 4.0 %all-to-all-done.3 = bf16[8,27,128]{2,1,0:T(8,128)(2,1)S(1)} async-done(((bf16[8,27,128]{2,1,0:T(8,128)(2,1)}), bf16[8,27,128]{2,1,0:T(8,128)(2,1)S(1)}, u32[]{:S(2)}, u32[]{:S(2)}) %all-to-all-start.3) | async-done | bytes 55328 | tf_op jit(solution)/shard_map/all_to_all | solution.py:284
  147.9 1.0 broadcast_in_dim.40
  149.0 4.3 %all-to-all-start.4 = ((bf16[16,216,128]{2,1,0:T(8,128)(2,1)}), bf16[16,216,128]{2,1,0:T(8,128)(2,1)}, u32[]{:S(2)}, u32[]{:S(2)}) async-start(bf16[16,216,128]{2,1,0:T(8,128)(2,1)} %broadcast_in_dim.40), calls=%async_computation.4 | async-start | bytes 1769472 | tf_op jit(solution)/shard_map/all_to_all | solution.py:284
  153.4 3.1 %collective-permute-start.6 = (bf16[10,32,128]{2,1,0:T(8,128)(2,1)S(1)}, bf16[10,32,128]{2,1,0:T(8,128)(2,1)S(1)}, u32[]{:S(2)}, u32[]{:S(2)}) collective-permute-start(bf16[10,32,128]{2,1,0:T(8,128)(2,1)S(1)} %pad_maximum_fusion.2), channel_id=1, source_target_pairs={{0,2},{2,4},{4,6},{6,8},{8,10},{10,12},{12,14},{14,16},{16,18},{18... | collective-permute-start | bytes 245768 | tf_op jit(solution)/shard_map/ppermute | solution.py:23
  156.5 0.6 pad_maximum_fusion.3
  157.1 1.4 collective-permute-start.7
  158.5 0.1 reverse_bitcast_fusion
  158.6 1.3 copy.27
  159.9 1.2 collective-permute-done.6.ym
  161.1 2.9 %collective-permute-done.7.yp = bf16[10,32,128]{2,1,0:T(8,128)(2,1)S(1)} collective-permute-done((bf16[10,32,128]{2,1,0:T(8,128)(2,1)}, bf16[10,32,128]{2,1,0:T(8,128)(2,1)S(1)}, u32[]{:S(2)}, u32[]{:S(2)}) %collective-permute-start.7) | collective-permute-done | bytes 81952 | tf_op jit(solution)/shard_map/ppermute | solution.py:24
  164.0 6.6 %shard_map.94 = bf16[8,8,32,128]{3,2,1,0:T(8,128)(2,1)} custom-call(s32[1152]{0:T(1024)S(1)} %bitcast_convert_fusion.tab, bf16[8,8,32,128]{3,2,1,0:T(8,128)(2,1)S(1)} %copy-done.8, bf16[8,8,32,128]{3,2,1,0:T(8,128)(2,1)S(1)} %copy-done.12, bf16[8,32,128]{2,1,0:T(8,128)(2,1)S(1)} %collective-permute-done.4.xm, ...), custom_call_target="tpu_custom_call" | custom-call | flops 1811939328 | bytes 4194304 | tf_op jit(solution)/shard_map/pallas_call | solution.py:264
  170.6 1.4 broadcast_in_dim.42
  171.9 9.0 %all_to_all.32 = bf16[2,3456,128]{2,1,0:T(8,128)(2,1)S(1)} all-to-all(bf16[2,3456,128]{2,1,0:T(8,128)(2,1)S(1)} %broadcast_in_dim.42), channel_id=1, replica_groups=mesh['sx'=8,'sy'=16,'dp'=2] {'dp'}, dimensions={0} | all-to-all | bytes 3538944 | tf_op jit(solution)/shard_map/all_to_all | solution.py:284
  180.9 2.0 %fusion.4 = (f32[1,3456,128]{2,1,0:T(8,128)}, f32[1,3456,128]{2,1,0:T(8,128)}) fusion(bf16[2,3456,128]{2,1,0:T(8,128)(2,1)S(1)} %all_to_all.32), kind=kLoop, calls=%fused_computation.49 | loop fusion | bytes 7077888 | tf_op jit(solution)/shard_map/slice | solution.py:368
  (43 shorter events, 0.3 us)
Async XLA Ops:
  0.6 9.5 %copy-start.3 = (bf16[1,8,8,4,8,128]{5,4,3,2,1,0:T(8,128)(2,1)S(1)}, bf16[1,8,8,4,8,128]{5,4,3,2,1,0:T(8,128)(2,1)}, u32[]{:S(2)}) copy-start(bf16[1,8,8,4,8,128]{5,4,3,2,1,0:T(8,128)(2,1)} %param.7) | copy-start | bytes 1572868
  0.6 9.5 %copy-start = (bf16[1,8,8,4,8,128]{5,4,3,2,1,0:T(8,128)(2,1)S(1)}, bf16[1,8,8,4,8,128]{5,4,3,2,1,0:T(8,128)(2,1)}, u32[]{:S(2)}) copy-start(bf16[1,8,8,4,8,128]{5,4,3,2,1,0:T(8,128)(2,1)} %param.6) | copy-start | bytes 1572868
  4.4 9.5 %collective-permute-start = (bf16[33,32,128]{2,1,0:T(8,128)(2,1)S(1)}, bf16[33,32,128]{2,1,0:T(8,128)(2,1)S(1)}, u32[]{:S(2)}, u32[]{:S(2)}) collective-permute-start(bf16[33,32,128]{2,1,0:T(8,128)(2,1)S(1)} %get-tuple-element.49), channel_id=1, source_target_pairs={{0,32},{32,64},{64,96},{96,128},{128,160},{160,192},{192,224},{1,3... | collective-permute-start | bytes 811016 | tf_op jit(solution)/shard_map/ppermute | solution.py:23
  8.8 9.3 %collective-permute-start.1 = (bf16[33,32,128]{2,1,0:T(8,128)(2,1)S(1)}, bf16[33,32,128]{2,1,0:T(8,128)(2,1)S(1)}, u32[]{:S(2)}, u32[]{:S(2)}) collective-permute-start(bf16[33,32,128]{2,1,0:T(8,128)(2,1)S(1)} %get-tuple-element.48), channel_id=1, source_target_pairs={{32,0},{64,32},{96,64},{128,96},{160,128},{192,160},{224,192},{33,... | collective-permute-start | bytes 811016 | tf_op jit(solution)/shard_map/ppermute | solution.py:24
  10.2 17.8 %copy-start.1 = (bf16[27,128,128]{2,1,0:T(8,128)(2,1)S(1)}, bf16[27,128,128]{2,1,0:T(8,128)(2,1)}, u32[]{:S(2)}) copy-start(bf16[27,128,128]{2,1,0:T(8,128)(2,1)} %param.9) | copy-start | bytes 2654212
  18.1 5.1 %copy-start.5 = (bf16[33,32,128]{2,1,0:T(8,128)(2,1)}, bf16[33,32,128]{2,1,0:T(8,128)(2,1)S(1)}, u32[]{:S(2)}) copy-start(bf16[33,32,128]{2,1,0:T(8,128)(2,1)S(1)} %collective-permute-done.1.xp) | copy-start | bytes 811012
  23.2 0.8 copy-start.13
  23.9 19.7 %copy-start.2 = (bf16[27,128,128]{2,1,0:T(8,128)(2,1)S(1)}, bf16[27,128,128]{2,1,0:T(8,128)(2,1)}, u32[]{:S(2)}) copy-start(bf16[27,128,128]{2,1,0:T(8,128)(2,1)} %param.8) | copy-start | bytes 2654212
  23.9 11.5 %collective-permute-start.2 = (bf16[55,32,128]{2,1,0:T(8,128)(2,1)}, bf16[55,32,128]{2,1,0:T(8,128)(2,1)}, u32[]{:S(2)}, u32[]{:S(2)}) collective-permute-start(bf16[55,32,128]{2,1,0:T(8,128)(2,1)} %get-tuple-element.33), channel_id=1, source_target_pairs={{0,2},{2,4},{4,6},{6,8},{8,10},{10,12},{12,14},{14,16},{16,18},{18... | collective-permute-start | bytes 1351688 | tf_op jit(solution)/shard_map/ppermute | solution.py:23
  30.8 12.0 %collective-permute-start.3 = (bf16[55,32,128]{2,1,0:T(8,128)(2,1)}, bf16[55,32,128]{2,1,0:T(8,128)(2,1)S(1)}, u32[]{:S(2)}, u32[]{:S(2)}) collective-permute-start(bf16[55,32,128]{2,1,0:T(8,128)(2,1)} %copy-done.13), channel_id=1, source_target_pairs={{2,0},{4,2},{6,4},{8,6},{10,8},{12,10},{14,12},{16,14},{18,16},{20... | collective-permute-start | bytes 1351688 | tf_op jit(solution)/shard_map/ppermute | solution.py:24
  42.8 0.8 copy-start.9
  43.6 1.0 copy-start.4
  44.7 1.0 copy-start.6
  45.6 1.0 copy-start.10
  83.7 0.8 copy-start.7
  84.5 0.8 copy-start.11
  98.5 30.8 %copy-start.8 = (bf16[8,8,32,128]{3,2,1,0:T(8,128)(2,1)S(1)}, bf16[8,8,32,128]{3,2,1,0:T(8,128)(2,1)}, u32[]{:S(2)}) copy-start(bf16[8,8,32,128]{3,2,1,0:T(8,128)(2,1)} %copy-done.7) | copy-start | bytes 1572868
  121.6 15.0 %all-to-all-start.2 = ((bf16[8,27,128]{2,1,0:T(8,128)(2,1)}), bf16[8,27,128]{2,1,0:T(8,128)(2,1)S(1)}, u32[]{:S(2)}, u32[]{:S(2)}) async-start(bf16[8,27,128]{2,1,0:T(8,128)(2,1)} %reshape.138), calls=%async_computation.2 | async-start | bytes 131072 | tf_op jit(solution)/shard_map/all_to_all | solution.py:277
  129.3 24.0 %collective-permute-start.5 = (bf16[8,32,128]{2,1,0:T(8,128)(2,1)S(1)}, bf16[8,32,128]{2,1,0:T(8,128)(2,1)S(1)}, u32[]{:S(2)}, u32[]{:S(2)}) collective-permute-start(bf16[8,32,128]{2,1,0:T(8,128)(2,1)S(1)} %get-tuple-element.16), channel_id=1, source_target_pairs={{32,0},{64,32},{96,64},{128,96},{160,128},{192,160},{224,192},{33,... | collective-permute-start | bytes 196616 | tf_op jit(solution)/shard_map/ppermute | solution.py:24
  137.3 10.6 %all-to-all-start.3 = ((bf16[8,27,128]{2,1,0:T(8,128)(2,1)}), bf16[8,27,128]{2,1,0:T(8,128)(2,1)S(1)}, u32[]{:S(2)}, u32[]{:S(2)}) async-start(bf16[8,27,128]{2,1,0:T(8,128)(2,1)} %broadcast_in_dim.38), calls=%async_computation.3 | async-start | bytes 131072 | tf_op jit(solution)/shard_map/all_to_all | solution.py:284
  140.7 12.6 %collective-permute-start.4 = (bf16[8,32,128]{2,1,0:T(8,128)(2,1)S(1)}, bf16[8,32,128]{2,1,0:T(8,128)(2,1)S(1)}, u32[]{:S(2)}, u32[]{:S(2)}) collective-permute-start(bf16[8,32,128]{2,1,0:T(8,128)(2,1)S(1)} %get-tuple-element.17), channel_id=1, source_target_pairs={{0,32},{32,64},{64,96},{96,128},{128,160},{160,192},{192,224},{1,3... | collective-permute-start | bytes 196616 | tf_op jit(solution)/shard_map/ppermute | solution.py:23
  149.0 21.6 %all-to-all-start.4 = ((bf16[16,216,128]{2,1,0:T(8,128)(2,1)}), bf16[16,216,128]{2,1,0:T(8,128)(2,1)}, u32[]{:S(2)}, u32[]{:S(2)}) async-start(bf16[16,216,128]{2,1,0:T(8,128)(2,1)} %broadcast_in_dim.40), calls=%async_computation.4 | async-start | bytes 1769472 | tf_op jit(solution)/shard_map/all_to_all | solution.py:284
  153.4 7.8 %collective-permute-start.6 = (bf16[10,32,128]{2,1,0:T(8,128)(2,1)S(1)}, bf16[10,32,128]{2,1,0:T(8,128)(2,1)S(1)}, u32[]{:S(2)}, u32[]{:S(2)}) collective-permute-start(bf16[10,32,128]{2,1,0:T(8,128)(2,1)S(1)} %pad_maximum_fusion.2), channel_id=1, source_target_pairs={{0,2},{2,4},{4,6},{6,8},{8,10},{10,12},{12,14},{14,16},{16,18},{18... | collective-permute-start | bytes 245768 | tf_op jit(solution)/shard_map/ppermute | solution.py:23
  157.1 6.9 %copy-start.12 = (bf16[8,8,32,128]{3,2,1,0:T(8,128)(2,1)S(1)}, bf16[8,8,32,128]{3,2,1,0:T(8,128)(2,1)}, u32[]{:S(2)}) copy-start(bf16[8,8,32,128]{3,2,1,0:T(8,128)(2,1)} %copy-done.11) | copy-start | bytes 1572868
  157.1 6.9 %collective-permute-start.7 = (bf16[10,32,128]{2,1,0:T(8,128)(2,1)}, bf16[10,32,128]{2,1,0:T(8,128)(2,1)S(1)}, u32[]{:S(2)}, u32[]{:S(2)}) collective-permute-start(bf16[10,32,128]{2,1,0:T(8,128)(2,1)} %pad_maximum_fusion.3), channel_id=1, source_target_pairs={{2,0},{4,2},{6,4},{8,6},{10,8},{12,10},{14,12},{16,14},{18,16},{20... | collective-permute-start | bytes 245768 | tf_op jit(solution)/shard_map/ppermute | solution.py:24

commit v2 on v1

v2 whole, which is shorter than its diff:
```python
import functools

import jax
import jax.numpy as jnp
from jax import lax
from jax.experimental import pallas as pl
from jax.experimental.pallas import tpu as pltpu
from jax.sharding import PartitionSpec as P

C = 128
BE = 8
NB = 4
ROWS = NB * BE
ZERO = ROWS
F32 = jnp.float32
BF16 = jnp.bfloat16
COLUMNS = [(cx, cy) for cx in (-1, 0, 1) for cy in (-1, 0, 1)]
OWN = 4


def shift_pair(low, high, axis):
    ends = lax.axis_size(axis) - 1
    from_low = lax.ppermute(high, axis, [(i, i + 1) for i in range(ends)])
    from_high = lax.ppermute(low, axis, [(i + 1, i) for i in range(ends)])
    return from_low, from_high


def spans(halo):
    return {-1: (0, halo), 0: (halo, halo + BE), 1: (halo + BE, 2 * halo + BE)}


def build_patches(tab, field, put, halo, column, xs, ys):
    cx, cy = COLUMNS[column]
    row = lax.broadcasted_iota(jnp.int32, (1, BE, C), 1)
    for sx, (x0, x1) in spans(halo).items():
        xa, xb = max(x0, xs[0]), min(x1, xs[1] + 2)
        if xa >= xb:
            continue
        for sy, (y0, y1) in spans(halo).items():
            ya, yb = max(y0, ys[0]), min(y1, ys[1] + 2)
            if ya >= yb:
                continue
            first = (sx - cx + 1) * 9 + (sy - cy + 1) * 3
            offsets = [
                [pl.multiple_of(tab[column, s * 27 + first + j], BE) for j in range(3)]
                for s in range(NB)
            ]

            def line(x):
                parts = [[], [], []]
                for below, here, above in offsets:
                    v = field[x, ya:yb, pl.ds(here, BE), :]
                    lo = field[x, ya:yb, pl.ds(below, BE), :]
                    hi = field[x, ya:yb, pl.ds(above, BE), :]
                    parts[0].append(pltpu.roll(jnp.where(row == BE - 1, lo, v), 1, 1))
                    parts[1].append(v)
                    parts[2].append(pltpu.roll(jnp.where(row == 0, hi, v), BE - 1, 1))
                for j in range(3):
                    value = jnp.concatenate(parts[j], axis=1).astype(BF16)
                    put(x - xs[0], ya - ys[0], yb - ys[0], j * C, value)

            if xb - xa > 3:

                def body(x, unused):
                    line(x)
                    return unused

                lax.fori_loop(xa, xb, body, 0)
            else:
                for x in range(xa, xb):
                    line(x)


def into(ref, lead=None):
    def put(x, ya, yb, lane, value):
        if lead is None:
            ref[x, ya:yb, :, lane : lane + C] = value
        else:
            ref[lead, x, ya:yb, :, lane : lane + C] = value

    return put


def product(get, weight):
    parts = []
    for a in range(3):
        for b in range(3):
            piece = get(a, b)
            parts.append(piece.reshape(-1, piece.shape[-1]))
    return jnp.dot(jnp.concatenate(parts, axis=1), weight[...], preferred_element_type=F32)


def band(weight, wide):
    wide[0 : 27 * C, 0:C] = weight[...]
    wide[9 * C : 36 * C, C : 2 * C] = weight[...]


def flip_kernel(first, second, first_out, second_out):
    for weight, out in ((second, second_out), (first, first_out)):

        def body(n, unused):
            for j in range(9):
                k = n * 9 + j
                block = weight[pl.ds(pl.multiple_of((26 - k) * C, C), C), :].T
                out[pl.ds(pl.multiple_of(k * C, C), C), :] = block
            return unused

        lax.fori_loop(0, 3, body, 0)


def clear_band(wide):
    wide[27 * C : 36 * C, 0:C] = jnp.zeros((9 * C, C), BF16)
    wide[0 : 9 * C, C : 2 * C] = jnp.zeros((9 * C, C), BF16)


def pairs(gets, wide):
    parts, sizes = [], None
    for j in range(4):
        for b in range(3):
            pieces = [get(j, b) for get in gets]
            pieces = [piece.reshape(-1, piece.shape[-1]) for piece in pieces]
            sizes = [piece.shape[0] for piece in pieces]
            parts.append(pieces[0] if len(pieces) == 1 else jnp.concatenate(pieces, axis=0))
    value = jnp.dot(jnp.concatenate(parts, axis=1), wide[...], preferred_element_type=F32)
    results, at = [], 0
    for size in sizes:
        results.append((value[at : at + size, 0:C], value[at : at + size, C : 2 * C]))
        at += size
    return results


def rounded(value):
    return value.astype(BF16).astype(F32)


def slope_of(value):
    sig = jax.nn.sigmoid(value)
    return sig * (1.0 + value * (1.0 - sig))


def live_rows(tab):
    parts = [
        jnp.where(tab[OWN, s * 27 + 13] < ZERO, jnp.ones((BE, C), F32), jnp.zeros((BE, C), F32))
        for s in range(NB)
    ]
    return jnp.concatenate(parts, axis=0)


def zero_slot(field):
    def body(x, unused):
        field[x, :, ZERO : ZERO + BE, :] = jnp.zeros((field.shape[1], BE, C), F32)
        return unused

    lax.fori_loop(0, field.shape[0], body, 0)


def rows_at(field, x, y, value):
    n, m = value.shape[:2]
    field[x : x + n, y : y + m, 0:ROWS, :] = value


def weight_grad(patch, grads, turned, out, which, scale):
    for x in range(BE):
        block = grads[x].reshape(BE * ROWS, C).T
        for a in range(3):
            at = (x + a) * BE * ROWS
            turned[a * C : (a + 1) * C, at : at + BE * ROWS] = block

    for b in range(3):
        right = patch[:, b : b + BE].reshape((BE + 2) * BE * ROWS, 3 * C)
        term = (jnp.dot(turned[...], right, preferred_element_type=F32) * scale).astype(BF16)
        for a in range(3):
            for c in range(3):
                at = (a * 9 + b * 3 + c) * C
                out[which, at : at + C, :] = term[a * C : (a + 1) * C, c * C : (c + 1) * C].T


def clear_turned(turned):
    width = BE * ROWS
    for a in range(3):
        for x in list(range(a)) + list(range(a + BE, BE + 2)):
            turned[a * C : (a + 1) * C, x * width : (x + 1) * width] = jnp.zeros((C, width), BF16)


def load_tables(lines, staged, tab, sem):
    for column, (ref, at) in lines.items():
        staged[column : column + 1, :] = ref[at, 0:16, :].astype(F32)[0:1].astype(jnp.int32)
    copy = pltpu.make_async_copy(staged, tab, sem)
    copy.start()
    copy.wait()


def first_payload_kernel(links, count, x, cot, xlow, xhigh, ylow, yhigh, own):
    lane = lax.broadcasted_iota(jnp.int32, (ROWS, C), 1)
    row = jnp.zeros((ROWS, C), jnp.int32)
    for s in range(NB):
        for d in range(27):
            if d == 13:
                named = jnp.where(s < count[0], s, -1)
            else:
                named = links[s, d if d < 13 else d - 1]
            start = jnp.where(named < 0, NB, named) * BE
            row = jnp.where(lane == s * 27 + d, start, row)
    line = row.astype(F32).astype(BF16)
    own[0] = line
    for ref, xa, xc in ((xlow, 0, 0), (xhigh, 5, 7)):
        ref[0:24] = x[xa : xa + 3].reshape(24, ROWS, C)
        ref[24:32] = cot[xc]
        ref[32] = line
    for ref, ya, yc in ((ylow, 0, 0), (yhigh, 5, 7)):
        for i in range(BE):
            ref[3 * i : 3 * i + 3] = x[i, ya : ya + 3]
        ref[24:32] = cot[:, yc]
        ref[32] = line


def corner_payload_kernel(xm, xp, low, high):
    for ref, ya, yc in ((low, 0, 0), (high, 5, 7)):
        for j, near in enumerate((xm, xp)):
            for i in range(3):
                ref[9 * j + 3 * i : 9 * j + 3 * i + 3] = near[8 * i + ya : 8 * i + ya + 3]
            ref[18 + j] = near[24 + yc]
            ref[20 + j] = near[32]


def edge_payload_kernel(xm, xp, b1, low, high):
    for ref, y in ((low, 0), (high, 7)):
        ref[0] = xm[y]
        ref[1:9] = b1[:, y]
        ref[9] = xp[y]


def main_kernel(scale, core, own, x, cot, xm, xp, ym, yp, qm, qp, w1, w2, w2f, out, b2o, b1o, elow, ehigh, gr,
                field, hid, back, p1, p2, px, py, pc, slope1, turned, wide, staged, tab, sem):
    load_tables(
        {0: (qm, 20), 1: (xm, 32), 2: (qp, 20), 3: (ym, 32), 4: (own, 0), 5: (yp, 32), 6: (qm, 21), 7: (xp, 32), 8: (qp, 21)},
        staged, tab, sem,
    )
    live = live_rows(tab)
    for ref in (field, hid, back):
        zero_slot(ref)
    clear_turned(turned)
    clear_band(wide)
    band(w1, wide)

    def fill(i, unused):
        field[3 + i, 3:11, 0:ROWS, :] = x[i].astype(F32)
        field[3 + i, 0:3, 0:ROWS, :] = ym[pl.ds(3 * i, 3)].astype(F32)
        field[3 + i, 11:14, 0:ROWS, :] = yp[pl.ds(3 * i, 3)].astype(F32)
        return unused

    lax.fori_loop(0, BE, fill, 0)
    for i in range(3):
        for at, near, q in ((i, xm, 3 * i), (11 + i, xp, 9 + 3 * i)):
            field[at, 3:11, 0:ROWS, :] = near[8 * i : 8 * i + 8].astype(F32)
            field[at, 0:3, 0:ROWS, :] = qm[q : q + 3].astype(F32)
            field[at, 11:14, 0:ROWS, :] = qp[q : q + 3].astype(F32)

    ends = spans(2)
    corners = [0, 2, 6, 8]
    build_patches(tab, field, into(p1), 3, OWN, ends[0], ends[0])
    for j, cx in enumerate((-1, 1)):
        build_patches(tab, field, into(px, j), 3, COLUMNS.index((cx, 0)), ends[cx], ends[0])
        build_patches(tab, field, into(py, j), 3, COLUMNS.index((0, cx)), ends[0], ends[cx])
    for j, c in enumerate(corners):
        build_patches(tab, field, into(pc, j), 3, c, ends[COLUMNS[c][0]], ends[COLUMNS[c][1]])

    def hide(pre):
        return rounded(pre * jax.nn.sigmoid(pre))

    def own_pairs(patch, i):
        results = pairs([lambda j, b, g=g: patch[4 * i + g + j, b : b + BE] for g in (0, 2)], wide)
        return [(4 * i + 2 * g + h, results[g][h].reshape(BE, ROWS, C)) for g in range(2) for h in range(2)]

    def y_pairs(m):
        gets = [lambda j, b, s=s, p=p: py[s, 2 * p + j, b : b + m] for s in range(2) for p in range(4)]
        results = pairs(gets, wide)
        return [
            (s, 2 * p + h, results[4 * s + p][h].reshape(m, ROWS, C)) for s in range(2) for p in range(4) for h in range(2)
        ]

    def first_own(i, unused):
        for at, pre in own_pairs(p1, i):
            slope1[at] = slope_of(pre)
            hid[2 + at, 2:10, 0:ROWS, :] = hide(pre)
        return unused

    lax.fori_loop(0, 2, first_own, 0)
    results = pairs([lambda j, b, s=s: px[s, j, b : b + BE] for s in range(2)], wide)
    for s in range(2):
        for h in range(2):
            hid[10 * s + h, 2:10, 0:ROWS, :] = hide(results[s][h]).reshape(BE, ROWS, C)
    for s, at, pre in y_pairs(2):
        hid[2 + at, 10 * s : 10 * s + 2, 0:ROWS, :] = hide(pre)
    [result] = pairs([lambda j, b: pc[:, j, b : b + 2]], wide)
    for h in range(2):
        value = hide(result[h]).reshape(4, 2, ROWS, C)
        for j, (ax, ay) in enumerate(((0, 0), (0, 10), (10, 0), (10, 10))):
            hid[ax + h, ay : ay + 2, 0:ROWS, :] = value[j]

    ends = spans(1)
    band(w2, wide)
    build_patches(tab, hid, into(p2), 2, OWN, ends[0], ends[0])
    for j, cx in enumerate((-1, 1)):
        build_patches(tab, hid, into(px, j), 2, COLUMNS.index((cx, 0)), ends[cx], ends[0])
        build_patches(tab, hid, into(py, j), 2, COLUMNS.index((0, cx)), ends[0], ends[cx])
    for j, c in enumerate(corners):
        build_patches(tab, hid, into(pc, j), 2, c, ends[COLUMNS[c][0]], ends[COLUMNS[c][1]])

    def second_own(i, unused):
        for at, pre in own_pairs(p2, i):
            total = field[3 + at, 3:11, 0:ROWS, :] * live + pre
            sig = jax.nn.sigmoid(total)
            out[at] = (total * sig * live).astype(BF16)
            slope = sig * (1.0 + total * (1.0 - sig))
            grad = (cot[at].astype(F32) * slope * live).astype(BF16)
            b2o[at] = grad
            back[1 + at, 1:9, 0:ROWS, :] = grad.astype(F32)
        return unused

    lax.fori_loop(0, 2, second_own, 0)
    for s, at, pre in y_pairs(1):
        near = (ym, yp)[s]
        total = field[3 + at, (2, 11)[s], 0:ROWS, :] + pre[0]
        back[1 + at, 9 * s, 0:ROWS, :] = rounded(near[24 + at].astype(F32) * slope_of(total))
    pre = product(lambda a, b: px[:, a : a + 1, b : b + BE], w2).reshape(2, BE, ROWS, C)
    for j, (at, cx, near) in enumerate(((2, 0, xm), (11, 9, xp))):
        total = field[at, 3:11, 0:ROWS, :] + pre[j]
        back[cx, 1:9, 0:ROWS, :] = rounded(near[24:32].astype(F32) * slope_of(total))
    pre = product(lambda a, b: pc[:, a : a + 1, b : b + 1], w2).reshape(4, ROWS, C)
    for j, (ax, ay, cx, cy, near, at) in enumerate(
        ((2, 2, 0, 0, qm, 18), (2, 11, 0, 9, qp, 18), (11, 2, 9, 0, qm, 19), (11, 11, 9, 9, qp, 19))
    ):
        total = field[ax, ay, 0:ROWS, :] + pre[j]
        back[cx, cy, 0:ROWS, :] = rounded(near[at].astype(F32) * slope_of(total))
    weight_grad(p2, b2o, turned, gr, 1 - core[0], scale)

    band(w2f, wide)
    build_patches(tab, back, into(p2), 1, OWN, (0, BE), (0, BE))

    def third(i, unused):
        for at, pre in own_pairs(p2, i):
            b1o[at] = (pre * slope1[at] * live).astype(BF16)
        return unused

    lax.fori_loop(0, 2, third, 0)
    elow[...] = b1o[0]
    ehigh[...] = b1o[7]
    weight_grad(p1, b1o, turned, gr, core[0], scale)


def last_kernel(own, b1, b2, xm, xp, ym, yp, w1f, out, field, patch, wide, staged, tab, sem):
    load_tables({OWN: (own, 0)}, staged, tab, sem)
    live = live_rows(tab)
    zero_slot(field)
    clear_band(wide)
    band(w1f, wide)

    def fill(i, unused):
        field[1 + i, 1:9, 0:ROWS, :] = b1[i].astype(F32)
        return unused

    lax.fori_loop(0, BE, fill, 0)
    field[0, 1:9, 0:ROWS, :] = xm[...].astype(F32)
    field[9, 1:9, 0:ROWS, :] = xp[...].astype(F32)
    field[:, 0, 0:ROWS, :] = ym[...].astype(F32)
    field[:, 9, 0:ROWS, :] = yp[...].astype(F32)
    build_patches(tab, field, into(patch), 1, OWN, (0, BE), (0, BE))

    def step(i, unused):
        results = pairs([lambda j, b, g=g: patch[4 * i + g + j, b : b + BE] for g in (0, 2)], wide)
        for g in range(2):
            for h in range(2):
                at = 4 * i + 2 * g + h
                out[at] = ((b2[at].astype(F32) + results[g][h].reshape(BE, ROWS, C)) * live).astype(BF16)
        return unused

    lax.fori_loop(0, 2, step, 0)


def call(kernel, outs, scratch, cost, mib, scalars, *args):
    smem = pl.BlockSpec(memory_space=pltpu.SMEM)
    vmem = pl.BlockSpec(memory_space=pltpu.VMEM)
    return pl.pallas_call(
        kernel,
        out_shape=outs,
        in_specs=[smem] * scalars + [vmem] * (len(args) - scalars),
        out_specs=jax.tree.map(lambda o: vmem, outs),
        scratch_shapes=scratch,
        compiler_params=pltpu.CompilerParams(vmem_limit_bytes=mib * 2**20),
        cost_estimate=pl.CostEstimate(flops=cost[0], bytes_accessed=cost[1], transcendentals=0),
    )(*args)


def swap_cores(part):
    return lax.ppermute(part, "dp", [(0, 1), (1, 0)])


def sum_scatter(part, axis):
    n = lax.axis_size(axis)
    swapped = lax.all_to_all(part.reshape(n, part.shape[0] // n, C), axis, 0, 0, tiled=True)
    return jnp.sum(swapped.astype(F32), axis=0).astype(BF16)


def sum_pairs(part, axis):
    n = lax.axis_size(axis)
    reach = 1
    while reach < n:
        other = lax.ppermute(part, axis, [(i, i ^ (2 * reach - 1)) for i in range(n)])
        part = (part.astype(F32) + other.astype(F32)).astype(BF16)
        reach *= 2
    return part


def gather_axis(part, axis):
    n = lax.axis_size(axis)
    copies = jnp.broadcast_to(part[None], (n,) + part.shape)
    return lax.all_to_all(copies, axis, 0, 0, tiled=True).reshape(n * part.shape[0], C)


def shape_of(*sizes):
    return jax.ShapeDtypeStruct(sizes, BF16)


def shards(features, cotangent, first_weight, second_weight, neighbours, counts):
    x = features.reshape(BE, BE, ROWS, C)
    cot = cotangent.reshape(BE, BE, ROWS, C)
    w1, w2 = first_weight.reshape(27 * C, C), second_weight.reshape(27 * C, C)
    n_devices = lax.axis_size("sx") * lax.axis_size("sy") * lax.axis_size("dp")
    scale = float(n_devices * NB * BE**3) ** -0.5
    core = lax.axis_index("dp").astype(jnp.int32)

    payload = shape_of(33, ROWS, C)
    xlow, xhigh, ylow, yhigh, own = call(
        first_payload_kernel, [payload] * 4 + [shape_of(1, ROWS, C)], [], (0, 2**21), 8, 2,
        neighbours.reshape(NB, 26), counts.reshape(1), x, cot,
    )
    xm, xp = shift_pair(xlow, xhigh, "sx")
    ym, yp = shift_pair(ylow, yhigh, "sy")
    qlow, qhigh = call(corner_payload_kernel, [shape_of(22, ROWS, C)] * 2, [], (0, 2**19), 8, 0, xm, xp)
    held1, held2, qlow, qhigh = lax.optimization_barrier((w1, w2, qlow, qhigh))
    qm, qp = shift_pair(qlow, qhigh, "sy")
    w1f, w2f = call(flip_kernel, [shape_of(27 * C, C)] * 2, [], (2**24, 2**22), 8, 0, held1, held2)

    block, edge = shape_of(BE, BE, ROWS, C), shape_of(BE, ROWS, C)
    lanes = 3 * C
    unit = 2 * BE * BE * ROWS * 27 * C * C
    tables = [pltpu.VMEM((16, C), jnp.int32), pltpu.SMEM((16, C), jnp.int32), pltpu.SemaphoreType.DMA]
    out, b2, b1, elow, ehigh, grads = call(
        functools.partial(main_kernel, scale),
        [block, block, block, edge, edge, shape_of(2, 27 * C, C)],
        [
            pltpu.VMEM((14, 14, ROWS + BE, C), F32),
            pltpu.VMEM((12, 12, ROWS + BE, C), F32),
            pltpu.VMEM((10, 10, ROWS + BE, C), F32),
            pltpu.VMEM((10, 10, ROWS, lanes), BF16),
            pltpu.VMEM((10, 10, ROWS, lanes), BF16),
            pltpu.VMEM((2, 4, 10, ROWS, lanes), BF16),
            pltpu.VMEM((2, 10, 4, ROWS, lanes), BF16),
            pltpu.VMEM((4, 4, 4, ROWS, lanes), BF16),
            pltpu.VMEM((BE, BE, ROWS, C), F32),
            pltpu.VMEM((3 * C, (BE + 2) * BE * ROWS), BF16),
            pltpu.VMEM((36 * C, 2 * C), BF16),
            *tables,
        ],
        (7 * unit, 10 * 2**20), 32, 1,
        core.reshape(1), own, x, cot, xm, xp, ym, yp, qm, qp, w1, w2, w2f,
    )

    received = swap_cores(grads[1])
    bxm, bxp = shift_pair(elow, ehigh, "sx")
    part = (grads[0].astype(F32) + received.astype(F32)).astype(BF16)
    blow, bhigh = call(edge_payload_kernel, [shape_of(BE + 2, ROWS, C)] * 2, [], (0, 2**19), 8, 0, bxm, bxp, b1)
    part, blow, bhigh = lax.optimization_barrier((part, blow, bhigh))
    bym, byp = shift_pair(blow, bhigh, "sy")
    part, bym, byp = lax.optimization_barrier((sum_scatter(part, "sy"), bym, byp))
    part, b2 = lax.optimization_barrier((sum_pairs(part, "sx"), b2))

    grad_input = call(
        last_kernel,
        block,
        [
            pltpu.VMEM((10, 10, ROWS + BE, C), F32),
            pltpu.VMEM((10, 10, ROWS, lanes), BF16),
            pltpu.VMEM((36 * C, 2 * C), BF16),
            *tables,
        ],
        (unit, 4 * 2**20), 12, 0,
        own, b1, b2, bxm, bxp, bym, byp, w1f,
    )
    part, grad_input = lax.optimization_barrier((gather_axis(part, "sy"), grad_input))
    other = swap_cores(part)
    first = jnp.where(core == 0, part, other).astype(F32).reshape(27, C, C)
    second = jnp.where(core == 0, other, part).astype(F32).reshape(27, C, C)
    shape = features.shape
    return out.reshape(shape), grad_input.reshape(shape), first, second


def solution(mesh):
    column = P("dp", "sx", "sy", None, None, None)
    return jax.shard_map(
        shards,
        mesh=mesh,
        in_specs=(column, column, P(), P(), P("dp", "sx", "sy", None, None), P("dp", "sx", "sy")),
        out_specs=(column, column, P(), P()),
        check_vma=False,
    )
```

time: 185 us -> 141 us (0.76)
  blocking collectives: 42.2 us -> 0 us
  starting transfers between devices: 35.4 us -> 54.4 us
  local copies, waits for them, and re-layouts: 26.3 us -> 8.28 us
  Pallas kernels: 43.6 us -> 36.3 us
  waiting for transfers between devices: 30.5 us -> 36 us
    all_to_all x3 -> x0, blocking collectives: 42.2 us -> none  [the longest x2 33.2 us: reduce_axis(): lax.all_to_all(part.reshape(n, part.shape[0] // n, C), axis, 0, 0, tiled=...]
    ppermute x0 -> x5, starting transfers between devices: none -> 16.2 us  [the longest x2 9.01 us: swap_cores(): return lax.ppermute(part, 'dp', [(0, 1), (1, 0)])]
    ppermute x0 -> x5, waiting for transfers between devices: none -> 9.79 us  [the longest x3 7.73 us: sum_pairs(): other = lax.ppermute(part, axis, [(i, i ^ 2 * reach - 1) for i in range(n)])]
    pallas_call x2 -> x6, Pallas kernels: 43.6 us -> 36.3 us  [call(): pl.pallas_call(kernel, out_shape=outs, in_specs=[smem] * scalars + [vmem]...]
    ppermute x4 -> x5, waiting for transfers between devices: 7.53 us -> 0.19 us  [shift_pair(): from_low = lax.ppermute(high, axis, [(i, i + 1) for i in range(ends)])]
    transpose x4 -> x0, local copies, waits for them, and re-layouts: 4.23 us -> none  [flipped_weight(): return jnp.transpose(weight[::-1], (0, 2, 1)).reshape(27 * C, C)]
    unnamed x39 -> x28, local copies, waits for them, and re-layouts: 11.3 us -> 7.19 us
    slice x10 -> x0, local copies, waits for them, and re-layouts: 4.01 us -> none  [the longest x1 2.02 us: shards(): return (out.reshape(shape), grad_input.reshape(shape), grads[0], grads[1])]
  transfers between devices with their start and end apart: 11 -> 17, of which waited for: 8 -> 10; matrix products, arithmetic and copies ran while one was open for 5% -> 0% of each run, Pallas kernels for 4% -> 5%
where the time goes in v2:
time: 141 us
  starting transfers between devices  54.4 us (39%)
  Pallas kernels  36.3 us (26%)
  waiting for transfers between devices  36 us (26%)
  local copies, waits for them, and re-layouts  8.28 us (6%)
  other arithmetic  4.25 us (3%)
  between operations  1.64 us (1%)
    pallas_call x6, Pallas kernels, call(): pl.pallas_call(kernel, out_shape=outs, in_specs=[smem] * scalars + [vmem]...  36.3 us
    ppermute x5, starting transfers between devices, shift_pair(): from_low = lax.ppermute(high, axis, [(i, i + 1) for i in range(ends)])  18.2 us
    ppermute x5, waiting for transfers between devices, shift_pair(): from_high = lax.ppermute(low, axis, [(i + 1, i) for i in range(ends)])  11.5 us
    ppermute x2, starting transfers between devices, swap_cores(): return lax.ppermute(part, 'dp', [(0, 1), (1, 0)])  9.01 us
    all_to_all x1, waiting for transfers between devices, sum_scatter(): lax.all_to_all(part.reshape(n, part.shape[0] // n, C), axis, 0, 0, tiled=...  8.79 us
    all_to_all x1, starting transfers between devices, sum_scatter(): lax.all_to_all(part.reshape(n, part.shape[0] // n, C), axis, 0, 0, tiled=...  8.33 us
    ppermute x3, waiting for transfers between devices, sum_pairs(): other = lax.ppermute(part, axis, [(i, i ^ 2 * reach - 1) for i in range(n)])  7.73 us
    ppermute x3, starting transfers between devices, sum_pairs(): other = lax.ppermute(part, axis, [(i, i ^ 2 * reach - 1) for i in range(n)])  7.21 us
  transfers between devices with their start and end apart: 17, of which 10 were waited for; matrix products, arithmetic and copies ran while one was open for 0% of the time, Pallas kernels for 5%

profile of v2, /device:TPU:1, one launch (start us, length us, event | category | flops | bytes accessed | tf_op | source)
XLA Modules:
  0.0 140.7 jit_solution(7415688306505097837)
XLA Ops:
  0.6 0.0 copy-start
  1.4 0.0 copy-start.3
  1.4 1.0 copy-done.3
  2.4 1.0 copy-done.5
  3.5 0.7 copy-done.7
  4.1 1.5 %shard_map.93 = (bf16[33,32,128]{2,1,0:T(8,128)(2,1)S(1)}, bf16[33,32,128]{2,1,0:T(8,128)(2,1)S(1)}, bf16[33,32,128]{2,1,0:T(8,128)(2,1)}, bf16[33,32,128]{2,1,0:T(8,128)(2,1)}, bf16[1,32,128]{2,1,0:T(8,128)(2,1)S(1)}) custom-call(s32[4,26]{1,0:T(4,128)S(1)} %bitcast.29, s32[1]{0:T(128)} %bitcast.20.count, bf16[8,8,32,128]{3,2,1,0:T(8,128)(2,1)S(1)} %bitcast.25, ...), custom_call_target="tpu_custom_call" | custom-call | bytes 2097152 | tf_op jit(solution)/shard_map/pallas_call | solution.py:384
  5.6 4.4 %collective-permute-start = (bf16[33,32,128]{2,1,0:T(8,128)(2,1)S(1)}, bf16[33,32,128]{2,1,0:T(8,128)(2,1)S(1)}, u32[]{:S(2)}, u32[]{:S(2)}) collective-permute-start(bf16[33,32,128]{2,1,0:T(8,128)(2,1)S(1)} %get-tuple-element.36), channel_id=1, source_target_pairs={{0,32},{32,64},{64,96},{96,128},{128,160},{160,192},{192,224},{1,3... | collective-permute-start | bytes 811016 | tf_op jit(solution)/shard_map/ppermute | solution.py:23
  10.0 1.3 collective-permute-start.1
  11.3 3.1 %collective-permute-start.2 = (bf16[33,32,128]{2,1,0:T(8,128)(2,1)}, bf16[33,32,128]{2,1,0:T(8,128)(2,1)S(1)}, u32[]{:S(2)}, u32[]{:S(2)}) collective-permute-start(bf16[33,32,128]{2,1,0:T(8,128)(2,1)} %get-tuple-element.38), channel_id=1, source_target_pairs={{0,2},{2,4},{4,6},{6,8},{8,10},{10,12},{12,14},{14,16},{16,18},{18... | collective-permute-start | bytes 811016 | tf_op jit(solution)/shard_map/ppermute | solution.py:23
  14.5 1.3 collective-permute-start.3
  15.8 0.0 collective-permute-done.xm
  15.8 3.5 %collective-permute-done.1.xp = bf16[33,32,128]{2,1,0:T(8,128)(2,1)S(1)} collective-permute-done((bf16[33,32,128]{2,1,0:T(8,128)(2,1)S(1)}, bf16[33,32,128]{2,1,0:T(8,128)(2,1)S(1)}, u32[]{:S(2)}, u32[]{:S(2)}) %collective-permute-start.1) | collective-permute-done | bytes 270368 | tf_op jit(solution)/shard_map/ppermute | solution.py:24
  19.3 0.8 shard_map.94
  20.1 3.1 %collective-permute-start.4 = (bf16[22,32,128]{2,1,0:T(8,128)(2,1)}, bf16[22,32,128]{2,1,0:T(8,128)(2,1)S(1)}, u32[]{:S(2)}, u32[]{:S(2)}) collective-permute-start(bf16[22,32,128]{2,1,0:T(8,128)(2,1)} %get-tuple-element.42), channel_id=1, source_target_pairs={{0,2},{2,4},{4,6},{6,8},{8,10},{10,12},{12,14},{14,16},{16,18},{18... | collective-permute-start | bytes 540680 | tf_op jit(solution)/shard_map/ppermute | solution.py:23
  23.2 1.3 collective-permute-start.5
  24.5 0.0 copy-done
  24.5 0.0 copy-start.1
  24.5 1.2 copy-done.1
  25.7 0.8 shard_map.95
  26.5 0.0 collective-permute-done.2.ym
  26.5 0.0 copy-start.8
  26.5 0.7 copy-done.8
  27.2 0.0 collective-permute-done.3.yp
  27.2 0.0 collective-permute-done.4.qm
  27.2 2.4 %collective-permute-done.5.qp = bf16[22,32,128]{2,1,0:T(8,128)(2,1)S(1)} collective-permute-done((bf16[22,32,128]{2,1,0:T(8,128)(2,1)}, bf16[22,32,128]{2,1,0:T(8,128)(2,1)S(1)}, u32[]{:S(2)}, u32[]{:S(2)}) %collective-permute-start.5) | collective-permute-done | bytes 180256 | tf_op jit(solution)/shard_map/ppermute | solution.py:24
  29.6 0.7 copy-done.10
  30.3 0.0 copy-done.4
  30.3 0.0 copy-done.2
  30.3 0.0 copy-done.6
  30.3 0.9 copy-done.9
  31.3 0.9 copy-done.11
  32.2 27.6 %shard_map.96 = (bf16[8,8,32,128]{3,2,1,0:T(8,128)(2,1)}, bf16[8,8,32,128]{3,2,1,0:T(8,128)(2,1)S(1)}, bf16[8,8,32,128]{3,2,1,0:T(8,128)(2,1)S(1)}, bf16[8,32,12...) custom-call(s32[1]{0:T(128)} %bitcast.core, ...), custom_call_target="tpu_custom_call" | custom-call | flops 12683575296 | bytes 10485760 | tf_op jit(solution)/shard_map/pallas_call | solution.py:384
  59.8 0.0 copy-start.12
  59.9 0.1 slice_bitcast_fusion
  59.9 3.1 %collective-permute-start.6 = (bf16[3456,128]{1,0:T(8,128)(2,1)S(1)}, bf16[3456,128]{1,0:T(8,128)(2,1)S(1)}, u32[]{:S(2)}, u32[]{:S(2)}) collective-permute-start(bf16[3456,128]{1,0:T(8,128)(2,1)S(1)} %slice_bitcast_fusion), channel_id=1, source_target_pairs={{0,1},{1,0},{2,3},{3,2},{4,5},{5,4},{6,7},{7,6},{8,9},{9,8},{10,11... | collective-permute-start | bytes 2654216 | tf_op jit(solution)/shard_map/ppermute | solution.py:396
  63.1 3.6 %collective-permute-start.7 = (bf16[8,32,128]{2,1,0:T(8,128)(2,1)S(1)}, bf16[8,32,128]{2,1,0:T(8,128)(2,1)S(1)}, u32[]{:S(2)}, u32[]{:S(2)}) collective-permute-start(bf16[8,32,128]{2,1,0:T(8,128)(2,1)S(1)} %get-tuple-element.49), channel_id=1, source_target_pairs={{0,32},{32,64},{64,96},{96,128},{128,160},{160,192},{192,224},{1,3... | collective-permute-start | bytes 196616 | tf_op jit(solution)/shard_map/ppermute | solution.py:23
  66.7 1.3 collective-permute-start.8
  68.0 0.2 collective-permute-done.7.xm
  68.1 5.5 %collective-permute-done.8.xp = bf16[8,32,128]{2,1,0:T(8,128)(2,1)S(1)} collective-permute-done((bf16[8,32,128]{2,1,0:T(8,128)(2,1)S(1)}, bf16[8,32,128]{2,1,0:T(8,128)(2,1)S(1)}, u32[]{:S(2)}, u32[]{:S(2)}) %collective-permute-start.8) | collective-permute-done | bytes 65568 | tf_op jit(solution)/shard_map/ppermute | solution.py:24
  73.7 0.0 collective-permute-done.6
  73.7 1.1 fusion
  74.8 8.3 %all-to-all-start = ((bf16[16,216,128]{2,1,0:T(8,128)(2,1)}), bf16[16,216,128]{2,1,0:T(8,128)(2,1)S(1)}, u32[]{:S(2)}, u32[]{:S(2)}) async-start(bf16[16,216,128]{2,1,0:T(8,128)(2,1)} %bitcast.32), calls=%async_computation | async-start | bytes 1769472 | tf_op jit(solution)/shard_map/all_to_all | solution.py:401
  83.2 1.3 collective-permute-start.10
  84.5 4.0 %collective-permute-start.9 = (bf16[10,32,128]{2,1,0:T(8,128)(2,1)S(1)}, bf16[10,32,128]{2,1,0:T(8,128)(2,1)S(1)}, u32[]{:S(2)}, u32[]{:S(2)}) collective-permute-start(bf16[10,32,128]{2,1,0:T(8,128)(2,1)S(1)} %get-tuple-element.55), channel_id=1, source_target_pairs={{0,2},{2,4},{4,6},{6,8},{8,10},{10,12},{12,14},{14,16},{16,18},{18... | collective-permute-start | bytes 245768 | tf_op jit(solution)/shard_map/ppermute | solution.py:23
  88.5 8.8 %all-to-all-done = bf16[16,216,128]{2,1,0:T(8,128)(2,1)S(1)} async-done(((bf16[16,216,128]{2,1,0:T(8,128)(2,1)}), bf16[16,216,128]{2,1,0:T(8,128)(2,1)S(1)}, u32[]{:S(2)}, u32[]{:S(2)}) %all-to-all-start) | async-done | bytes 884768 | tf_op jit(solution)/shard_map/all_to_all | solution.py:401
  97.3 0.1 reduce_sum.12
  97.4 0.0 copy-start.13
  97.4 0.0 collective-permute-done.10.yp
  97.4 0.0 collective-permute-done.9.ym
  97.4 2.7 %collective-permute-start.11 = (bf16[216,128]{1,0:T(8,128)(2,1)S(1)}, bf16[216,128]{1,0:T(8,128)(2,1)S(1)}, u32[]{:S(2)}, u32[]{:S(2)}) collective-permute-start(bf16[216,128]{1,0:T(8,128)(2,1)S(1)} %reduce_sum.12), channel_id=1, source_target_pairs={{0,32},{32,0},{64,96},{96,64},{128,160},{160,128},{192,224},{224,1... | collective-permute-start | bytes 165896 | tf_op jit(solution)/shard_map/ppermute | solution.py:409
  100.1 1.5 %collective-permute-done.11 = bf16[216,128]{1,0:T(8,128)(2,1)S(1)} collective-permute-done((bf16[216,128]{1,0:T(8,128)(2,1)S(1)}, bf16[216,128]{1,0:T(8,128)(2,1)S(1)}, u32[]{:S(2)}, u32[]{:S(2)}) %collective-permute-start.11) | collective-permute-done | bytes 55328 | tf_op jit(solution)/shard_map/ppermute | solution.py:409
  101.7 4.4 %collective-permute-start.12 = (bf16[216,128]{1,0:T(8,128)(2,1)S(1)}, bf16[216,128]{1,0:T(8,128)(2,1)S(1)}, u32[]{:S(2)}, u32[]{:S(2)}) collective-permute-start(bf16[216,128]{1,0:T(8,128)(2,1)S(1)} %add_convert_fusion.2), channel_id=1, source_target_pairs={{0,96},{32,64},{64,32},{96,0},{128,224},{160,192},{192,160},{224,1... | collective-permute-start | bytes 165896 | tf_op jit(solution)/shard_map/ppermute | solution.py:409
  106.1 1.5 %collective-permute-done.12 = bf16[216,128]{1,0:T(8,128)(2,1)S(1)} collective-permute-done((bf16[216,128]{1,0:T(8,128)(2,1)S(1)}, bf16[216,128]{1,0:T(8,128)(2,1)S(1)}, u32[]{:S(2)}, u32[]{:S(2)}) %collective-permute-start.12) | collective-permute-done | bytes 55328 | tf_op jit(solution)/shard_map/ppermute | solution.py:409
  107.7 0.1 collective-permute-start.13
  107.8 4.6 %collective-permute-done.13 = bf16[216,128]{1,0:T(8,128)(2,1)S(1)} collective-permute-done((bf16[216,128]{1,0:T(8,128)(2,1)S(1)}, bf16[216,128]{1,0:T(8,128)(2,1)S(1)}, u32[]{:S(2)}, u32[]{:S(2)}) %collective-permute-start.13) | collective-permute-done | bytes 55328 | tf_op jit(solution)/shard_map/ppermute | solution.py:409
  112.4 1.0 broadcast_in_dim.2
  113.5 5.2 %all-to-all-start.1 = ((bf16[16,216,128]{2,1,0:T(8,128)(2,1)}), bf16[16,216,128]{2,1,0:T(8,128)(2,1)S(1)}, u32[]{:S(2)}, u32[]{:S(2)}) async-start(bf16[16,216,128]{2,1,0:T(8,128)(2,1)} %broadcast_in_dim.2), calls=%async_computation.1 | async-start | bytes 1769472 | tf_op jit(solution)/shard_map/all_to_all | solution.py:418
  118.7 5.5 %shard_map.98 = bf16[8,8,32,128]{3,2,1,0:T(8,128)(2,1)} custom-call(bf16[1,32,128]{2,1,0:T(8,128)(2,1)S(1)} %get-tuple-element.35.own, bf16[8,8,32,128]{3,2,1,0:T(8,128)(2,1)S(1)} %get-tuple-element.51.b1, bf16[8,8,32,128]{3,2,1,0:T(8,128)(2,1)S(1)} %copy-done.13, bf16[8,32,128]{2,1,0:T(8,128)(2,1)S(1)} %collective-permute-done.7.xm, ...), custom_call_target="tpu_custom_call" | custom-call | flops 1811939328 | bytes 4194304 | tf_op jit(solution)/shard_map/pallas_call | solution.py:384
  124.2 5.7 %all-to-all-done.1 = bf16[16,216,128]{2,1,0:T(8,128)(2,1)S(1)} async-done(((bf16[16,216,128]{2,1,0:T(8,128)(2,1)}), bf16[16,216,128]{2,1,0:T(8,128)(2,1)S(1)}, u32[]{:S(2)}, u32[]{:S(2)}) %all-to-all-start.1) | async-done | bytes 884768 | tf_op jit(solution)/shard_map/all_to_all | solution.py:418
  129.9 5.9 %collective-permute-start.14 = (bf16[3456,128]{1,0:T(8,128)(2,1)S(1)}, bf16[3456,128]{1,0:T(8,128)(2,1)S(1)}, u32[]{:S(2)}, u32[]{:S(2)}) collective-permute-start(bf16[3456,128]{1,0:T(8,128)(2,1)S(1)} %bitcast.30), channel_id=1, source_target_pairs={{0,1},{1,0},{2,3},{3,2},{4,5},{5,4},{6,7},{7,6},{8,9},{9,8},{10,11... | collective-permute-start | bytes 2654216 | tf_op jit(solution)/shard_map/ppermute | solution.py:396
  135.8 2.1 %collective-permute-done.14 = bf16[3456,128]{1,0:T(8,128)(2,1)S(1)} collective-permute-done((bf16[3456,128]{1,0:T(8,128)(2,1)S(1)}, bf16[3456,128]{1,0:T(8,128)(2,1)S(1)}, u32[]{:S(2)}, u32[]{:S(2)}) %collective-permute-start.14) | collective-permute-done | bytes 884768 | tf_op jit(solution)/shard_map/ppermute | solution.py:396
  137.8 0.1 broadcast_select_fusion
  137.9 1.4 convert.5
  139.3 1.4 convert.6
  (14 shorter events, 0.1 us)
Async XLA Ops:
  0.6 23.9 %copy-start = (bf16[27,128,128]{2,1,0:T(8,128)(2,1)S(1)}, bf16[27,128,128]{2,1,0:T(8,128)(2,1)}, u32[]{:S(2)}) copy-start(bf16[27,128,128]{2,1,0:T(8,128)(2,1)} %param.8) | copy-start | bytes 2654212
  1.4 1.0 copy-start.3
  2.4 1.0 copy-start.5
  3.5 0.7 copy-start.7
  4.1 26.2 %copy-start.4 = (bf16[1,8,8,4,8,128]{5,4,3,2,1,0:T(8,128)(2,1)S(1)}, bf16[1,8,8,4,8,128]{5,4,3,2,1,0:T(8,128)(2,1)}, u32[]{:S(2)}) copy-start(bf16[1,8,8,4,8,128]{5,4,3,2,1,0:T(8,128)(2,1)} %param.6) | copy-start | bytes 1572868
  5.6 10.1 %collective-permute-start = (bf16[33,32,128]{2,1,0:T(8,128)(2,1)S(1)}, bf16[33,32,128]{2,1,0:T(8,128)(2,1)S(1)}, u32[]{:S(2)}, u32[]{:S(2)}) collective-permute-start(bf16[33,32,128]{2,1,0:T(8,128)(2,1)S(1)} %get-tuple-element.36), channel_id=1, source_target_pairs={{0,32},{32,64},{64,96},{96,128},{128,160},{160,192},{192,224},{1,3... | collective-permute-start | bytes 811016 | tf_op jit(solution)/shard_map/ppermute | solution.py:23
  10.0 9.3 %collective-permute-start.1 = (bf16[33,32,128]{2,1,0:T(8,128)(2,1)S(1)}, bf16[33,32,128]{2,1,0:T(8,128)(2,1)S(1)}, u32[]{:S(2)}, u32[]{:S(2)}) collective-permute-start(bf16[33,32,128]{2,1,0:T(8,128)(2,1)S(1)} %get-tuple-element.37), channel_id=1, source_target_pairs={{32,0},{64,32},{96,64},{128,96},{160,128},{192,160},{224,192},{33,... | collective-permute-start | bytes 811016 | tf_op jit(solution)/shard_map/ppermute | solution.py:24
  11.3 15.2 %collective-permute-start.2 = (bf16[33,32,128]{2,1,0:T(8,128)(2,1)}, bf16[33,32,128]{2,1,0:T(8,128)(2,1)S(1)}, u32[]{:S(2)}, u32[]{:S(2)}) collective-permute-start(bf16[33,32,128]{2,1,0:T(8,128)(2,1)} %get-tuple-element.38), channel_id=1, source_target_pairs={{0,2},{2,4},{4,6},{6,8},{8,10},{10,12},{12,14},{14,16},{16,18},{18... | collective-permute-start | bytes 811016 | tf_op jit(solution)/shard_map/ppermute | solution.py:23
  14.5 12.8 %collective-permute-start.3 = (bf16[33,32,128]{2,1,0:T(8,128)(2,1)}, bf16[33,32,128]{2,1,0:T(8,128)(2,1)}, u32[]{:S(2)}, u32[]{:S(2)}) collective-permute-start(bf16[33,32,128]{2,1,0:T(8,128)(2,1)} %get-tuple-element.39), channel_id=1, source_target_pairs={{2,0},{4,2},{6,4},{8,6},{10,8},{12,10},{14,12},{16,14},{18,16},{20... | collective-permute-start | bytes 811016 | tf_op jit(solution)/shard_map/ppermute | solution.py:24
  20.1 7.2 %collective-permute-start.4 = (bf16[22,32,128]{2,1,0:T(8,128)(2,1)}, bf16[22,32,128]{2,1,0:T(8,128)(2,1)S(1)}, u32[]{:S(2)}, u32[]{:S(2)}) collective-permute-start(bf16[22,32,128]{2,1,0:T(8,128)(2,1)} %get-tuple-element.42), channel_id=1, source_target_pairs={{0,2},{2,4},{4,6},{6,8},{8,10},{10,12},{12,14},{14,16},{16,18},{18... | collective-permute-start | bytes 540680 | tf_op jit(solution)/shard_map/ppermute | solution.py:23
  23.2 6.4 %collective-permute-start.5 = (bf16[22,32,128]{2,1,0:T(8,128)(2,1)}, bf16[22,32,128]{2,1,0:T(8,128)(2,1)S(1)}, u32[]{:S(2)}, u32[]{:S(2)}) collective-permute-start(bf16[22,32,128]{2,1,0:T(8,128)(2,1)} %get-tuple-element.43), channel_id=1, source_target_pairs={{2,0},{4,2},{6,4},{8,6},{10,8},{12,10},{14,12},{16,14},{18,16},{20... | collective-permute-start | bytes 540680 | tf_op jit(solution)/shard_map/ppermute | solution.py:24
  24.5 1.2 copy-start.1
  25.7 4.6 %copy-start.2 = (bf16[27,128,128]{2,1,0:T(8,128)(2,1)S(1)}, bf16[27,128,128]{2,1,0:T(8,128)(2,1)}, u32[]{:S(2)}) copy-start(bf16[27,128,128]{2,1,0:T(8,128)(2,1)} %param.9) | copy-start | bytes 2654212
  25.7 4.6 %copy-start.6 = (bf16[1,8,8,4,8,128]{5,4,3,2,1,0:T(8,128)(2,1)S(1)}, bf16[1,8,8,4,8,128]{5,4,3,2,1,0:T(8,128)(2,1)}, u32[]{:S(2)}) copy-start(bf16[1,8,8,4,8,128]{5,4,3,2,1,0:T(8,128)(2,1)} %param.7) | copy-start | bytes 1572868
  26.5 0.7 copy-start.8
  29.6 0.7 copy-start.10
  30.3 1.0 copy-start.9
  31.3 0.9 copy-start.11
  59.8 15.0 %copy-start.12 = (bf16[8,8,32,128]{3,2,1,0:T(8,128)(2,1)}, bf16[8,8,32,128]{3,2,1,0:T(8,128)(2,1)S(1)}, u32[]{:S(2)}) copy-start(bf16[8,8,32,128]{3,2,1,0:T(8,128)(2,1)S(1)} %get-tuple-element.60.b2) | copy-start | bytes 1572868
  59.9 13.7 %collective-permute-start.6 = (bf16[3456,128]{1,0:T(8,128)(2,1)S(1)}, bf16[3456,128]{1,0:T(8,128)(2,1)S(1)}, u32[]{:S(2)}, u32[]{:S(2)}) collective-permute-start(bf16[3456,128]{1,0:T(8,128)(2,1)S(1)} %slice_bitcast_fusion), channel_id=1, source_target_pairs={{0,1},{1,0},{2,3},{3,2},{4,5},{5,4},{6,7},{7,6},{8,9},{9,8},{10,11... | collective-permute-start | bytes 2654216 | tf_op jit(solution)/shard_map/ppermute | solution.py:396
  63.1 5.1 %collective-permute-start.7 = (bf16[8,32,128]{2,1,0:T(8,128)(2,1)S(1)}, bf16[8,32,128]{2,1,0:T(8,128)(2,1)S(1)}, u32[]{:S(2)}, u32[]{:S(2)}) collective-permute-start(bf16[8,32,128]{2,1,0:T(8,128)(2,1)S(1)} %get-tuple-element.49), channel_id=1, source_target_pairs={{0,32},{32,64},{64,96},{96,128},{128,160},{160,192},{192,224},{1,3... | collective-permute-start | bytes 196616 | tf_op jit(solution)/shard_map/ppermute | solution.py:23
  66.7 7.0 %collective-permute-start.8 = (bf16[8,32,128]{2,1,0:T(8,128)(2,1)S(1)}, bf16[8,32,128]{2,1,0:T(8,128)(2,1)S(1)}, u32[]{:S(2)}, u32[]{:S(2)}) collective-permute-start(bf16[8,32,128]{2,1,0:T(8,128)(2,1)S(1)} %get-tuple-element.50), channel_id=1, source_target_pairs={{32,0},{64,32},{96,64},{128,96},{160,128},{192,160},{224,192},{33,... | collective-permute-start | bytes 196616 | tf_op jit(solution)/shard_map/ppermute | solution.py:24
  74.8 22.4 %all-to-all-start = ((bf16[16,216,128]{2,1,0:T(8,128)(2,1)}), bf16[16,216,128]{2,1,0:T(8,128)(2,1)S(1)}, u32[]{:S(2)}, u32[]{:S(2)}) async-start(bf16[16,216,128]{2,1,0:T(8,128)(2,1)} %bitcast.32), calls=%async_computation | async-start | bytes 1769472 | tf_op jit(solution)/shard_map/all_to_all | solution.py:401
  83.2 14.2 %collective-permute-start.10 = (bf16[10,32,128]{2,1,0:T(8,128)(2,1)S(1)}, bf16[10,32,128]{2,1,0:T(8,128)(2,1)S(1)}, u32[]{:S(2)}, u32[]{:S(2)}) collective-permute-start(bf16[10,32,128]{2,1,0:T(8,128)(2,1)S(1)} %get-tuple-element.56), channel_id=1, source_target_pairs={{2,0},{4,2},{6,4},{8,6},{10,8},{12,10},{14,12},{16,14},{18,16},{20... | collective-permute-start | bytes 245768 | tf_op jit(solution)/shard_map/ppermute | solution.py:24
  84.5 12.9 %collective-permute-start.9 = (bf16[10,32,128]{2,1,0:T(8,128)(2,1)S(1)}, bf16[10,32,128]{2,1,0:T(8,128)(2,1)S(1)}, u32[]{:S(2)}, u32[]{:S(2)}) collective-permute-start(bf16[10,32,128]{2,1,0:T(8,128)(2,1)S(1)} %get-tuple-element.55), channel_id=1, source_target_pairs={{0,2},{2,4},{4,6},{6,8},{8,10},{10,12},{12,14},{14,16},{16,18},{18... | collective-permute-start | bytes 245768 | tf_op jit(solution)/shard_map/ppermute | solution.py:23
  97.4 21.3 %copy-start.13 = (bf16[8,8,32,128]{3,2,1,0:T(8,128)(2,1)S(1)}, bf16[8,8,32,128]{3,2,1,0:T(8,128)(2,1)}, u32[]{:S(2)}) copy-start(bf16[8,8,32,128]{3,2,1,0:T(8,128)(2,1)} %copy-done.12) | copy-start | bytes 1572868
  97.4 4.3 %collective-permute-start.11 = (bf16[216,128]{1,0:T(8,128)(2,1)S(1)}, bf16[216,128]{1,0:T(8,128)(2,1)S(1)}, u32[]{:S(2)}, u32[]{:S(2)}) collective-permute-start(bf16[216,128]{1,0:T(8,128)(2,1)S(1)} %reduce_sum.12), channel_id=1, source_target_pairs={{0,32},{32,0},{64,96},{96,64},{128,160},{160,128},{192,224},{224,1... | collective-permute-start | bytes 165896 | tf_op jit(solution)/shard_map/ppermute | solution.py:409
  101.7 5.9 %collective-permute-start.12 = (bf16[216,128]{1,0:T(8,128)(2,1)S(1)}, bf16[216,128]{1,0:T(8,128)(2,1)S(1)}, u32[]{:S(2)}, u32[]{:S(2)}) collective-permute-start(bf16[216,128]{1,0:T(8,128)(2,1)S(1)} %add_convert_fusion.2), channel_id=1, source_target_pairs={{0,96},{32,64},{64,32},{96,0},{128,224},{160,192},{192,160},{224,1... | collective-permute-start | bytes 165896 | tf_op jit(solution)/shard_map/ppermute | solution.py:409
  107.7 4.7 %collective-permute-start.13 = (bf16[216,128]{1,0:T(8,128)(2,1)S(1)}, bf16[216,128]{1,0:T(8,128)(2,1)S(1)}, u32[]{:S(2)}, u32[]{:S(2)}) collective-permute-start(bf16[216,128]{1,0:T(8,128)(2,1)S(1)} %add_convert_fusion.1), channel_id=1, source_target_pairs={{0,224},{32,192},{64,160},{96,128},{128,96},{160,64},{192,32},{224... | collective-permute-start | bytes 165896 | tf_op jit(solution)/shard_map/ppermute | solution.py:409
  113.5 16.4 %all-to-all-start.1 = ((bf16[16,216,128]{2,1,0:T(8,128)(2,1)}), bf16[16,216,128]{2,1,0:T(8,128)(2,1)S(1)}, u32[]{:S(2)}, u32[]{:S(2)}) async-start(bf16[16,216,128]{2,1,0:T(8,128)(2,1)} %broadcast_in_dim.2), calls=%async_computation.1 | async-start | bytes 1769472 | tf_op jit(solution)/shard_map/all_to_all | solution.py:418
  129.9 7.9 %collective-permute-start.14 = (bf16[3456,128]{1,0:T(8,128)(2,1)S(1)}, bf16[3456,128]{1,0:T(8,128)(2,1)S(1)}, u32[]{:S(2)}, u32[]{:S(2)}) collective-permute-start(bf16[3456,128]{1,0:T(8,128)(2,1)S(1)} %bitcast.30), channel_id=1, source_target_pairs={{0,1},{1,0},{2,3},{3,2},{4,5},{5,4},{6,7},{7,6},{8,9},{9,8},{10,11... | collective-permute-start | bytes 2654216 | tf_op jit(solution)/shard_map/ppermute | solution.py:396

commit v3 on v2

--- a/solution.py
+++ b/solution.py
@@ -19,9 +19,9 @@
 
 
 def shift_pair(low, high, axis):
-    ends = lax.axis_size(axis) - 1
-    from_low = lax.ppermute(high, axis, [(i, i + 1) for i in range(ends)])
-    from_high = lax.ppermute(low, axis, [(i + 1, i) for i in range(ends)])
+    n = lax.axis_size(axis)
+    from_low = lax.ppermute(high, axis, [(i, (i + 1) % n) for i in range(n)])
+    from_high = lax.ppermute(low, axis, [((i + 1) % n, i) for i in range(n)])
     return from_low, from_high
 
 
@@ -190,7 +190,10 @@
     copy.wait()
 
 
-def first_payload_kernel(links, count, x, cot, xlow, xhigh, ylow, yhigh, own):
+def first_payload_kernel(links, count, x_far, cot_far, xlow, xhigh, ylow, yhigh, own, x, cot, sems):
+    copies = [pltpu.make_async_copy(x_far, x, sems.at[0]), pltpu.make_async_copy(cot_far, cot, sems.at[1])]
+    for copy in copies:
+        copy.start()
     lane = lax.broadcasted_iota(jnp.int32, (ROWS, C), 1)
     row = jnp.zeros((ROWS, C), jnp.int32)
     for s in range(NB):
@@ -203,6 +206,8 @@
             row = jnp.where(lane == s * 27 + d, start, row)
     line = row.astype(F32).astype(BF16)
     own[0] = line
+    for copy in copies:
+        copy.wait()
     for ref, xa, xc in ((xlow, 0, 0), (xhigh, 5, 7)):
         ref[0:24] = x[xa : xa + 3].reshape(24, ROWS, C)
         ref[24:32] = cot[xc]
@@ -230,18 +235,28 @@
         ref[9] = xp[y]
 
 
-def main_kernel(scale, core, own, x, cot, xm, xp, ym, yp, qm, qp, w1, w2, w2f, out, b2o, b1o, elow, ehigh, gr,
-                field, hid, back, p1, p2, px, py, pc, slope1, turned, wide, staged, tab, sem):
+def main_kernel(scale, core, *refs):
+    far, own, refs = refs[:11], refs[11], refs[12:]
+    out, b2o, b1o, elow, ehigh, gr = refs[:6]
+    near, (sems, field, hid, back, p1, p2, px, py, pc, slope1, turned, wide, staged, tab, sem) = refs[6:17], refs[17:]
+    x, cot, xm, xp, ym, yp, qm, qp, w1, w2, w2f = near
+    copies = [pltpu.make_async_copy(far[i], near[i], sems.at[i]) for i in range(11)]
+    order = [8, 0, 2, 3, 4, 5, 6, 7, 1, 9, 10]
+    for i in order:
+        copies[i].start()
+    for ref in (field, hid, back):
+        zero_slot(ref)
+    clear_turned(turned)
+    clear_band(wide)
+    copies[8].wait()
+    band(w1, wide)
+    for i in order[1:8]:
+        copies[i].wait()
     load_tables(
         {0: (qm, 20), 1: (xm, 32), 2: (qp, 20), 3: (ym, 32), 4: (own, 0), 5: (yp, 32), 6: (qm, 21), 7: (xp, 32), 8: (qp, 21)},
         staged, tab, sem,
     )
     live = live_rows(tab)
-    for ref in (field, hid, back):
-        zero_slot(ref)
-    clear_turned(turned)
-    clear_band(wide)
-    band(w1, wide)
 
     def fill(i, unused):
         field[3 + i, 3:11, 0:ROWS, :] = x[i].astype(F32)
@@ -299,6 +314,8 @@
             hid[ax + h, ay : ay + 2, 0:ROWS, :] = value[j]
 
     ends = spans(1)
+    for i in order[8:]:
+        copies[i].wait()
     band(w2, wide)
     build_patches(tab, hid, into(p2), 2, OWN, ends[0], ends[0])
     for j, cx in enumerate((-1, 1)):
@@ -378,13 +395,18 @@
     lax.fori_loop(0, 2, step, 0)
 
 
-def call(kernel, outs, scratch, cost, mib, scalars, *args):
+def call(kernel, outs, scratch, cost, mib, scalars, far, *args):
     smem = pl.BlockSpec(memory_space=pltpu.SMEM)
     vmem = pl.BlockSpec(memory_space=pltpu.VMEM)
+    anywhere = pl.BlockSpec(memory_space=pltpu.HBM)
+    args = [
+        pltpu.with_memory_space_constraint(arg, pltpu.HBM) if scalars <= i < scalars + far else arg
+        for i, arg in enumerate(args)
+    ]
     return pl.pallas_call(
         kernel,
         out_shape=outs,
-        in_specs=[smem] * scalars + [vmem] * (len(args) - scalars),
+        in_specs=[smem] * scalars + [anywhere] * far + [vmem] * (len(args) - scalars - far),
         out_specs=jax.tree.map(lambda o: vmem, outs),
         scratch_shapes=scratch,
         compiler_params=pltpu.CompilerParams(vmem_limit_bytes=mib * 2**20),
@@ -432,15 +454,16 @@
 
     payload = shape_of(33, ROWS, C)
     xlow, xhigh, ylow, yhigh, own = call(
-        first_payload_kernel, [payload] * 4 + [shape_of(1, ROWS, C)], [], (0, 2**21), 8, 2,
+        first_payload_kernel, [payload] * 4 + [shape_of(1, ROWS, C)],
+        [pltpu.VMEM((BE, BE, ROWS, C), BF16)] * 2 + [pltpu.SemaphoreType.DMA((2,))], (0, 2**21), 8, 2, 2,
         neighbours.reshape(NB, 26), counts.reshape(1), x, cot,
     )
     xm, xp = shift_pair(xlow, xhigh, "sx")
     ym, yp = shift_pair(ylow, yhigh, "sy")
-    qlow, qhigh = call(corner_payload_kernel, [shape_of(22, ROWS, C)] * 2, [], (0, 2**19), 8, 0, xm, xp)
+    qlow, qhigh = call(corner_payload_kernel, [shape_of(22, ROWS, C)] * 2, [], (0, 2**19), 8, 0, 0, xm, xp)
     held1, held2, qlow, qhigh = lax.optimization_barrier((w1, w2, qlow, qhigh))
     qm, qp = shift_pair(qlow, qhigh, "sy")
-    w1f, w2f = call(flip_kernel, [shape_of(27 * C, C)] * 2, [], (2**24, 2**22), 8, 0, held1, held2)
+    w1f, w2f = call(flip_kernel, [shape_of(27 * C, C)] * 2, [], (2**24, 2**22), 8, 0, 0, held1, held2)
 
     block, edge = shape_of(BE, BE, ROWS, C), shape_of(BE, ROWS, C)
     lanes = 3 * C
@@ -450,6 +473,11 @@
         functools.partial(main_kernel, scale),
         [block, block, block, edge, edge, shape_of(2, 27 * C, C)],
         [
+            *[pltpu.VMEM((BE, BE, ROWS, C), BF16)] * 2,
+            *[pltpu.VMEM((33, ROWS, C), BF16)] * 4,
+            *[pltpu.VMEM((22, ROWS, C), BF16)] * 2,
+            *[pltpu.VMEM((27 * C, C), BF16)] * 3,
+            pltpu.SemaphoreType.DMA((11,)),
             pltpu.VMEM((14, 14, ROWS + BE, C), F32),
             pltpu.VMEM((12, 12, ROWS + BE, C), F32),
             pltpu.VMEM((10, 10, ROWS + BE, C), F32),
@@ -463,18 +491,17 @@
             pltpu.VMEM((36 * C, 2 * C), BF16),
             *tables,
         ],
-        (7 * unit, 10 * 2**20), 32, 1,
-        core.reshape(1), own, x, cot, xm, xp, ym, yp, qm, qp, w1, w2, w2f,
+        (7 * unit, 10 * 2**20), 40, 1, 11,
+        core.reshape(1), x, cot, xm, xp, ym, yp, qm, qp, w1, w2, w2f, own,
     )
 
     received = swap_cores(grads[1])
     bxm, bxp = shift_pair(elow, ehigh, "sx")
     part = (grads[0].astype(F32) + received.astype(F32)).astype(BF16)
-    blow, bhigh = call(edge_payload_kernel, [shape_of(BE + 2, ROWS, C)] * 2, [], (0, 2**19), 8, 0, bxm, bxp, b1)
-    part, blow, bhigh = lax.optimization_barrier((part, blow, bhigh))
+    part, bxm, bxp = lax.optimization_barrier((sum_scatter(part, "sy"), bxm, bxp))
+    blow, bhigh = call(edge_payload_kernel, [shape_of(BE + 2, ROWS, C)] * 2, [], (0, 2**19), 8, 0, 0, bxm, bxp, b1)
     bym, byp = shift_pair(blow, bhigh, "sy")
-    part, bym, byp = lax.optimization_barrier((sum_scatter(part, "sy"), bym, byp))
-    part, b2 = lax.optimization_barrier((sum_pairs(part, "sx"), b2))
+    part, bym, byp, b2 = lax.optimization_barrier((sum_pairs(part, "sx"), bym, byp, b2))
 
     grad_input = call(
         last_kernel,
@@ -485,13 +512,14 @@
             pltpu.VMEM((36 * C, 2 * C), BF16),
             *tables,
         ],
-        (unit, 4 * 2**20), 12, 0,
+        (unit, 4 * 2**20), 12, 0, 0,
         own, b1, b2, bxm, bxp, bym, byp, w1f,
     )
     part, grad_input = lax.optimization_barrier((gather_axis(part, "sy"), grad_input))
+    part = part.reshape(27, C, C)
     other = swap_cores(part)
-    first = jnp.where(core == 0, part, other).astype(F32).reshape(27, C, C)
-    second = jnp.where(core == 0, other, part).astype(F32).reshape(27, C, C)
+    first = jnp.where(core == 0, part, other).astype(F32)
+    second = jnp.where(core == 0, other, part).astype(F32)
     shape = features.shape
     return out.reshape(shape), grad_input.reshape(shape), first, second
 

time: 141 us -> 128 us (0.908)
  waiting for transfers between devices: 36 us -> 29.6 us
  local copies, waits for them, and re-layouts: 8.28 us -> 3.85 us
  starting transfers between devices: 54.4 us -> 52.3 us
    ppermute x10, waiting for transfers between devices: 11.7 us -> 3.41 us  [the longest x5 3.4 us: shift_pair(): from_low = lax.ppermute(high, axis, [(i, (i + 1) % n) for i in range(n)])]
    unnamed x28 -> x12, local copies, waits for them, and re-layouts: 7.19 us -> 2.76 us
    ppermute x3, waiting for transfers between devices: 7.73 us -> 4.54 us  [sum_pairs(): other = lax.ppermute(part, axis, [(i, i ^ 2 * reach - 1) for i in range(n)])]
    all_to_all x1, waiting for transfers between devices: 8.79 us -> 11.9 us  [sum_scatter(): lax.all_to_all(part.reshape(n, part.shape[0] // n, C), axis, 0, 0, tiled=...]
    reshape x2 -> x0, other arithmetic: 2.81 us -> none  [the longest x1 1.41 us: shards(): first = jnp.where(core == 0, part, other).astype(F32).reshape(27, C, C)]
    ppermute x2, waiting for transfers between devices: 2.06 us -> 4.11 us  [swap_cores(): return lax.ppermute(part, 'dp', [(0, 1), (1, 0)])]
    convert_element_type x0 -> x1, other arithmetic: none -> 2.02 us  [shards(): second = jnp.where(core == 0, other, part).astype(F32)]
    all_to_all x1, starting transfers between devices: 8.33 us -> 6.43 us  [sum_scatter(): lax.all_to_all(part.reshape(n, part.shape[0] // n, C), axis, 0, 0, tiled=...]
  transfers between devices with their start and end apart: 17 -> 17, of which waited for: 10 -> 9; matrix products, arithmetic and copies ran while one was open for 0% -> 1% of each run, Pallas kernels for 5% -> 5%
where the time goes in v3:
time: 128 us
  starting transfers between devices  52.3 us (41%)
  Pallas kernels  36.2 us (28%)
  waiting for transfers between devices  29.6 us (23%)
  other arithmetic  4.51 us (4%)
  local copies, waits for them, and re-layouts  3.85 us (3%)
  between operations  1.51 us (1%)
    pallas_call x6, Pallas kernels, call(): pl.pallas_call(kernel, out_shape=outs, in_specs=[smem] * scalars + [anywh...  36.2 us
    ppermute x5, starting transfers between devices, shift_pair(): from_high = lax.ppermute(low, axis, [((i + 1) % n, i) for i in range(n)])  18.8 us
    all_to_all x1, waiting for transfers between devices, sum_scatter(): lax.all_to_all(part.reshape(n, part.shape[0] // n, C), axis, 0, 0, tiled=...  11.9 us
    ppermute x2, starting transfers between devices, swap_cores(): return lax.ppermute(part, 'dp', [(0, 1), (1, 0)])  9.3 us
    all_to_all x1, starting transfers between devices, sum_scatter(): lax.all_to_all(part.reshape(n, part.shape[0] // n, C), axis, 0, 0, tiled=...  6.43 us
    all_to_all x1, starting transfers between devices, gather_axis(): lax.all_to_all(copies, axis, 0, 0, tiled=True).reshape(n * part.shape[0], C)  6.16 us
    ppermute x3, starting transfers between devices, sum_pairs(): other = lax.ppermute(part, axis, [(i, i ^ 2 * reach - 1) for i in range(n)])  6.06 us
    all_to_all x1, waiting for transfers between devices, gather_axis(): lax.all_to_all(copies, axis, 0, 0, tiled=True).reshape(n * part.shape[0], C)  5.7 us
  transfers between devices with their start and end apart: 17, of which 9 were waited for; matrix products, arithmetic and copies ran while one was open for 1% of the time, Pallas kernels for 5%

profile of v3, /device:TPU:1, one launch (start us, length us, event | category | flops | bytes accessed | tf_op | source)
XLA Modules:
  0.0 128.1 jit_solution(1853221791052425197)
XLA Ops:
  0.6 0.0 copy-start
  1.4 0.0 copy-start.4
  1.4 0.7 copy-done.4
  2.0 1.9 %shard_map.93 = (bf16[33,32,128]{2,1,0:T(8,128)(2,1)S(1)}, bf16[33,32,128]{2,1,0:T(8,128)(2,1)S(1)}, bf16[33,32,128]{2,1,0:T(8,128)(2,1)S(1)}, bf16[33,32,128]{2,1,0:T(8,128)(2,1)S(1)}, bf16[1,32,128]{2,1,0:T(8,128)(2,1)S(1)}) custom-call(s32[4,26]{1,0:T(4,128)S(1)} %bitcast.22, s32[1]{0:T(128)} %bitcast.17.count, bf16[8,8,32,128]{3,2,1,0:T(8,128)(2,1)} %bitcast.25, ...), custom_call_target="tpu_custom_call" | custom-call | bytes 2097152 | tf_op jit(solution)/shard_map/pallas_call | solution.py:406
  3.9 2.5 %collective-permute-start = (bf16[33,32,128]{2,1,0:T(8,128)(2,1)S(1)}, bf16[33,32,128]{2,1,0:T(8,128)(2,1)S(1)}, u32[]{:S(2)}, u32[]{:S(2)}) collective-permute-start(bf16[33,32,128]{2,1,0:T(8,128)(2,1)S(1)} %get-tuple-element.34), channel_id=1, source_target_pairs={{0,32},{32,64},{64,96},{96,128},{128,160},{160,192},{192,224},{224... | collective-permute-start | bytes 811016 | tf_op jit(solution)/shard_map/ppermute | solution.py:23
  6.5 4.0 %collective-permute-start.1 = (bf16[33,32,128]{2,1,0:T(8,128)(2,1)S(1)}, bf16[33,32,128]{2,1,0:T(8,128)(2,1)S(1)}, u32[]{:S(2)}, u32[]{:S(2)}) collective-permute-start(bf16[33,32,128]{2,1,0:T(8,128)(2,1)S(1)} %get-tuple-element.35), channel_id=1, source_target_pairs={{32,0},{64,32},{96,64},{128,96},{160,128},{192,160},{224,192},{0,2... | collective-permute-start | bytes 811016 | tf_op jit(solution)/shard_map/ppermute | solution.py:24
  10.5 1.2 collective-permute-start.2
  11.7 3.7 %collective-permute-start.3 = (bf16[33,32,128]{2,1,0:T(8,128)(2,1)S(1)}, bf16[33,32,128]{2,1,0:T(8,128)(2,1)}, u32[]{:S(2)}, u32[]{:S(2)}) collective-permute-start(bf16[33,32,128]{2,1,0:T(8,128)(2,1)S(1)} %get-tuple-element.37), channel_id=1, source_target_pairs={{2,0},{4,2},{6,4},{8,6},{10,8},{12,10},{14,12},{16,14},{18,16},{20... | collective-permute-start | bytes 811016 | tf_op jit(solution)/shard_map/ppermute | solution.py:24
  15.4 1.2 collective-permute-done.xm.refs_2_
  16.6 0.0 copy-start.2
  16.6 0.0 collective-permute-done.1.xp.refs_3_
  16.6 0.0 copy-start.3
  16.7 1.3 %collective-permute-start.4 = (bf16[22,32,128]{2,1,0:T(8,128)(2,1)S(1)}, bf16[22,32,128]{2,1,0:T(8,128)(2,1)}, u32[]{:S(2)}, u32[]{:S(2)}) collective-permute-start(bf16[22,32,128]{2,1,0:T(8,128)(2,1)S(1)} %get-tuple-element.40), channel_id=1, source_target_pairs={{0,2},{2,4},{4,6},{6,8},{8,10},{10,12},{12,14},{14,16},{16,18},{18... | collective-permute-start | bytes 540680 | tf_op jit(solution)/shard_map/ppermute | solution.py:23
  18.0 4.0 %collective-permute-start.5 = (bf16[22,32,128]{2,1,0:T(8,128)(2,1)S(1)}, bf16[22,32,128]{2,1,0:T(8,128)(2,1)}, u32[]{:S(2)}, u32[]{:S(2)}) collective-permute-start(bf16[22,32,128]{2,1,0:T(8,128)(2,1)S(1)} %get-tuple-element.41), channel_id=1, source_target_pairs={{2,0},{4,2},{6,4},{8,6},{10,8},{12,10},{14,12},{16,14},{18,16},{20... | collective-permute-start | bytes 540680 | tf_op jit(solution)/shard_map/ppermute | solution.py:24
  21.9 0.0 copy-done
  21.9 0.0 copy-start.1
  21.9 1.2 copy-done.1
  23.1 0.8 shard_map.95
  23.9 0.0 copy-start.5
  24.0 0.9 copy-done.5
  24.9 0.0 collective-permute-done.2.refs_4_
  24.9 0.0 collective-permute-done.3.refs_5_
  24.9 0.4 collective-permute-done.4.refs_6_
  25.3 0.0 collective-permute-done.5.refs_7_
  25.3 0.0 copy-done.2
  25.3 0.0 copy-done.3
  25.3 28.0 %shard_map.96 = (bf16[8,8,32,128]{3,2,1,0:T(8,128)(2,1)}, bf16[8,8,32,128]{3,2,1,0:T(8,128)(2,1)S(1)}, bf16[8,8,32,128]{3,2,1,0:T(8,128)(2,1)S(1)}, bf16[8,32,12...) custom-call(s32[1]{0:T(128)} %bitcast.core, ...), custom_call_target="tpu_custom_call" | custom-call | flops 12683575296 | bytes 10485760 | tf_op jit(solution)/shard_map/pallas_call | solution.py:406
  53.3 0.1 slice_bitcast_fusion
  53.3 2.1 %collective-permute-start.6 = (bf16[3456,128]{1,0:T(8,128)(2,1)S(1)}, bf16[3456,128]{1,0:T(8,128)(2,1)S(1)}, u32[]{:S(2)}, u32[]{:S(2)}) collective-permute-start(bf16[3456,128]{1,0:T(8,128)(2,1)S(1)} %slice_bitcast_fusion), channel_id=1, source_target_pairs={{0,1},{1,0},{2,3},{3,2},{4,5},{5,4},{6,7},{7,6},{8,9},{9,8},{10,11... | collective-permute-start | bytes 2654216 | tf_op jit(solution)/shard_map/ppermute | solution.py:418
  55.4 2.1 %collective-permute-done.6 = bf16[3456,128]{1,0:T(8,128)(2,1)S(1)} collective-permute-done((bf16[3456,128]{1,0:T(8,128)(2,1)S(1)}, bf16[3456,128]{1,0:T(8,128)(2,1)S(1)}, u32[]{:S(2)}, u32[]{:S(2)}) %collective-permute-start.6) | collective-permute-done | bytes 884768 | tf_op jit(solution)/shard_map/ppermute | solution.py:418
  57.5 1.1 fusion
  58.6 6.4 %all-to-all-start = ((bf16[16,216,128]{2,1,0:T(8,128)(2,1)}), bf16[16,216,128]{2,1,0:T(8,128)(2,1)}, u32[]{:S(2)}, u32[]{:S(2)}) async-start(bf16[16,216,128]{2,1,0:T(8,128)(2,1)} %bitcast.10), calls=%async_computation | async-start | bytes 1769472 | tf_op jit(solution)/shard_map/all_to_all | solution.py:423
  65.1 0.1 collective-permute-start.7
  65.1 2.7 %collective-permute-start.8 = (bf16[8,32,128]{2,1,0:T(8,128)(2,1)S(1)}, bf16[8,32,128]{2,1,0:T(8,128)(2,1)S(1)}, u32[]{:S(2)}, u32[]{:S(2)}) collective-permute-start(bf16[8,32,128]{2,1,0:T(8,128)(2,1)S(1)} %get-tuple-element.49), channel_id=1, source_target_pairs={{32,0},{64,32},{96,64},{128,96},{160,128},{192,160},{224,192},{0,2... | collective-permute-start | bytes 196616 | tf_op jit(solution)/shard_map/ppermute | solution.py:24
  67.8 11.9 %all-to-all-done = bf16[16,216,128]{2,1,0:T(8,128)(2,1)} async-done(((bf16[16,216,128]{2,1,0:T(8,128)(2,1)}), bf16[16,216,128]{2,1,0:T(8,128)(2,1)}, u32[]{:S(2)}, u32[]{:S(2)}) %all-to-all-start) | async-done | bytes 884768 | tf_op jit(solution)/shard_map/all_to_all | solution.py:423
  79.7 1.3 %reduce_sum.12 = bf16[216,128]{1,0:T(8,128)(2,1)S(1)} reduce(bf16[16,216,128]{2,1,0:T(8,128)(2,1)} %all-to-all-done, bf16[]{:T(256)} %constant.2.clone.1), dimensions={0}, to_apply=%region_0.0 | reduce | flops 414720 | bytes 940034 | tf_op jit(solution)/shard_map/reduce_sum | solution.py:424
  81.0 0.0 collective-permute-done.7.xm
  81.0 0.0 collective-permute-done.8.xp
  81.0 0.1 collective-permute-start.9
  81.1 3.0 %collective-permute-done.9 = bf16[216,128]{1,0:T(8,128)(2,1)S(1)} collective-permute-done((bf16[216,128]{1,0:T(8,128)(2,1)S(1)}, bf16[216,128]{1,0:T(8,128)(2,1)S(1)}, u32[]{:S(2)}, u32[]{:S(2)}) %collective-permute-start.9) | collective-permute-done | bytes 55328 | tf_op jit(solution)/shard_map/ppermute | solution.py:431
  84.1 4.2 %collective-permute-start.10 = (bf16[216,128]{1,0:T(8,128)(2,1)S(1)}, bf16[216,128]{1,0:T(8,128)(2,1)S(1)}, u32[]{:S(2)}, u32[]{:S(2)}) collective-permute-start(bf16[216,128]{1,0:T(8,128)(2,1)S(1)} %add_convert_fusion.2), channel_id=1, source_target_pairs={{0,96},{32,64},{64,32},{96,0},{128,224},{160,192},{192,160},{224,1... | collective-permute-start | bytes 165896 | tf_op jit(solution)/shard_map/ppermute | solution.py:431
  88.3 1.5 %collective-permute-done.10 = bf16[216,128]{1,0:T(8,128)(2,1)S(1)} collective-permute-done((bf16[216,128]{1,0:T(8,128)(2,1)S(1)}, bf16[216,128]{1,0:T(8,128)(2,1)S(1)}, u32[]{:S(2)}, u32[]{:S(2)}) %collective-permute-start.10) | collective-permute-done | bytes 55328 | tf_op jit(solution)/shard_map/ppermute | solution.py:431
  89.9 1.8 %collective-permute-start.11 = (bf16[216,128]{1,0:T(8,128)(2,1)S(1)}, bf16[216,128]{1,0:T(8,128)(2,1)S(1)}, u32[]{:S(2)}, u32[]{:S(2)}) collective-permute-start(bf16[216,128]{1,0:T(8,128)(2,1)S(1)} %add_convert_fusion.1), channel_id=1, source_target_pairs={{0,224},{32,192},{64,160},{96,128},{128,96},{160,64},{192,32},{224... | collective-permute-start | bytes 165896 | tf_op jit(solution)/shard_map/ppermute | solution.py:431
  91.7 0.4 collective-permute-start.12
  92.1 4.4 %collective-permute-start.13 = (bf16[10,32,128]{2,1,0:T(8,128)(2,1)S(1)}, bf16[10,32,128]{2,1,0:T(8,128)(2,1)S(1)}, u32[]{:S(2)}, u32[]{:S(2)}) collective-permute-start(bf16[10,32,128]{2,1,0:T(8,128)(2,1)S(1)} %get-tuple-element.55), channel_id=1, source_target_pairs={{2,0},{4,2},{6,4},{8,6},{10,8},{12,10},{14,12},{16,14},{18,16},{20... | collective-permute-start | bytes 245768 | tf_op jit(solution)/shard_map/ppermute | solution.py:24
  96.5 0.0 collective-permute-done.11
  96.6 1.8 %collective-permute-done.12.ym = bf16[10,32,128]{2,1,0:T(8,128)(2,1)S(1)} collective-permute-done((bf16[10,32,128]{2,1,0:T(8,128)(2,1)S(1)}, bf16[10,32,128]{2,1,0:T(8,128)(2,1)S(1)}, u32[]{:S(2)}, u32[]{:S(2)}) %collective-permute-start.12) | collective-permute-done | bytes 81952 | tf_op jit(solution)/shard_map/ppermute | solution.py:23
  98.4 0.0 collective-permute-done.13.yp
  98.4 1.0 broadcast_in_dim.2
  99.4 6.2 %all-to-all-start.1 = ((bf16[16,216,128]{2,1,0:T(8,128)(2,1)}), bf16[16,216,128]{2,1,0:T(8,128)(2,1)S(1)}, u32[]{:S(2)}, u32[]{:S(2)}) async-start(bf16[16,216,128]{2,1,0:T(8,128)(2,1)} %broadcast_in_dim.2), calls=%async_computation.1 | async-start | bytes 1769472 | tf_op jit(solution)/shard_map/all_to_all | solution.py:440
  105.6 5.5 %shard_map.98 = bf16[8,8,32,128]{3,2,1,0:T(8,128)(2,1)} custom-call(bf16[1,32,128]{2,1,0:T(8,128)(2,1)S(1)} %get-tuple-element.45.refs_11_.own, bf16[8,8,32,128]{3,2,1,0:T(8,128)(2,1)S(1)} %get-tuple-element.53.b1, bf16[8,8,32,128]{3,2,1,0:T(8,128)(2,1)S(1)} %get-tuple-element.58.b2, bf16[8,32,128]{2,1,0:T(8,128)(2,1)S(1)} %collective-permute-done.7.xm, ...), custom_call_target="tpu_custom_call" | custom-call | flops 1811939328 | bytes 4194304 | tf_op jit(solution)/shard_map/pallas_call | solution.py:406
  111.1 5.7 %all-to-all-done.1 = bf16[16,216,128]{2,1,0:T(8,128)(2,1)S(1)} async-done(((bf16[16,216,128]{2,1,0:T(8,128)(2,1)}), bf16[16,216,128]{2,1,0:T(8,128)(2,1)S(1)}, u32[]{:S(2)}, u32[]{:S(2)}) %all-to-all-start.1) | async-done | bytes 884768 | tf_op jit(solution)/shard_map/all_to_all | solution.py:440
  116.8 7.2 %collective-permute-start.14 = (bf16[27,128,128]{2,1,0:T(8,128)(2,1)S(1)}, bf16[27,128,128]{2,1,0:T(8,128)(2,1)S(1)}, u32[]{:S(2)}, u32[]{:S(2)}) collective-permute-start(bf16[27,128,128]{2,1,0:T(8,128)(2,1)S(1)} %bitcast.23), channel_id=1, source_target_pairs={{0,1},{1,0},{2,3},{3,2},{4,5},{5,4},{6,7},{7,6},{8,9},{9,8},{10,11... | collective-permute-start | bytes 2654216 | tf_op jit(solution)/shard_map/ppermute | solution.py:418
  124.0 2.1 %collective-permute-done.14 = bf16[27,128,128]{2,1,0:T(8,128)(2,1)S(1)} collective-permute-done((bf16[27,128,128]{2,1,0:T(8,128)(2,1)S(1)}, bf16[27,128,128]{2,1,0:T(8,128)(2,1)S(1)}, u32[]{:S(2)}, u32[]{:S(2)}) %collective-permute-start.14) | collective-permute-done | bytes 884768 | tf_op jit(solution)/shard_map/ppermute | solution.py:418
  126.0 2.0 %select_convert_fusion = (f32[27,128,128]{2,1,0:T(8,128)}, f32[27,128,128]{2,1,0:T(8,128)}) fusion(bf16[27,128,128]{2,1,0:T(8,128)(2,1)S(1)} %collective-permute-done.14, bf16[27,128,128]{2,1,0:T(8,128)(2,1)S(1)} %bitcast.24, pred[]{:T(512)S(6)} %eq.4), kind=kLoop, calls=%fused_computation.2 | loop fusion | flops 1769472 | bytes 5308417 | tf_op jit(solution)/shard_map/convert_element_type | solution.py:522
  (5 shorter events, 0.1 us)
Async XLA Ops:
  0.6 21.3 %copy-start = (bf16[27,128,128]{2,1,0:T(8,128)(2,1)S(1)}, bf16[27,128,128]{2,1,0:T(8,128)(2,1)}, u32[]{:S(2)}) copy-start(bf16[27,128,128]{2,1,0:T(8,128)(2,1)} %param.8) | copy-start | bytes 2654212
  1.4 0.7 copy-start.4
  3.9 12.7 %collective-permute-start = (bf16[33,32,128]{2,1,0:T(8,128)(2,1)S(1)}, bf16[33,32,128]{2,1,0:T(8,128)(2,1)S(1)}, u32[]{:S(2)}, u32[]{:S(2)}) collective-permute-start(bf16[33,32,128]{2,1,0:T(8,128)(2,1)S(1)} %get-tuple-element.34), channel_id=1, source_target_pairs={{0,32},{32,64},{64,96},{96,128},{128,160},{160,192},{192,224},{224... | collective-permute-start | bytes 811016 | tf_op jit(solution)/shard_map/ppermute | solution.py:23
  6.5 10.2 %collective-permute-start.1 = (bf16[33,32,128]{2,1,0:T(8,128)(2,1)S(1)}, bf16[33,32,128]{2,1,0:T(8,128)(2,1)S(1)}, u32[]{:S(2)}, u32[]{:S(2)}) collective-permute-start(bf16[33,32,128]{2,1,0:T(8,128)(2,1)S(1)} %get-tuple-element.35), channel_id=1, source_target_pairs={{32,0},{64,32},{96,64},{128,96},{160,128},{192,160},{224,192},{0,2... | collective-permute-start | bytes 811016 | tf_op jit(solution)/shard_map/ppermute | solution.py:24
  10.5 14.4 %collective-permute-start.2 = (bf16[33,32,128]{2,1,0:T(8,128)(2,1)S(1)}, bf16[33,32,128]{2,1,0:T(8,128)(2,1)}, u32[]{:S(2)}, u32[]{:S(2)}) collective-permute-start(bf16[33,32,128]{2,1,0:T(8,128)(2,1)S(1)} %get-tuple-element.36), channel_id=1, source_target_pairs={{0,2},{2,4},{4,6},{6,8},{8,10},{10,12},{12,14},{14,16},{16,18},{18... | collective-permute-start | bytes 811016 | tf_op jit(solution)/shard_map/ppermute | solution.py:23
  11.7 13.1 %collective-permute-start.3 = (bf16[33,32,128]{2,1,0:T(8,128)(2,1)S(1)}, bf16[33,32,128]{2,1,0:T(8,128)(2,1)}, u32[]{:S(2)}, u32[]{:S(2)}) collective-permute-start(bf16[33,32,128]{2,1,0:T(8,128)(2,1)S(1)} %get-tuple-element.37), channel_id=1, source_target_pairs={{2,0},{4,2},{6,4},{8,6},{10,8},{12,10},{14,12},{16,14},{18,16},{20... | collective-permute-start | bytes 811016 | tf_op jit(solution)/shard_map/ppermute | solution.py:24
  16.6 8.7 %copy-start.2 = (bf16[33,32,128]{2,1,0:T(8,128)(2,1)}, bf16[33,32,128]{2,1,0:T(8,128)(2,1)S(1)}, u32[]{:S(2)}) copy-start(bf16[33,32,128]{2,1,0:T(8,128)(2,1)S(1)} %collective-permute-done.xm.refs_2_) | copy-start | bytes 811012
  16.6 8.7 %copy-start.3 = (bf16[33,32,128]{2,1,0:T(8,128)(2,1)}, bf16[33,32,128]{2,1,0:T(8,128)(2,1)S(1)}, u32[]{:S(2)}) copy-start(bf16[33,32,128]{2,1,0:T(8,128)(2,1)S(1)} %collective-permute-done.1.xp.refs_3_) | copy-start | bytes 811012
  16.7 8.6 %collective-permute-start.4 = (bf16[22,32,128]{2,1,0:T(8,128)(2,1)S(1)}, bf16[22,32,128]{2,1,0:T(8,128)(2,1)}, u32[]{:S(2)}, u32[]{:S(2)}) collective-permute-start(bf16[22,32,128]{2,1,0:T(8,128)(2,1)S(1)} %get-tuple-element.40), channel_id=1, source_target_pairs={{0,2},{2,4},{4,6},{6,8},{8,10},{10,12},{12,14},{14,16},{16,18},{18... | collective-permute-start | bytes 540680 | tf_op jit(solution)/shard_map/ppermute | solution.py:23
  18.0 7.3 %collective-permute-start.5 = (bf16[22,32,128]{2,1,0:T(8,128)(2,1)S(1)}, bf16[22,32,128]{2,1,0:T(8,128)(2,1)}, u32[]{:S(2)}, u32[]{:S(2)}) collective-permute-start(bf16[22,32,128]{2,1,0:T(8,128)(2,1)S(1)} %get-tuple-element.41), channel_id=1, source_target_pairs={{2,0},{4,2},{6,4},{8,6},{10,8},{12,10},{14,12},{16,14},{18,16},{20... | collective-permute-start | bytes 540680 | tf_op jit(solution)/shard_map/ppermute | solution.py:24
  21.9 1.2 copy-start.1
  23.9 0.9 copy-start.5
  53.3 4.1 %collective-permute-start.6 = (bf16[3456,128]{1,0:T(8,128)(2,1)S(1)}, bf16[3456,128]{1,0:T(8,128)(2,1)S(1)}, u32[]{:S(2)}, u32[]{:S(2)}) collective-permute-start(bf16[3456,128]{1,0:T(8,128)(2,1)S(1)} %slice_bitcast_fusion), channel_id=1, source_target_pairs={{0,1},{1,0},{2,3},{3,2},{4,5},{5,4},{6,7},{7,6},{8,9},{9,8},{10,11... | collective-permute-start | bytes 2654216 | tf_op jit(solution)/shard_map/ppermute | solution.py:418
  58.6 21.1 %all-to-all-start = ((bf16[16,216,128]{2,1,0:T(8,128)(2,1)}), bf16[16,216,128]{2,1,0:T(8,128)(2,1)}, u32[]{:S(2)}, u32[]{:S(2)}) async-start(bf16[16,216,128]{2,1,0:T(8,128)(2,1)} %bitcast.10), calls=%async_computation | async-start | bytes 1769472 | tf_op jit(solution)/shard_map/all_to_all | solution.py:423
  65.1 15.9 %collective-permute-start.7 = (bf16[8,32,128]{2,1,0:T(8,128)(2,1)S(1)}, bf16[8,32,128]{2,1,0:T(8,128)(2,1)S(1)}, u32[]{:S(2)}, u32[]{:S(2)}) collective-permute-start(bf16[8,32,128]{2,1,0:T(8,128)(2,1)S(1)} %get-tuple-element.48), channel_id=1, source_target_pairs={{0,32},{32,64},{64,96},{96,128},{128,160},{160,192},{192,224},{224... | collective-permute-start | bytes 196616 | tf_op jit(solution)/shard_map/ppermute | solution.py:23
  65.1 15.9 %collective-permute-start.8 = (bf16[8,32,128]{2,1,0:T(8,128)(2,1)S(1)}, bf16[8,32,128]{2,1,0:T(8,128)(2,1)S(1)}, u32[]{:S(2)}, u32[]{:S(2)}) collective-permute-start(bf16[8,32,128]{2,1,0:T(8,128)(2,1)S(1)} %get-tuple-element.49), channel_id=1, source_target_pairs={{32,0},{64,32},{96,64},{128,96},{160,128},{192,160},{224,192},{0,2... | collective-permute-start | bytes 196616 | tf_op jit(solution)/shard_map/ppermute | solution.py:24
  81.0 3.1 %collective-permute-start.9 = (bf16[216,128]{1,0:T(8,128)(2,1)S(1)}, bf16[216,128]{1,0:T(8,128)(2,1)S(1)}, u32[]{:S(2)}, u32[]{:S(2)}) collective-permute-start(bf16[216,128]{1,0:T(8,128)(2,1)S(1)} %reduce_sum.12), channel_id=1, source_target_pairs={{0,32},{32,0},{64,96},{96,64},{128,160},{160,128},{192,224},{224,1... | collective-permute-start | bytes 165896 | tf_op jit(solution)/shard_map/ppermute | solution.py:431
  84.1 5.7 %collective-permute-start.10 = (bf16[216,128]{1,0:T(8,128)(2,1)S(1)}, bf16[216,128]{1,0:T(8,128)(2,1)S(1)}, u32[]{:S(2)}, u32[]{:S(2)}) collective-permute-start(bf16[216,128]{1,0:T(8,128)(2,1)S(1)} %add_convert_fusion.2), channel_id=1, source_target_pairs={{0,96},{32,64},{64,32},{96,0},{128,224},{160,192},{192,160},{224,1... | collective-permute-start | bytes 165896 | tf_op jit(solution)/shard_map/ppermute | solution.py:431
  89.9 6.7 %collective-permute-start.11 = (bf16[216,128]{1,0:T(8,128)(2,1)S(1)}, bf16[216,128]{1,0:T(8,128)(2,1)S(1)}, u32[]{:S(2)}, u32[]{:S(2)}) collective-permute-start(bf16[216,128]{1,0:T(8,128)(2,1)S(1)} %add_convert_fusion.1), channel_id=1, source_target_pairs={{0,224},{32,192},{64,160},{96,128},{128,96},{160,64},{192,32},{224... | collective-permute-start | bytes 165896 | tf_op jit(solution)/shard_map/ppermute | solution.py:431
  91.7 6.7 %collective-permute-start.12 = (bf16[10,32,128]{2,1,0:T(8,128)(2,1)S(1)}, bf16[10,32,128]{2,1,0:T(8,128)(2,1)S(1)}, u32[]{:S(2)}, u32[]{:S(2)}) collective-permute-start(bf16[10,32,128]{2,1,0:T(8,128)(2,1)S(1)} %get-tuple-element.54), channel_id=1, source_target_pairs={{0,2},{2,4},{4,6},{6,8},{8,10},{10,12},{12,14},{14,16},{16,18},{18... | collective-permute-start | bytes 245768 | tf_op jit(solution)/shard_map/ppermute | solution.py:23
  92.1 6.3 %collective-permute-start.13 = (bf16[10,32,128]{2,1,0:T(8,128)(2,1)S(1)}, bf16[10,32,128]{2,1,0:T(8,128)(2,1)S(1)}, u32[]{:S(2)}, u32[]{:S(2)}) collective-permute-start(bf16[10,32,128]{2,1,0:T(8,128)(2,1)S(1)} %get-tuple-element.55), channel_id=1, source_target_pairs={{2,0},{4,2},{6,4},{8,6},{10,8},{12,10},{14,12},{16,14},{18,16},{20... | collective-permute-start | bytes 245768 | tf_op jit(solution)/shard_map/ppermute | solution.py:24
  99.4 17.4 %all-to-all-start.1 = ((bf16[16,216,128]{2,1,0:T(8,128)(2,1)}), bf16[16,216,128]{2,1,0:T(8,128)(2,1)S(1)}, u32[]{:S(2)}, u32[]{:S(2)}) async-start(bf16[16,216,128]{2,1,0:T(8,128)(2,1)} %broadcast_in_dim.2), calls=%async_computation.1 | async-start | bytes 1769472 | tf_op jit(solution)/shard_map/all_to_all | solution.py:440
  116.8 9.3 %collective-permute-start.14 = (bf16[27,128,128]{2,1,0:T(8,128)(2,1)S(1)}, bf16[27,128,128]{2,1,0:T(8,128)(2,1)S(1)}, u32[]{:S(2)}, u32[]{:S(2)}) collective-permute-start(bf16[27,128,128]{2,1,0:T(8,128)(2,1)S(1)} %bitcast.23), channel_id=1, source_target_pairs={{0,1},{1,0},{2,3},{3,2},{4,5},{5,4},{6,7},{7,6},{8,9},{9,8},{10,11... | collective-permute-start | bytes 2654216 | tf_op jit(solution)/shard_map/ppermute | solution.py:418

commit v4 on v3

--- a/solution.py
+++ b/solution.py
@@ -59,7 +59,7 @@
                     value = jnp.concatenate(parts[j], axis=1).astype(BF16)
                     put(x - xs[0], ya - ys[0], yb - ys[0], j * C, value)
 
-            if xb - xa > 3:
+            if xb - xa > 8:
 
                 def body(x, unused):
                     line(x)
@@ -166,13 +166,12 @@
             at = (x + a) * BE * ROWS
             turned[a * C : (a + 1) * C, at : at + BE * ROWS] = block
 
-    for b in range(3):
-        right = patch[:, b : b + BE].reshape((BE + 2) * BE * ROWS, 3 * C)
-        term = (jnp.dot(turned[...], right, preferred_element_type=F32) * scale).astype(BF16)
-        for a in range(3):
-            for c in range(3):
-                at = (a * 9 + b * 3 + c) * C
-                out[which, at : at + C, :] = term[a * C : (a + 1) * C, c * C : (c + 1) * C].T
+    right = jnp.concatenate([patch[:, b : b + BE].reshape((BE + 2) * BE * ROWS, 3 * C) for b in range(3)], axis=1)
+    term = (jnp.dot(turned[...], right, preferred_element_type=F32) * scale).astype(BF16)
+    for a in range(3):
+        for j in range(9):
+            at = (a * 9 + j) * C
+            out[which, at : at + C, :] = term[a * C : (a + 1) * C, j * C : (j + 1) * C].T
 
 
 def clear_turned(turned):
@@ -300,7 +299,8 @@
             hid[2 + at, 2:10, 0:ROWS, :] = hide(pre)
         return unused
 
-    lax.fori_loop(0, 2, first_own, 0)
+    for i in range(2):
+        first_own(i, 0)
     results = pairs([lambda j, b, s=s: px[s, j, b : b + BE] for s in range(2)], wide)
     for s in range(2):
         for h in range(2):
@@ -335,7 +335,8 @@
             back[1 + at, 1:9, 0:ROWS, :] = grad.astype(F32)
         return unused
 
-    lax.fori_loop(0, 2, second_own, 0)
+    for i in range(2):
+        second_own(i, 0)
     for s, at, pre in y_pairs(1):
         near = (ym, yp)[s]
         total = field[3 + at, (2, 11)[s], 0:ROWS, :] + pre[0]
@@ -350,7 +351,9 @@
     ):
         total = field[ax, ay, 0:ROWS, :] + pre[j]
         back[cx, cy, 0:ROWS, :] = rounded(near[at].astype(F32) * slope_of(total))
-    weight_grad(p2, b2o, turned, gr, 1 - core[0], scale)
+    @pl.when(core[0] >= 0)
+    def second_weight_grad():
+        weight_grad(p2, b2o, turned, gr, 1 - core[0], scale)
 
     band(w2f, wide)
     build_patches(tab, back, into(p2), 1, OWN, (0, BE), (0, BE))
@@ -360,10 +363,13 @@
             b1o[at] = (pre * slope1[at] * live).astype(BF16)
         return unused
 
-    lax.fori_loop(0, 2, third, 0)
+    for i in range(2):
+        third(i, 0)
     elow[...] = b1o[0]
     ehigh[...] = b1o[7]
-    weight_grad(p1, b1o, turned, gr, core[0], scale)
+    @pl.when(core[0] >= 0)
+    def first_weight_grad():
+        weight_grad(p1, b1o, turned, gr, core[0], scale)
 
 
 def last_kernel(own, b1, b2, xm, xp, ym, yp, w1f, out, field, patch, wide, staged, tab, sem):
@@ -392,7 +398,8 @@
                 out[at] = ((b2[at].astype(F32) + results[g][h].reshape(BE, ROWS, C)) * live).astype(BF16)
         return unused
 
-    lax.fori_loop(0, 2, step, 0)
+    for i in range(2):
+        step(i, 0)
 
 
 def call(kernel, outs, scratch, cost, mib, scalars, far, *args):

time: 128 us -> 125 us (0.977)
  Pallas kernels: 36.2 us -> 32.1 us
    pallas_call x6, Pallas kernels: 36.2 us -> 32.1 us  [call(): pl.pallas_call(kernel, out_shape=outs, in_specs=[smem] * scalars + [anywh...]
where the time goes in v4:
time: 125 us
  starting transfers between devices  52.4 us (42%)
  Pallas kernels  32.1 us (26%)
  waiting for transfers between devices  30.3 us (24%)
  other arithmetic  4.51 us (4%)
  local copies, waits for them, and re-layouts  3.85 us (3%)
  between operations  1.51 us (1%)
    pallas_call x6, Pallas kernels, call(): pl.pallas_call(kernel, out_shape=outs, in_specs=[smem] * scalars + [anywh...  32.1 us
    ppermute x5, starting transfers between devices, shift_pair(): from_high = lax.ppermute(low, axis, [((i + 1) % n, i) for i in range(n)])  18.8 us
    all_to_all x1, waiting for transfers between devices, sum_scatter(): lax.all_to_all(part.reshape(n, part.shape[0] // n, C), axis, 0, 0, tiled=...  11.9 us
    ppermute x2, starting transfers between devices, swap_cores(): return lax.ppermute(part, 'dp', [(0, 1), (1, 0)])  9.34 us
    all_to_all x1, starting transfers between devices, sum_scatter(): lax.all_to_all(part.reshape(n, part.shape[0] // n, C), axis, 0, 0, tiled=...  6.44 us
    all_to_all x1, waiting for transfers between devices, gather_axis(): lax.all_to_all(copies, axis, 0, 0, tiled=True).reshape(n * part.shape[0], C)  6.38 us
    all_to_all x1, starting transfers between devices, gather_axis(): lax.all_to_all(copies, axis, 0, 0, tiled=True).reshape(n * part.shape[0], C)  6.16 us
    ppermute x3, starting transfers between devices, sum_pairs(): other = lax.ppermute(part, axis, [(i, i ^ 2 * reach - 1) for i in range(n)])  6.03 us
  transfers between devices with their start and end apart: 17, of which 9 were waited for; matrix products, arithmetic and copies ran while one was open for 1% of the time, Pallas kernels for 5%

profile of v4, /device:TPU:1, one launch (start us, length us, event | category | flops | bytes accessed | tf_op | source)
XLA Modules:
  0.0 124.7 jit_solution(5515329167198032075)
XLA Ops:
  0.6 0.0 copy-start
  1.4 0.0 copy-start.4
  1.4 0.7 copy-done.4
  2.0 1.9 %shard_map.93 = (bf16[33,32,128]{2,1,0:T(8,128)(2,1)S(1)}, bf16[33,32,128]{2,1,0:T(8,128)(2,1)S(1)}, bf16[33,32,128]{2,1,0:T(8,128)(2,1)S(1)}, bf16[33,32,128]{2,1,0:T(8,128)(2,1)S(1)}, bf16[1,32,128]{2,1,0:T(8,128)(2,1)S(1)}) custom-call(s32[4,26]{1,0:T(4,128)S(1)} %bitcast.22, s32[1]{0:T(128)} %bitcast.17.count, bf16[8,8,32,128]{3,2,1,0:T(8,128)(2,1)} %bitcast.25, ...), custom_call_target="tpu_custom_call" | custom-call | bytes 2097152 | tf_op jit(solution)/shard_map/pallas_call | solution.py:413
  3.9 2.5 %collective-permute-start = (bf16[33,32,128]{2,1,0:T(8,128)(2,1)S(1)}, bf16[33,32,128]{2,1,0:T(8,128)(2,1)S(1)}, u32[]{:S(2)}, u32[]{:S(2)}) collective-permute-start(bf16[33,32,128]{2,1,0:T(8,128)(2,1)S(1)} %get-tuple-element.34), channel_id=1, source_target_pairs={{0,32},{32,64},{64,96},{96,128},{128,160},{160,192},{192,224},{224... | collective-permute-start | bytes 811016 | tf_op jit(solution)/shard_map/ppermute | solution.py:23
  6.5 4.0 %collective-permute-start.1 = (bf16[33,32,128]{2,1,0:T(8,128)(2,1)S(1)}, bf16[33,32,128]{2,1,0:T(8,128)(2,1)S(1)}, u32[]{:S(2)}, u32[]{:S(2)}) collective-permute-start(bf16[33,32,128]{2,1,0:T(8,128)(2,1)S(1)} %get-tuple-element.35), channel_id=1, source_target_pairs={{32,0},{64,32},{96,64},{128,96},{160,128},{192,160},{224,192},{0,2... | collective-permute-start | bytes 811016 | tf_op jit(solution)/shard_map/ppermute | solution.py:24
  10.5 1.2 collective-permute-start.2
  11.7 3.7 %collective-permute-start.3 = (bf16[33,32,128]{2,1,0:T(8,128)(2,1)S(1)}, bf16[33,32,128]{2,1,0:T(8,128)(2,1)}, u32[]{:S(2)}, u32[]{:S(2)}) collective-permute-start(bf16[33,32,128]{2,1,0:T(8,128)(2,1)S(1)} %get-tuple-element.37), channel_id=1, source_target_pairs={{2,0},{4,2},{6,4},{8,6},{10,8},{12,10},{14,12},{16,14},{18,16},{20... | collective-permute-start | bytes 811016 | tf_op jit(solution)/shard_map/ppermute | solution.py:24
  15.4 1.2 collective-permute-done.xm.refs_2_
  16.6 0.0 copy-start.2
  16.6 0.0 collective-permute-done.1.xp.refs_3_
  16.6 0.0 copy-start.3
  16.7 1.3 %collective-permute-start.4 = (bf16[22,32,128]{2,1,0:T(8,128)(2,1)S(1)}, bf16[22,32,128]{2,1,0:T(8,128)(2,1)}, u32[]{:S(2)}, u32[]{:S(2)}) collective-permute-start(bf16[22,32,128]{2,1,0:T(8,128)(2,1)S(1)} %get-tuple-element.40), channel_id=1, source_target_pairs={{0,2},{2,4},{4,6},{6,8},{8,10},{10,12},{12,14},{14,16},{16,18},{18... | collective-permute-start | bytes 540680 | tf_op jit(solution)/shard_map/ppermute | solution.py:23
  18.0 4.0 %collective-permute-start.5 = (bf16[22,32,128]{2,1,0:T(8,128)(2,1)S(1)}, bf16[22,32,128]{2,1,0:T(8,128)(2,1)}, u32[]{:S(2)}, u32[]{:S(2)}) collective-permute-start(bf16[22,32,128]{2,1,0:T(8,128)(2,1)S(1)} %get-tuple-element.41), channel_id=1, source_target_pairs={{2,0},{4,2},{6,4},{8,6},{10,8},{12,10},{14,12},{16,14},{18,16},{20... | collective-permute-start | bytes 540680 | tf_op jit(solution)/shard_map/ppermute | solution.py:24
  21.9 0.0 copy-done
  21.9 0.0 copy-start.1
  21.9 1.2 copy-done.1
  23.1 0.8 shard_map.95
  23.9 0.0 copy-start.5
  24.0 0.9 copy-done.5
  24.9 0.0 collective-permute-done.2.refs_4_
  24.9 0.0 collective-permute-done.3.refs_5_
  24.9 0.4 collective-permute-done.4.refs_6_
  25.3 0.0 collective-permute-done.5.refs_7_
  25.3 0.0 copy-done.2
  25.3 0.0 copy-done.3
  25.3 24.5 %shard_map.96 = (bf16[8,8,32,128]{3,2,1,0:T(8,128)(2,1)}, bf16[8,8,32,128]{3,2,1,0:T(8,128)(2,1)S(1)}, bf16[8,8,32,128]{3,2,1,0:T(8,128)(2,1)S(1)}, bf16[8,32,12...) custom-call(s32[1]{0:T(128)} %bitcast.core, ...), custom_call_target="tpu_custom_call" | custom-call | flops 12683575296 | bytes 10485760 | tf_op jit(solution)/shard_map/pallas_call | solution.py:413
  49.8 0.1 slice_bitcast_fusion
  49.9 2.1 %collective-permute-start.6 = (bf16[3456,128]{1,0:T(8,128)(2,1)S(1)}, bf16[3456,128]{1,0:T(8,128)(2,1)S(1)}, u32[]{:S(2)}, u32[]{:S(2)}) collective-permute-start(bf16[3456,128]{1,0:T(8,128)(2,1)S(1)} %slice_bitcast_fusion), channel_id=1, source_target_pairs={{0,1},{1,0},{2,3},{3,2},{4,5},{5,4},{6,7},{7,6},{8,9},{9,8},{10,11... | collective-permute-start | bytes 2654216 | tf_op jit(solution)/shard_map/ppermute | solution.py:425
  52.0 2.1 %collective-permute-done.6 = bf16[3456,128]{1,0:T(8,128)(2,1)S(1)} collective-permute-done((bf16[3456,128]{1,0:T(8,128)(2,1)S(1)}, bf16[3456,128]{1,0:T(8,128)(2,1)S(1)}, u32[]{:S(2)}, u32[]{:S(2)}) %collective-permute-start.6) | collective-permute-done | bytes 884768 | tf_op jit(solution)/shard_map/ppermute | solution.py:425
  54.1 1.1 fusion
  55.2 6.4 %all-to-all-start = ((bf16[16,216,128]{2,1,0:T(8,128)(2,1)}), bf16[16,216,128]{2,1,0:T(8,128)(2,1)}, u32[]{:S(2)}, u32[]{:S(2)}) async-start(bf16[16,216,128]{2,1,0:T(8,128)(2,1)} %bitcast.10), calls=%async_computation | async-start | bytes 1769472 | tf_op jit(solution)/shard_map/all_to_all | solution.py:430
  61.7 0.1 collective-permute-start.7
  61.8 2.7 %collective-permute-start.8 = (bf16[8,32,128]{2,1,0:T(8,128)(2,1)S(1)}, bf16[8,32,128]{2,1,0:T(8,128)(2,1)S(1)}, u32[]{:S(2)}, u32[]{:S(2)}) collective-permute-start(bf16[8,32,128]{2,1,0:T(8,128)(2,1)S(1)} %get-tuple-element.49), channel_id=1, source_target_pairs={{32,0},{64,32},{96,64},{128,96},{160,128},{192,160},{224,192},{0,2... | collective-permute-start | bytes 196616 | tf_op jit(solution)/shard_map/ppermute | solution.py:24
  64.4 11.9 %all-to-all-done = bf16[16,216,128]{2,1,0:T(8,128)(2,1)} async-done(((bf16[16,216,128]{2,1,0:T(8,128)(2,1)}), bf16[16,216,128]{2,1,0:T(8,128)(2,1)}, u32[]{:S(2)}, u32[]{:S(2)}) %all-to-all-start) | async-done | bytes 884768 | tf_op jit(solution)/shard_map/all_to_all | solution.py:430
  76.3 1.3 %reduce_sum.12 = bf16[216,128]{1,0:T(8,128)(2,1)S(1)} reduce(bf16[16,216,128]{2,1,0:T(8,128)(2,1)} %all-to-all-done, bf16[]{:T(256)} %constant.2.clone.1), dimensions={0}, to_apply=%region_0.0 | reduce | flops 414720 | bytes 940034 | tf_op jit(solution)/shard_map/reduce_sum | solution.py:431
  77.6 0.0 collective-permute-done.7.xm
  77.6 0.0 collective-permute-done.8.xp
  77.6 0.1 collective-permute-start.9
  77.7 3.0 %collective-permute-done.9 = bf16[216,128]{1,0:T(8,128)(2,1)S(1)} collective-permute-done((bf16[216,128]{1,0:T(8,128)(2,1)S(1)}, bf16[216,128]{1,0:T(8,128)(2,1)S(1)}, u32[]{:S(2)}, u32[]{:S(2)}) %collective-permute-start.9) | collective-permute-done | bytes 55328 | tf_op jit(solution)/shard_map/ppermute | solution.py:438
  80.7 4.1 %collective-permute-start.10 = (bf16[216,128]{1,0:T(8,128)(2,1)S(1)}, bf16[216,128]{1,0:T(8,128)(2,1)S(1)}, u32[]{:S(2)}, u32[]{:S(2)}) collective-permute-start(bf16[216,128]{1,0:T(8,128)(2,1)S(1)} %add_convert_fusion.2), channel_id=1, source_target_pairs={{0,96},{32,64},{64,32},{96,0},{128,224},{160,192},{192,160},{224,1... | collective-permute-start | bytes 165896 | tf_op jit(solution)/shard_map/ppermute | solution.py:438
  84.8 1.5 %collective-permute-done.10 = bf16[216,128]{1,0:T(8,128)(2,1)S(1)} collective-permute-done((bf16[216,128]{1,0:T(8,128)(2,1)S(1)}, bf16[216,128]{1,0:T(8,128)(2,1)S(1)}, u32[]{:S(2)}, u32[]{:S(2)}) %collective-permute-start.10) | collective-permute-done | bytes 55328 | tf_op jit(solution)/shard_map/ppermute | solution.py:438
  86.4 1.8 %collective-permute-start.11 = (bf16[216,128]{1,0:T(8,128)(2,1)S(1)}, bf16[216,128]{1,0:T(8,128)(2,1)S(1)}, u32[]{:S(2)}, u32[]{:S(2)}) collective-permute-start(bf16[216,128]{1,0:T(8,128)(2,1)S(1)} %add_convert_fusion.1), channel_id=1, source_target_pairs={{0,224},{32,192},{64,160},{96,128},{128,96},{160,64},{192,32},{224... | collective-permute-start | bytes 165896 | tf_op jit(solution)/shard_map/ppermute | solution.py:438
  88.3 0.4 collective-permute-start.12
  88.7 4.4 %collective-permute-start.13 = (bf16[10,32,128]{2,1,0:T(8,128)(2,1)S(1)}, bf16[10,32,128]{2,1,0:T(8,128)(2,1)S(1)}, u32[]{:S(2)}, u32[]{:S(2)}) collective-permute-start(bf16[10,32,128]{2,1,0:T(8,128)(2,1)S(1)} %get-tuple-element.55), channel_id=1, source_target_pairs={{2,0},{4,2},{6,4},{8,6},{10,8},{12,10},{14,12},{16,14},{18,16},{20... | collective-permute-start | bytes 245768 | tf_op jit(solution)/shard_map/ppermute | solution.py:24
  93.1 0.0 collective-permute-done.11
  93.2 1.8 %collective-permute-done.12.ym = bf16[10,32,128]{2,1,0:T(8,128)(2,1)S(1)} collective-permute-done((bf16[10,32,128]{2,1,0:T(8,128)(2,1)S(1)}, bf16[10,32,128]{2,1,0:T(8,128)(2,1)S(1)}, u32[]{:S(2)}, u32[]{:S(2)}) %collective-permute-start.12) | collective-permute-done | bytes 81952 | tf_op jit(solution)/shard_map/ppermute | solution.py:23
  95.0 0.0 collective-permute-done.13.yp
  95.0 1.0 broadcast_in_dim.2
  96.0 6.2 %all-to-all-start.1 = ((bf16[16,216,128]{2,1,0:T(8,128)(2,1)}), bf16[16,216,128]{2,1,0:T(8,128)(2,1)S(1)}, u32[]{:S(2)}, u32[]{:S(2)}) async-start(bf16[16,216,128]{2,1,0:T(8,128)(2,1)} %broadcast_in_dim.2), calls=%async_computation.1 | async-start | bytes 1769472 | tf_op jit(solution)/shard_map/all_to_all | solution.py:447
  102.2 4.8 %shard_map.98 = bf16[8,8,32,128]{3,2,1,0:T(8,128)(2,1)} custom-call(bf16[1,32,128]{2,1,0:T(8,128)(2,1)S(1)} %get-tuple-element.45.refs_11_.own, bf16[8,8,32,128]{3,2,1,0:T(8,128)(2,1)S(1)} %get-tuple-element.53.b1, bf16[8,8,32,128]{3,2,1,0:T(8,128)(2,1)S(1)} %get-tuple-element.58.b2, bf16[8,32,128]{2,1,0:T(8,128)(2,1)S(1)} %collective-permute-done.7.xm, ...), custom_call_target="tpu_custom_call" | custom-call | flops 1811939328 | bytes 4194304 | tf_op jit(solution)/shard_map/pallas_call | solution.py:413
  107.0 6.4 %all-to-all-done.1 = bf16[16,216,128]{2,1,0:T(8,128)(2,1)S(1)} async-done(((bf16[16,216,128]{2,1,0:T(8,128)(2,1)}), bf16[16,216,128]{2,1,0:T(8,128)(2,1)S(1)}, u32[]{:S(2)}, u32[]{:S(2)}) %all-to-all-start.1) | async-done | bytes 884768 | tf_op jit(solution)/shard_map/all_to_all | solution.py:447
  113.4 7.2 %collective-permute-start.14 = (bf16[27,128,128]{2,1,0:T(8,128)(2,1)S(1)}, bf16[27,128,128]{2,1,0:T(8,128)(2,1)S(1)}, u32[]{:S(2)}, u32[]{:S(2)}) collective-permute-start(bf16[27,128,128]{2,1,0:T(8,128)(2,1)S(1)} %bitcast.23), channel_id=1, source_target_pairs={{0,1},{1,0},{2,3},{3,2},{4,5},{5,4},{6,7},{7,6},{8,9},{9,8},{10,11... | collective-permute-start | bytes 2654216 | tf_op jit(solution)/shard_map/ppermute | solution.py:425
  120.6 2.1 %collective-permute-done.14 = bf16[27,128,128]{2,1,0:T(8,128)(2,1)S(1)} collective-permute-done((bf16[27,128,128]{2,1,0:T(8,128)(2,1)S(1)}, bf16[27,128,128]{2,1,0:T(8,128)(2,1)S(1)}, u32[]{:S(2)}, u32[]{:S(2)}) %collective-permute-start.14) | collective-permute-done | bytes 884768 | tf_op jit(solution)/shard_map/ppermute | solution.py:425
  122.6 2.0 %select_convert_fusion = (f32[27,128,128]{2,1,0:T(8,128)}, f32[27,128,128]{2,1,0:T(8,128)}) fusion(bf16[27,128,128]{2,1,0:T(8,128)(2,1)S(1)} %collective-permute-done.14, bf16[27,128,128]{2,1,0:T(8,128)(2,1)S(1)} %bitcast.24, pred[]{:T(512)S(6)} %eq.4), kind=kLoop, calls=%fused_computation.2 | loop fusion | flops 1769472 | bytes 5308417 | tf_op jit(solution)/shard_map/convert_element_type | solution.py:529
  (5 shorter events, 0.1 us)
Async XLA Ops:
  0.6 21.3 %copy-start = (bf16[27,128,128]{2,1,0:T(8,128)(2,1)S(1)}, bf16[27,128,128]{2,1,0:T(8,128)(2,1)}, u32[]{:S(2)}) copy-start(bf16[27,128,128]{2,1,0:T(8,128)(2,1)} %param.8) | copy-start | bytes 2654212
  1.4 0.7 copy-start.4
  3.9 12.7 %collective-permute-start = (bf16[33,32,128]{2,1,0:T(8,128)(2,1)S(1)}, bf16[33,32,128]{2,1,0:T(8,128)(2,1)S(1)}, u32[]{:S(2)}, u32[]{:S(2)}) collective-permute-start(bf16[33,32,128]{2,1,0:T(8,128)(2,1)S(1)} %get-tuple-element.34), channel_id=1, source_target_pairs={{0,32},{32,64},{64,96},{96,128},{128,160},{160,192},{192,224},{224... | collective-permute-start | bytes 811016 | tf_op jit(solution)/shard_map/ppermute | solution.py:23
  6.5 10.2 %collective-permute-start.1 = (bf16[33,32,128]{2,1,0:T(8,128)(2,1)S(1)}, bf16[33,32,128]{2,1,0:T(8,128)(2,1)S(1)}, u32[]{:S(2)}, u32[]{:S(2)}) collective-permute-start(bf16[33,32,128]{2,1,0:T(8,128)(2,1)S(1)} %get-tuple-element.35), channel_id=1, source_target_pairs={{32,0},{64,32},{96,64},{128,96},{160,128},{192,160},{224,192},{0,2... | collective-permute-start | bytes 811016 | tf_op jit(solution)/shard_map/ppermute | solution.py:24
  10.5 14.4 %collective-permute-start.2 = (bf16[33,32,128]{2,1,0:T(8,128)(2,1)S(1)}, bf16[33,32,128]{2,1,0:T(8,128)(2,1)}, u32[]{:S(2)}, u32[]{:S(2)}) collective-permute-start(bf16[33,32,128]{2,1,0:T(8,128)(2,1)S(1)} %get-tuple-element.36), channel_id=1, source_target_pairs={{0,2},{2,4},{4,6},{6,8},{8,10},{10,12},{12,14},{14,16},{16,18},{18... | collective-permute-start | bytes 811016 | tf_op jit(solution)/shard_map/ppermute | solution.py:23
  11.7 13.1 %collective-permute-start.3 = (bf16[33,32,128]{2,1,0:T(8,128)(2,1)S(1)}, bf16[33,32,128]{2,1,0:T(8,128)(2,1)}, u32[]{:S(2)}, u32[]{:S(2)}) collective-permute-start(bf16[33,32,128]{2,1,0:T(8,128)(2,1)S(1)} %get-tuple-element.37), channel_id=1, source_target_pairs={{2,0},{4,2},{6,4},{8,6},{10,8},{12,10},{14,12},{16,14},{18,16},{20... | collective-permute-start | bytes 811016 | tf_op jit(solution)/shard_map/ppermute | solution.py:24
  16.6 8.7 %copy-start.2 = (bf16[33,32,128]{2,1,0:T(8,128)(2,1)}, bf16[33,32,128]{2,1,0:T(8,128)(2,1)S(1)}, u32[]{:S(2)}) copy-start(bf16[33,32,128]{2,1,0:T(8,128)(2,1)S(1)} %collective-permute-done.xm.refs_2_) | copy-start | bytes 811012
  16.6 8.7 %copy-start.3 = (bf16[33,32,128]{2,1,0:T(8,128)(2,1)}, bf16[33,32,128]{2,1,0:T(8,128)(2,1)S(1)}, u32[]{:S(2)}) copy-start(bf16[33,32,128]{2,1,0:T(8,128)(2,1)S(1)} %collective-permute-done.1.xp.refs_3_) | copy-start | bytes 811012
  16.7 8.6 %collective-permute-start.4 = (bf16[22,32,128]{2,1,0:T(8,128)(2,1)S(1)}, bf16[22,32,128]{2,1,0:T(8,128)(2,1)}, u32[]{:S(2)}, u32[]{:S(2)}) collective-permute-start(bf16[22,32,128]{2,1,0:T(8,128)(2,1)S(1)} %get-tuple-element.40), channel_id=1, source_target_pairs={{0,2},{2,4},{4,6},{6,8},{8,10},{10,12},{12,14},{14,16},{16,18},{18... | collective-permute-start | bytes 540680 | tf_op jit(solution)/shard_map/ppermute | solution.py:23
  18.0 7.3 %collective-permute-start.5 = (bf16[22,32,128]{2,1,0:T(8,128)(2,1)S(1)}, bf16[22,32,128]{2,1,0:T(8,128)(2,1)}, u32[]{:S(2)}, u32[]{:S(2)}) collective-permute-start(bf16[22,32,128]{2,1,0:T(8,128)(2,1)S(1)} %get-tuple-element.41), channel_id=1, source_target_pairs={{2,0},{4,2},{6,4},{8,6},{10,8},{12,10},{14,12},{16,14},{18,16},{20... | collective-permute-start | bytes 540680 | tf_op jit(solution)/shard_map/ppermute | solution.py:24
  21.9 1.2 copy-start.1
  23.9 0.9 copy-start.5
  49.9 4.2 %collective-permute-start.6 = (bf16[3456,128]{1,0:T(8,128)(2,1)S(1)}, bf16[3456,128]{1,0:T(8,128)(2,1)S(1)}, u32[]{:S(2)}, u32[]{:S(2)}) collective-permute-start(bf16[3456,128]{1,0:T(8,128)(2,1)S(1)} %slice_bitcast_fusion), channel_id=1, source_target_pairs={{0,1},{1,0},{2,3},{3,2},{4,5},{5,4},{6,7},{7,6},{8,9},{9,8},{10,11... | collective-permute-start | bytes 2654216 | tf_op jit(solution)/shard_map/ppermute | solution.py:425
  55.2 21.1 %all-to-all-start = ((bf16[16,216,128]{2,1,0:T(8,128)(2,1)}), bf16[16,216,128]{2,1,0:T(8,128)(2,1)}, u32[]{:S(2)}, u32[]{:S(2)}) async-start(bf16[16,216,128]{2,1,0:T(8,128)(2,1)} %bitcast.10), calls=%async_computation | async-start | bytes 1769472 | tf_op jit(solution)/shard_map/all_to_all | solution.py:430
  61.7 15.9 %collective-permute-start.7 = (bf16[8,32,128]{2,1,0:T(8,128)(2,1)S(1)}, bf16[8,32,128]{2,1,0:T(8,128)(2,1)S(1)}, u32[]{:S(2)}, u32[]{:S(2)}) collective-permute-start(bf16[8,32,128]{2,1,0:T(8,128)(2,1)S(1)} %get-tuple-element.48), channel_id=1, source_target_pairs={{0,32},{32,64},{64,96},{96,128},{128,160},{160,192},{192,224},{224... | collective-permute-start | bytes 196616 | tf_op jit(solution)/shard_map/ppermute | solution.py:23
  61.8 15.9 %collective-permute-start.8 = (bf16[8,32,128]{2,1,0:T(8,128)(2,1)S(1)}, bf16[8,32,128]{2,1,0:T(8,128)(2,1)S(1)}, u32[]{:S(2)}, u32[]{:S(2)}) collective-permute-start(bf16[8,32,128]{2,1,0:T(8,128)(2,1)S(1)} %get-tuple-element.49), channel_id=1, source_target_pairs={{32,0},{64,32},{96,64},{128,96},{160,128},{192,160},{224,192},{0,2... | collective-permute-start | bytes 196616 | tf_op jit(solution)/shard_map/ppermute | solution.py:24
  77.6 3.1 %collective-permute-start.9 = (bf16[216,128]{1,0:T(8,128)(2,1)S(1)}, bf16[216,128]{1,0:T(8,128)(2,1)S(1)}, u32[]{:S(2)}, u32[]{:S(2)}) collective-permute-start(bf16[216,128]{1,0:T(8,128)(2,1)S(1)} %reduce_sum.12), channel_id=1, source_target_pairs={{0,32},{32,0},{64,96},{96,64},{128,160},{160,128},{192,224},{224,1... | collective-permute-start | bytes 165896 | tf_op jit(solution)/shard_map/ppermute | solution.py:438
  80.7 5.6 %collective-permute-start.10 = (bf16[216,128]{1,0:T(8,128)(2,1)S(1)}, bf16[216,128]{1,0:T(8,128)(2,1)S(1)}, u32[]{:S(2)}, u32[]{:S(2)}) collective-permute-start(bf16[216,128]{1,0:T(8,128)(2,1)S(1)} %add_convert_fusion.2), channel_id=1, source_target_pairs={{0,96},{32,64},{64,32},{96,0},{128,224},{160,192},{192,160},{224,1... | collective-permute-start | bytes 165896 | tf_op jit(solution)/shard_map/ppermute | solution.py:438
  86.4 6.7 %collective-permute-start.11 = (bf16[216,128]{1,0:T(8,128)(2,1)S(1)}, bf16[216,128]{1,0:T(8,128)(2,1)S(1)}, u32[]{:S(2)}, u32[]{:S(2)}) collective-permute-start(bf16[216,128]{1,0:T(8,128)(2,1)S(1)} %add_convert_fusion.1), channel_id=1, source_target_pairs={{0,224},{32,192},{64,160},{96,128},{128,96},{160,64},{192,32},{224... | collective-permute-start | bytes 165896 | tf_op jit(solution)/shard_map/ppermute | solution.py:438
  88.3 6.7 %collective-permute-start.12 = (bf16[10,32,128]{2,1,0:T(8,128)(2,1)S(1)}, bf16[10,32,128]{2,1,0:T(8,128)(2,1)S(1)}, u32[]{:S(2)}, u32[]{:S(2)}) collective-permute-start(bf16[10,32,128]{2,1,0:T(8,128)(2,1)S(1)} %get-tuple-element.54), channel_id=1, source_target_pairs={{0,2},{2,4},{4,6},{6,8},{8,10},{10,12},{12,14},{14,16},{16,18},{18... | collective-permute-start | bytes 245768 | tf_op jit(solution)/shard_map/ppermute | solution.py:23
  88.7 6.3 %collective-permute-start.13 = (bf16[10,32,128]{2,1,0:T(8,128)(2,1)S(1)}, bf16[10,32,128]{2,1,0:T(8,128)(2,1)S(1)}, u32[]{:S(2)}, u32[]{:S(2)}) collective-permute-start(bf16[10,32,128]{2,1,0:T(8,128)(2,1)S(1)} %get-tuple-element.55), channel_id=1, source_target_pairs={{2,0},{4,2},{6,4},{8,6},{10,8},{12,10},{14,12},{16,14},{18,16},{20... | collective-permute-start | bytes 245768 | tf_op jit(solution)/shard_map/ppermute | solution.py:24
  96.0 17.4 %all-to-all-start.1 = ((bf16[16,216,128]{2,1,0:T(8,128)(2,1)}), bf16[16,216,128]{2,1,0:T(8,128)(2,1)S(1)}, u32[]{:S(2)}, u32[]{:S(2)}) async-start(bf16[16,216,128]{2,1,0:T(8,128)(2,1)} %broadcast_in_dim.2), calls=%async_computation.1 | async-start | bytes 1769472 | tf_op jit(solution)/shard_map/all_to_all | solution.py:447
  113.4 9.3 %collective-permute-start.14 = (bf16[27,128,128]{2,1,0:T(8,128)(2,1)S(1)}, bf16[27,128,128]{2,1,0:T(8,128)(2,1)S(1)}, u32[]{:S(2)}, u32[]{:S(2)}) collective-permute-start(bf16[27,128,128]{2,1,0:T(8,128)(2,1)S(1)} %bitcast.23), channel_id=1, source_target_pairs={{0,1},{1,0},{2,3},{3,2},{4,5},{5,4},{6,7},{7,6},{8,9},{9,8},{10,11... | collective-permute-start | bytes 2654216 | tf_op jit(solution)/shard_map/ppermute | solution.py:425

commit v5 on v4

--- a/solution.py
+++ b/solution.py
@@ -95,17 +95,9 @@
     wide[9 * C : 36 * C, C : 2 * C] = weight[...]
 
 
-def flip_kernel(first, second, first_out, second_out):
-    for weight, out in ((second, second_out), (first, first_out)):
-
-        def body(n, unused):
-            for j in range(9):
-                k = n * 9 + j
-                block = weight[pl.ds(pl.multiple_of((26 - k) * C, C), C), :].T
-                out[pl.ds(pl.multiple_of(k * C, C), C), :] = block
-            return unused
-
-        lax.fori_loop(0, 3, body, 0)
+def flip(weight, out):
+    for k in range(27):
+        out[k * C : (k + 1) * C, :] = weight[(26 - k) * C : (27 - k) * C, :].T
 
 
 def clear_band(wide):
@@ -235,12 +227,12 @@
 
 
 def main_kernel(scale, core, *refs):
-    far, own, refs = refs[:11], refs[11], refs[12:]
+    far, own, refs = refs[:10], refs[10], refs[11:]
     out, b2o, b1o, elow, ehigh, gr = refs[:6]
-    near, (sems, field, hid, back, p1, p2, px, py, pc, slope1, turned, wide, staged, tab, sem) = refs[6:17], refs[17:]
-    x, cot, xm, xp, ym, yp, qm, qp, w1, w2, w2f = near
-    copies = [pltpu.make_async_copy(far[i], near[i], sems.at[i]) for i in range(11)]
-    order = [8, 0, 2, 3, 4, 5, 6, 7, 1, 9, 10]
+    near, (w2f, sems, field, hid, back, p1, p2, px, py, pc, slope1, turned, wide, staged, tab, sem) = refs[6:16], refs[16:]
+    x, cot, xm, xp, ym, yp, qm, qp, w1, w2 = near
+    copies = [pltpu.make_async_copy(far[i], near[i], sems.at[i]) for i in range(10)]
+    order = [8, 0, 2, 3, 4, 5, 6, 7, 9, 1]
     for i in order:
         copies[i].start()
     for ref in (field, hid, back):
@@ -249,7 +241,7 @@
     clear_band(wide)
     copies[8].wait()
     band(w1, wide)
-    for i in order[1:8]:
+    for i in order[1:]:
         copies[i].wait()
     load_tables(
         {0: (qm, 20), 1: (xm, 32), 2: (qp, 20), 3: (ym, 32), 4: (own, 0), 5: (yp, 32), 6: (qm, 21), 7: (xp, 32), 8: (qp, 21)},
@@ -278,6 +270,8 @@
         build_patches(tab, field, into(py, j), 3, COLUMNS.index((0, cx)), ends[0], ends[cx])
     for j, c in enumerate(corners):
         build_patches(tab, field, into(pc, j), 3, c, ends[COLUMNS[c][0]], ends[COLUMNS[c][1]])
+
+    flip(w2, w2f)
 
     def hide(pre):
         return rounded(pre * jax.nn.sigmoid(pre))
@@ -314,8 +308,6 @@
             hid[ax + h, ay : ay + 2, 0:ROWS, :] = value[j]
 
     ends = spans(1)
-    for i in order[8:]:
-        copies[i].wait()
     band(w2, wide)
     build_patches(tab, hid, into(p2), 2, OWN, ends[0], ends[0])
     for j, cx in enumerate((-1, 1)):
@@ -372,11 +364,12 @@
         weight_grad(p1, b1o, turned, gr, core[0], scale)
 
 
-def last_kernel(own, b1, b2, xm, xp, ym, yp, w1f, out, field, patch, wide, staged, tab, sem):
+def last_kernel(own, b1, b2, xm, xp, ym, yp, w1, out, field, patch, w1f, wide, staged, tab, sem):
     load_tables({OWN: (own, 0)}, staged, tab, sem)
     live = live_rows(tab)
     zero_slot(field)
     clear_band(wide)
+    flip(w1, w1f)
     band(w1f, wide)
 
     def fill(i, unused):
@@ -468,9 +461,7 @@
     xm, xp = shift_pair(xlow, xhigh, "sx")
     ym, yp = shift_pair(ylow, yhigh, "sy")
     qlow, qhigh = call(corner_payload_kernel, [shape_of(22, ROWS, C)] * 2, [], (0, 2**19), 8, 0, 0, xm, xp)
-    held1, held2, qlow, qhigh = lax.optimization_barrier((w1, w2, qlow, qhigh))
     qm, qp = shift_pair(qlow, qhigh, "sy")
-    w1f, w2f = call(flip_kernel, [shape_of(27 * C, C)] * 2, [], (2**24, 2**22), 8, 0, 0, held1, held2)
 
     block, edge = shape_of(BE, BE, ROWS, C), shape_of(BE, ROWS, C)
     lanes = 3 * C
@@ -484,7 +475,7 @@
             *[pltpu.VMEM((33, ROWS, C), BF16)] * 4,
             *[pltpu.VMEM((22, ROWS, C), BF16)] * 2,
             *[pltpu.VMEM((27 * C, C), BF16)] * 3,
-            pltpu.SemaphoreType.DMA((11,)),
+            pltpu.SemaphoreType.DMA((10,)),
             pltpu.VMEM((14, 14, ROWS + BE, C), F32),
             pltpu.VMEM((12, 12, ROWS + BE, C), F32),
             pltpu.VMEM((10, 10, ROWS + BE, C), F32),
@@ -498,8 +489,8 @@
             pltpu.VMEM((36 * C, 2 * C), BF16),
             *tables,
         ],
-        (7 * unit, 10 * 2**20), 40, 1, 11,
-        core.reshape(1), x, cot, xm, xp, ym, yp, qm, qp, w1, w2, w2f, own,
+        (7 * unit, 10 * 2**20), 40, 1, 10,
+        core.reshape(1), x, cot, xm, xp, ym, yp, qm, qp, w1, w2, own,
     )
 
     received = swap_cores(grads[1])
@@ -516,11 +507,12 @@
         [
             pltpu.VMEM((10, 10, ROWS + BE, C), F32),
             pltpu.VMEM((10, 10, ROWS, lanes), BF16),
+            pltpu.VMEM((27 * C, C), BF16),
             pltpu.VMEM((36 * C, 2 * C), BF16),
             *tables,
         ],
         (unit, 4 * 2**20), 12, 0, 0,
-        own, b1, b2, bxm, bxp, bym, byp, w1f,
+        own, b1, b2, bxm, bxp, bym, byp, w1,
     )
     part, grad_input = lax.optimization_barrier((gather_axis(part, "sy"), grad_input))
     part = part.reshape(27, C, C)

time: 125 us -> 125 us (level)
  waiting for transfers between devices: 30.3 us -> 32.8 us
  local copies, waits for them, and re-layouts: 3.85 us -> 2.47 us
    ppermute x5, waiting for transfers between devices: 3.4 us -> 6.2 us  [shift_pair(): from_low = lax.ppermute(high, axis, [(i, (i + 1) % n) for i in range(n)])]
    unnamed x12 -> x16, local copies, waits for them, and re-layouts: 2.76 us -> 1.39 us
    pallas_call x6 -> x5, Pallas kernels: 32.1 us -> 32.1 us  [call(): pl.pallas_call(kernel, out_shape=outs, in_specs=[smem] * scalars + [anywh...]
  transfers between devices with their start and end apart: 17 -> 17, of which waited for: 9 -> 9; matrix products, arithmetic and copies ran while one was open for 1% -> 0% of each run, Pallas kernels for 5% -> 4%
where the time goes in v5:
time: 125 us; the launch traced here: 124 us
  starting transfers between devices  52.2 us (42%)
  waiting for transfers between devices  32.8 us (26%)
  Pallas kernels  32.1 us (26%)
  other arithmetic  3.34 us (3%)
  local copies, waits for them, and re-layouts  2.47 us (2%)
  between operations  1.46 us (1%)
    pallas_call x5, Pallas kernels, call(): pl.pallas_call(kernel, out_shape=outs, in_specs=[smem] * scalars + [anywh...  32.1 us
    ppermute x5, starting transfers between devices, shift_pair(): from_high = lax.ppermute(low, axis, [((i + 1) % n, i) for i in range(n)])  18.8 us
    all_to_all x1, waiting for transfers between devices, sum_scatter(): lax.all_to_all(part.reshape(n, part.shape[0] // n, C), axis, 0, 0, tiled=...  11.8 us
    ppermute x2, starting transfers between devices, swap_cores(): return lax.ppermute(part, 'dp', [(0, 1), (1, 0)])  9.29 us
    all_to_all x1, starting transfers between devices, sum_scatter(): lax.all_to_all(part.reshape(n, part.shape[0] // n, C), axis, 0, 0, tiled=...  6.38 us
    ppermute x5, waiting for transfers between devices, shift_pair(): from_low = lax.ppermute(high, axis, [(i, (i + 1) % n) for i in range(n)])  6.2 us
    all_to_all x1, starting transfers between devices, gather_axis(): lax.all_to_all(copies, axis, 0, 0, tiled=True).reshape(n * part.shape[0], C)  6.16 us
    all_to_all x1, waiting for transfers between devices, gather_axis(): lax.all_to_all(copies, axis, 0, 0, tiled=True).reshape(n * part.shape[0], C)  6.14 us
  transfers between devices with their start and end apart: 17, of which 9 were waited for; matrix products, arithmetic and copies ran while one was open for 0% of the time, Pallas kernels for 4%

profile of v5, /device:TPU:1, one launch (start us, length us, event | category | flops | bytes accessed | tf_op | source)
XLA Modules:
  0.0 124.5 jit_solution(12537938620960301875)
XLA Ops:
  1.3 0.0 copy-start.2
  1.3 0.7 copy-done.2
  2.0 1.9 %shard_map.93 = (bf16[33,32,128]{2,1,0:T(8,128)(2,1)S(1)}, bf16[33,32,128]{2,1,0:T(8,128)(2,1)S(1)}, bf16[33,32,128]{2,1,0:T(8,128)(2,1)S(1)}, bf16[33,32,128]{2,1,0:T(8,128)(2,1)S(1)}, bf16[1,32,128]{2,1,0:T(8,128)(2,1)S(1)}) custom-call(s32[4,26]{1,0:T(4,128)S(1)} %bitcast.18, s32[1]{0:T(128)} %bitcast.17.count, bf16[8,8,32,128]{3,2,1,0:T(8,128)(2,1)} %bitcast.23, ...), custom_call_target="tpu_custom_call" | custom-call | bytes 2097152 | tf_op jit(solution)/shard_map/pallas_call | solution.py:406
  3.8 2.5 %collective-permute-start = (bf16[33,32,128]{2,1,0:T(8,128)(2,1)S(1)}, bf16[33,32,128]{2,1,0:T(8,128)(2,1)S(1)}, u32[]{:S(2)}, u32[]{:S(2)}) collective-permute-start(bf16[33,32,128]{2,1,0:T(8,128)(2,1)S(1)} %get-tuple-element.28), channel_id=1, source_target_pairs={{0,32},{32,64},{64,96},{96,128},{128,160},{160,192},{192,224},{224... | collective-permute-start | bytes 811016 | tf_op jit(solution)/shard_map/ppermute | solution.py:23
  6.4 4.0 %collective-permute-start.1 = (bf16[33,32,128]{2,1,0:T(8,128)(2,1)S(1)}, bf16[33,32,128]{2,1,0:T(8,128)(2,1)S(1)}, u32[]{:S(2)}, u32[]{:S(2)}) collective-permute-start(bf16[33,32,128]{2,1,0:T(8,128)(2,1)S(1)} %get-tuple-element.29), channel_id=1, source_target_pairs={{32,0},{64,32},{96,64},{128,96},{160,128},{192,160},{224,192},{0,2... | collective-permute-start | bytes 811016 | tf_op jit(solution)/shard_map/ppermute | solution.py:24
  10.4 1.2 collective-permute-start.2
  11.6 3.7 %collective-permute-start.3 = (bf16[33,32,128]{2,1,0:T(8,128)(2,1)S(1)}, bf16[33,32,128]{2,1,0:T(8,128)(2,1)S(1)}, u32[]{:S(2)}, u32[]{:S(2)}) collective-permute-start(bf16[33,32,128]{2,1,0:T(8,128)(2,1)S(1)} %get-tuple-element.31), channel_id=1, source_target_pairs={{2,0},{4,2},{6,4},{8,6},{10,8},{12,10},{14,12},{16,14},{18,16},{20... | collective-permute-start | bytes 811016 | tf_op jit(solution)/shard_map/ppermute | solution.py:24
  15.3 1.2 collective-permute-done.xm.refs_2_
  16.5 0.0 copy-start
  16.5 0.0 collective-permute-done.1.xp.refs_3_
  16.5 0.0 copy-start.1
  16.6 1.3 %collective-permute-start.4 = (bf16[22,32,128]{2,1,0:T(8,128)(2,1)S(1)}, bf16[22,32,128]{2,1,0:T(8,128)(2,1)S(1)}, u32[]{:S(2)}, u32[]{:S(2)}) collective-permute-start(bf16[22,32,128]{2,1,0:T(8,128)(2,1)S(1)} %get-tuple-element.32), channel_id=1, source_target_pairs={{0,2},{2,4},{4,6},{6,8},{8,10},{10,12},{12,14},{14,16},{16,18},{18... | collective-permute-start | bytes 540680 | tf_op jit(solution)/shard_map/ppermute | solution.py:23
  17.9 4.0 %collective-permute-start.5 = (bf16[22,32,128]{2,1,0:T(8,128)(2,1)S(1)}, bf16[22,32,128]{2,1,0:T(8,128)(2,1)S(1)}, u32[]{:S(2)}, u32[]{:S(2)}) collective-permute-start(bf16[22,32,128]{2,1,0:T(8,128)(2,1)S(1)} %get-tuple-element.33), channel_id=1, source_target_pairs={{2,0},{4,2},{6,4},{8,6},{10,8},{12,10},{14,12},{16,14},{18,16},{20... | collective-permute-start | bytes 540680 | tf_op jit(solution)/shard_map/ppermute | solution.py:24
  21.9 0.0 collective-permute-done.2.refs_4_
  21.9 0.0 copy-start.4
  21.9 0.0 collective-permute-done.3.refs_5_
  21.9 0.0 copy-start.5
  21.9 3.2 %collective-permute-done.4.refs_6_ = bf16[22,32,128]{2,1,0:T(8,128)(2,1)S(1)} collective-permute-done((bf16[22,32,128]{2,1,0:T(8,128)(2,1)S(1)}, bf16[22,32,128]{2,1,0:T(8,128)(2,1)S(1)}, u32[]{:S(2)}, u32[]{:S(2)}) %collective-permute-start.4) | collective-permute-done | bytes 180256 | tf_op jit(solution)/shard_map/ppermute | solution.py:23
  25.1 0.0 copy-start.6
  25.1 0.0 collective-permute-done.5.refs_7_
  25.1 0.0 copy-start.7
  25.1 0.0 copy-done
  25.1 0.0 copy-done.1
  25.1 0.0 copy-done.4
  25.1 0.0 copy-done.5
  25.1 0.6 copy-done.6
  25.8 0.1 copy-done.7
  25.8 25.2 %shard_map.95 = (bf16[8,8,32,128]{3,2,1,0:T(8,128)(2,1)}, bf16[8,8,32,128]{3,2,1,0:T(8,128)(2,1)S(1)}, bf16[8,8,32,128]{3,2,1,0:T(8,128)(2,1)S(1)}, bf16[8,32,12...) custom-call(s32[1]{0:T(128)} %bitcast.core, ...), custom_call_target="tpu_custom_call" | custom-call | flops 12683575296 | bytes 10485760 | tf_op jit(solution)/shard_map/pallas_call | solution.py:406
  51.0 0.1 slice_bitcast_fusion
  51.0 2.1 %collective-permute-start.6 = (bf16[3456,128]{1,0:T(8,128)(2,1)S(1)}, bf16[3456,128]{1,0:T(8,128)(2,1)S(1)}, u32[]{:S(2)}, u32[]{:S(2)}) collective-permute-start(bf16[3456,128]{1,0:T(8,128)(2,1)S(1)} %slice_bitcast_fusion), channel_id=1, source_target_pairs={{0,1},{1,0},{2,3},{3,2},{4,5},{5,4},{6,7},{7,6},{8,9},{9,8},{10,11... | collective-permute-start | bytes 2654216 | tf_op jit(solution)/shard_map/ppermute | solution.py:418
  53.1 2.1 %collective-permute-done.6 = bf16[3456,128]{1,0:T(8,128)(2,1)S(1)} collective-permute-done((bf16[3456,128]{1,0:T(8,128)(2,1)S(1)}, bf16[3456,128]{1,0:T(8,128)(2,1)S(1)}, u32[]{:S(2)}, u32[]{:S(2)}) %collective-permute-start.6) | collective-permute-done | bytes 884768 | tf_op jit(solution)/shard_map/ppermute | solution.py:418
  55.2 1.1 fusion
  56.3 6.4 %all-to-all-start = ((bf16[16,216,128]{2,1,0:T(8,128)(2,1)}), bf16[16,216,128]{2,1,0:T(8,128)(2,1)S(1)}, u32[]{:S(2)}, u32[]{:S(2)}) async-start(bf16[16,216,128]{2,1,0:T(8,128)(2,1)} %bitcast.10), calls=%async_computation | async-start | bytes 1769472 | tf_op jit(solution)/shard_map/all_to_all | solution.py:423
  62.7 0.1 collective-permute-start.7
  62.8 2.7 %collective-permute-start.8 = (bf16[8,32,128]{2,1,0:T(8,128)(2,1)S(1)}, bf16[8,32,128]{2,1,0:T(8,128)(2,1)S(1)}, u32[]{:S(2)}, u32[]{:S(2)}) collective-permute-start(bf16[8,32,128]{2,1,0:T(8,128)(2,1)S(1)} %get-tuple-element.38), channel_id=1, source_target_pairs={{32,0},{64,32},{96,64},{128,96},{160,128},{192,160},{224,192},{0,2... | collective-permute-start | bytes 196616 | tf_op jit(solution)/shard_map/ppermute | solution.py:24
  65.5 11.8 %all-to-all-done = bf16[16,216,128]{2,1,0:T(8,128)(2,1)S(1)} async-done(((bf16[16,216,128]{2,1,0:T(8,128)(2,1)}), bf16[16,216,128]{2,1,0:T(8,128)(2,1)S(1)}, u32[]{:S(2)}, u32[]{:S(2)}) %all-to-all-start) | async-done | bytes 884768 | tf_op jit(solution)/shard_map/all_to_all | solution.py:423
  77.3 0.1 reduce_sum.12
  77.4 0.0 collective-permute-done.7.xm
  77.4 0.0 collective-permute-done.8.xp
  77.4 0.1 collective-permute-start.9
  77.5 3.0 %collective-permute-done.9 = bf16[216,128]{1,0:T(8,128)(2,1)S(1)} collective-permute-done((bf16[216,128]{1,0:T(8,128)(2,1)S(1)}, bf16[216,128]{1,0:T(8,128)(2,1)S(1)}, u32[]{:S(2)}, u32[]{:S(2)}) %collective-permute-start.9) | collective-permute-done | bytes 55328 | tf_op jit(solution)/shard_map/ppermute | solution.py:431
  80.5 4.1 %collective-permute-start.10 = (bf16[216,128]{1,0:T(8,128)(2,1)S(1)}, bf16[216,128]{1,0:T(8,128)(2,1)S(1)}, u32[]{:S(2)}, u32[]{:S(2)}) collective-permute-start(bf16[216,128]{1,0:T(8,128)(2,1)S(1)} %add_convert_fusion.2), channel_id=1, source_target_pairs={{0,96},{32,64},{64,32},{96,0},{128,224},{160,192},{192,160},{224,1... | collective-permute-start | bytes 165896 | tf_op jit(solution)/shard_map/ppermute | solution.py:431
  84.7 1.5 %collective-permute-done.10 = bf16[216,128]{1,0:T(8,128)(2,1)S(1)} collective-permute-done((bf16[216,128]{1,0:T(8,128)(2,1)S(1)}, bf16[216,128]{1,0:T(8,128)(2,1)S(1)}, u32[]{:S(2)}, u32[]{:S(2)}) %collective-permute-start.10) | collective-permute-done | bytes 55328 | tf_op jit(solution)/shard_map/ppermute | solution.py:431
  86.2 0.0 copy-start.3
  86.2 1.8 %collective-permute-start.11 = (bf16[216,128]{1,0:T(8,128)(2,1)S(1)}, bf16[216,128]{1,0:T(8,128)(2,1)S(1)}, u32[]{:S(2)}, u32[]{:S(2)}) collective-permute-start(bf16[216,128]{1,0:T(8,128)(2,1)S(1)} %add_convert_fusion.1), channel_id=1, source_target_pairs={{0,224},{32,192},{64,160},{96,128},{128,96},{160,64},{192,32},{224... | collective-permute-start | bytes 165896 | tf_op jit(solution)/shard_map/ppermute | solution.py:431
  88.1 0.4 collective-permute-start.12
  88.5 4.4 %collective-permute-start.13 = (bf16[10,32,128]{2,1,0:T(8,128)(2,1)S(1)}, bf16[10,32,128]{2,1,0:T(8,128)(2,1)S(1)}, u32[]{:S(2)}, u32[]{:S(2)}) collective-permute-start(bf16[10,32,128]{2,1,0:T(8,128)(2,1)S(1)} %get-tuple-element.44), channel_id=1, source_target_pairs={{2,0},{4,2},{6,4},{8,6},{10,8},{12,10},{14,12},{16,14},{18,16},{20... | collective-permute-start | bytes 245768 | tf_op jit(solution)/shard_map/ppermute | solution.py:24
  92.9 0.0 collective-permute-done.11
  93.0 1.8 %collective-permute-done.12.ym = bf16[10,32,128]{2,1,0:T(8,128)(2,1)S(1)} collective-permute-done((bf16[10,32,128]{2,1,0:T(8,128)(2,1)S(1)}, bf16[10,32,128]{2,1,0:T(8,128)(2,1)S(1)}, u32[]{:S(2)}, u32[]{:S(2)}) %collective-permute-start.12) | collective-permute-done | bytes 81952 | tf_op jit(solution)/shard_map/ppermute | solution.py:23
  94.8 0.0 collective-permute-done.13.yp
  94.8 1.0 broadcast_in_dim.2
  95.8 6.2 %all-to-all-start.1 = ((bf16[16,216,128]{2,1,0:T(8,128)(2,1)}), bf16[16,216,128]{2,1,0:T(8,128)(2,1)S(1)}, u32[]{:S(2)}, u32[]{:S(2)}) async-start(bf16[16,216,128]{2,1,0:T(8,128)(2,1)} %broadcast_in_dim.2), calls=%async_computation.1 | async-start | bytes 1769472 | tf_op jit(solution)/shard_map/all_to_all | solution.py:440
  102.0 0.0 copy-done.3
  102.0 5.0 %shard_map.97 = bf16[8,8,32,128]{3,2,1,0:T(8,128)(2,1)} custom-call(bf16[1,32,128]{2,1,0:T(8,128)(2,1)S(1)} %get-tuple-element.34.refs_10_.own, bf16[8,8,32,128]{3,2,1,0:T(8,128)(2,1)S(1)} %get-tuple-element.42.b1, bf16[8,8,32,128]{3,2,1,0:T(8,128)(2,1)S(1)} %get-tuple-element.47.b2, bf16[8,32,128]{2,1,0:T(8,128)(2,1)S(1)} %collective-permute-done.7.xm, ...), custom_call_target="tpu_custom_call" | custom-call | flops 1811939328 | bytes 4194304 | tf_op jit(solution)/shard_map/pallas_call | solution.py:406
  107.0 6.1 %all-to-all-done.1 = bf16[16,216,128]{2,1,0:T(8,128)(2,1)S(1)} async-done(((bf16[16,216,128]{2,1,0:T(8,128)(2,1)}), bf16[16,216,128]{2,1,0:T(8,128)(2,1)S(1)}, u32[]{:S(2)}, u32[]{:S(2)}) %all-to-all-start.1) | async-done | bytes 884768 | tf_op jit(solution)/shard_map/all_to_all | solution.py:440
  113.2 7.2 %collective-permute-start.14 = (bf16[27,128,128]{2,1,0:T(8,128)(2,1)S(1)}, bf16[27,128,128]{2,1,0:T(8,128)(2,1)S(1)}, u32[]{:S(2)}, u32[]{:S(2)}) collective-permute-start(bf16[27,128,128]{2,1,0:T(8,128)(2,1)S(1)} %bitcast.21), channel_id=1, source_target_pairs={{0,1},{1,0},{2,3},{3,2},{4,5},{5,4},{6,7},{7,6},{8,9},{9,8},{10,11... | collective-permute-start | bytes 2654216 | tf_op jit(solution)/shard_map/ppermute | solution.py:418
  120.4 2.1 %collective-permute-done.14 = bf16[27,128,128]{2,1,0:T(8,128)(2,1)S(1)} collective-permute-done((bf16[27,128,128]{2,1,0:T(8,128)(2,1)S(1)}, bf16[27,128,128]{2,1,0:T(8,128)(2,1)S(1)}, u32[]{:S(2)}, u32[]{:S(2)}) %collective-permute-start.14) | collective-permute-done | bytes 884768 | tf_op jit(solution)/shard_map/ppermute | solution.py:418
  122.4 2.0 %select_convert_fusion = (f32[27,128,128]{2,1,0:T(8,128)}, f32[27,128,128]{2,1,0:T(8,128)}) fusion(bf16[27,128,128]{2,1,0:T(8,128)(2,1)S(1)} %collective-permute-done.14, bf16[27,128,128]{2,1,0:T(8,128)(2,1)S(1)} %bitcast.22, pred[]{:T(512)S(6)} %eq.4), kind=kLoop, calls=%fused_computation.2 | loop fusion | flops 1769472 | bytes 5308417 | tf_op jit(solution)/shard_map/convert_element_type | solution.py:521
  (5 shorter events, 0.1 us)
Async XLA Ops:
  1.3 0.7 copy-start.2
  3.8 12.7 %collective-permute-start = (bf16[33,32,128]{2,1,0:T(8,128)(2,1)S(1)}, bf16[33,32,128]{2,1,0:T(8,128)(2,1)S(1)}, u32[]{:S(2)}, u32[]{:S(2)}) collective-permute-start(bf16[33,32,128]{2,1,0:T(8,128)(2,1)S(1)} %get-tuple-element.28), channel_id=1, source_target_pairs={{0,32},{32,64},{64,96},{96,128},{128,160},{160,192},{192,224},{224... | collective-permute-start | bytes 811016 | tf_op jit(solution)/shard_map/ppermute | solution.py:23
  6.4 10.2 %collective-permute-start.1 = (bf16[33,32,128]{2,1,0:T(8,128)(2,1)S(1)}, bf16[33,32,128]{2,1,0:T(8,128)(2,1)S(1)}, u32[]{:S(2)}, u32[]{:S(2)}) collective-permute-start(bf16[33,32,128]{2,1,0:T(8,128)(2,1)S(1)} %get-tuple-element.29), channel_id=1, source_target_pairs={{32,0},{64,32},{96,64},{128,96},{160,128},{192,160},{224,192},{0,2... | collective-permute-start | bytes 811016 | tf_op jit(solution)/shard_map/ppermute | solution.py:24
  10.4 11.4 %collective-permute-start.2 = (bf16[33,32,128]{2,1,0:T(8,128)(2,1)S(1)}, bf16[33,32,128]{2,1,0:T(8,128)(2,1)S(1)}, u32[]{:S(2)}, u32[]{:S(2)}) collective-permute-start(bf16[33,32,128]{2,1,0:T(8,128)(2,1)S(1)} %get-tuple-element.30), channel_id=1, source_target_pairs={{0,2},{2,4},{4,6},{6,8},{8,10},{10,12},{12,14},{14,16},{16,18},{18... | collective-permute-start | bytes 811016 | tf_op jit(solution)/shard_map/ppermute | solution.py:23
  11.6 10.2 %collective-permute-start.3 = (bf16[33,32,128]{2,1,0:T(8,128)(2,1)S(1)}, bf16[33,32,128]{2,1,0:T(8,128)(2,1)S(1)}, u32[]{:S(2)}, u32[]{:S(2)}) collective-permute-start(bf16[33,32,128]{2,1,0:T(8,128)(2,1)S(1)} %get-tuple-element.31), channel_id=1, source_target_pairs={{2,0},{4,2},{6,4},{8,6},{10,8},{12,10},{14,12},{16,14},{18,16},{20... | collective-permute-start | bytes 811016 | tf_op jit(solution)/shard_map/ppermute | solution.py:24
  16.5 8.6 %copy-start = (bf16[33,32,128]{2,1,0:T(8,128)(2,1)}, bf16[33,32,128]{2,1,0:T(8,128)(2,1)S(1)}, u32[]{:S(2)}) copy-start(bf16[33,32,128]{2,1,0:T(8,128)(2,1)S(1)} %collective-permute-done.xm.refs_2_) | copy-start | bytes 811012
  16.5 8.6 %copy-start.1 = (bf16[33,32,128]{2,1,0:T(8,128)(2,1)}, bf16[33,32,128]{2,1,0:T(8,128)(2,1)S(1)}, u32[]{:S(2)}) copy-start(bf16[33,32,128]{2,1,0:T(8,128)(2,1)S(1)} %collective-permute-done.1.xp.refs_3_) | copy-start | bytes 811012
  16.6 8.5 %collective-permute-start.4 = (bf16[22,32,128]{2,1,0:T(8,128)(2,1)S(1)}, bf16[22,32,128]{2,1,0:T(8,128)(2,1)S(1)}, u32[]{:S(2)}, u32[]{:S(2)}) collective-permute-start(bf16[22,32,128]{2,1,0:T(8,128)(2,1)S(1)} %get-tuple-element.32), channel_id=1, source_target_pairs={{0,2},{2,4},{4,6},{6,8},{8,10},{10,12},{12,14},{14,16},{16,18},{18... | collective-permute-start | bytes 540680 | tf_op jit(solution)/shard_map/ppermute | solution.py:23
  17.9 7.2 %collective-permute-start.5 = (bf16[22,32,128]{2,1,0:T(8,128)(2,1)S(1)}, bf16[22,32,128]{2,1,0:T(8,128)(2,1)S(1)}, u32[]{:S(2)}, u32[]{:S(2)}) collective-permute-start(bf16[22,32,128]{2,1,0:T(8,128)(2,1)S(1)} %get-tuple-element.33), channel_id=1, source_target_pairs={{2,0},{4,2},{6,4},{8,6},{10,8},{12,10},{14,12},{16,14},{18,16},{20... | collective-permute-start | bytes 540680 | tf_op jit(solution)/shard_map/ppermute | solution.py:24
  21.9 3.3 %copy-start.4 = (bf16[33,32,128]{2,1,0:T(8,128)(2,1)}, bf16[33,32,128]{2,1,0:T(8,128)(2,1)S(1)}, u32[]{:S(2)}) copy-start(bf16[33,32,128]{2,1,0:T(8,128)(2,1)S(1)} %collective-permute-done.2.refs_4_) | copy-start | bytes 811012
  21.9 3.3 %copy-start.5 = (bf16[33,32,128]{2,1,0:T(8,128)(2,1)}, bf16[33,32,128]{2,1,0:T(8,128)(2,1)S(1)}, u32[]{:S(2)}) copy-start(bf16[33,32,128]{2,1,0:T(8,128)(2,1)S(1)} %collective-permute-done.3.refs_5_) | copy-start | bytes 811012
  25.1 0.7 copy-start.6
  25.1 0.7 copy-start.7
  51.0 4.1 %collective-permute-start.6 = (bf16[3456,128]{1,0:T(8,128)(2,1)S(1)}, bf16[3456,128]{1,0:T(8,128)(2,1)S(1)}, u32[]{:S(2)}, u32[]{:S(2)}) collective-permute-start(bf16[3456,128]{1,0:T(8,128)(2,1)S(1)} %slice_bitcast_fusion), channel_id=1, source_target_pairs={{0,1},{1,0},{2,3},{3,2},{4,5},{5,4},{6,7},{7,6},{8,9},{9,8},{10,11... | collective-permute-start | bytes 2654216 | tf_op jit(solution)/shard_map/ppermute | solution.py:418
  56.3 21.0 %all-to-all-start = ((bf16[16,216,128]{2,1,0:T(8,128)(2,1)}), bf16[16,216,128]{2,1,0:T(8,128)(2,1)S(1)}, u32[]{:S(2)}, u32[]{:S(2)}) async-start(bf16[16,216,128]{2,1,0:T(8,128)(2,1)} %bitcast.10), calls=%async_computation | async-start | bytes 1769472 | tf_op jit(solution)/shard_map/all_to_all | solution.py:423
  62.7 14.7 %collective-permute-start.7 = (bf16[8,32,128]{2,1,0:T(8,128)(2,1)S(1)}, bf16[8,32,128]{2,1,0:T(8,128)(2,1)S(1)}, u32[]{:S(2)}, u32[]{:S(2)}) collective-permute-start(bf16[8,32,128]{2,1,0:T(8,128)(2,1)S(1)} %get-tuple-element.37), channel_id=1, source_target_pairs={{0,32},{32,64},{64,96},{96,128},{128,160},{160,192},{192,224},{224... | collective-permute-start | bytes 196616 | tf_op jit(solution)/shard_map/ppermute | solution.py:23
  62.8 14.6 %collective-permute-start.8 = (bf16[8,32,128]{2,1,0:T(8,128)(2,1)S(1)}, bf16[8,32,128]{2,1,0:T(8,128)(2,1)S(1)}, u32[]{:S(2)}, u32[]{:S(2)}) collective-permute-start(bf16[8,32,128]{2,1,0:T(8,128)(2,1)S(1)} %get-tuple-element.38), channel_id=1, source_target_pairs={{32,0},{64,32},{96,64},{128,96},{160,128},{192,160},{224,192},{0,2... | collective-permute-start | bytes 196616 | tf_op jit(solution)/shard_map/ppermute | solution.py:24
  77.4 3.1 %collective-permute-start.9 = (bf16[216,128]{1,0:T(8,128)(2,1)S(1)}, bf16[216,128]{1,0:T(8,128)(2,1)S(1)}, u32[]{:S(2)}, u32[]{:S(2)}) collective-permute-start(bf16[216,128]{1,0:T(8,128)(2,1)S(1)} %reduce_sum.12), channel_id=1, source_target_pairs={{0,32},{32,0},{64,96},{96,64},{128,160},{160,128},{192,224},{224,1... | collective-permute-start | bytes 165896 | tf_op jit(solution)/shard_map/ppermute | solution.py:431
  80.5 5.7 %collective-permute-start.10 = (bf16[216,128]{1,0:T(8,128)(2,1)S(1)}, bf16[216,128]{1,0:T(8,128)(2,1)S(1)}, u32[]{:S(2)}, u32[]{:S(2)}) collective-permute-start(bf16[216,128]{1,0:T(8,128)(2,1)S(1)} %add_convert_fusion.2), channel_id=1, source_target_pairs={{0,96},{32,64},{64,32},{96,0},{128,224},{160,192},{192,160},{224,1... | collective-permute-start | bytes 165896 | tf_op jit(solution)/shard_map/ppermute | solution.py:431
  86.2 15.7 %copy-start.3 = (bf16[27,128,128]{2,1,0:T(8,128)(2,1)S(1)}, bf16[27,128,128]{2,1,0:T(8,128)(2,1)}, u32[]{:S(2)}) copy-start(bf16[27,128,128]{2,1,0:T(8,128)(2,1)} %param.8) | copy-start | bytes 2654212
  86.2 6.7 %collective-permute-start.11 = (bf16[216,128]{1,0:T(8,128)(2,1)S(1)}, bf16[216,128]{1,0:T(8,128)(2,1)S(1)}, u32[]{:S(2)}, u32[]{:S(2)}) collective-permute-start(bf16[216,128]{1,0:T(8,128)(2,1)S(1)} %add_convert_fusion.1), channel_id=1, source_target_pairs={{0,224},{32,192},{64,160},{96,128},{128,96},{160,64},{192,32},{224... | collective-permute-start | bytes 165896 | tf_op jit(solution)/shard_map/ppermute | solution.py:431
  88.1 6.7 %collective-permute-start.12 = (bf16[10,32,128]{2,1,0:T(8,128)(2,1)S(1)}, bf16[10,32,128]{2,1,0:T(8,128)(2,1)S(1)}, u32[]{:S(2)}, u32[]{:S(2)}) collective-permute-start(bf16[10,32,128]{2,1,0:T(8,128)(2,1)S(1)} %get-tuple-element.43), channel_id=1, source_target_pairs={{0,2},{2,4},{4,6},{6,8},{8,10},{10,12},{12,14},{14,16},{16,18},{18... | collective-permute-start | bytes 245768 | tf_op jit(solution)/shard_map/ppermute | solution.py:23
  88.5 6.3 %collective-permute-start.13 = (bf16[10,32,128]{2,1,0:T(8,128)(2,1)S(1)}, bf16[10,32,128]{2,1,0:T(8,128)(2,1)S(1)}, u32[]{:S(2)}, u32[]{:S(2)}) collective-permute-start(bf16[10,32,128]{2,1,0:T(8,128)(2,1)S(1)} %get-tuple-element.44), channel_id=1, source_target_pairs={{2,0},{4,2},{6,4},{8,6},{10,8},{12,10},{14,12},{16,14},{18,16},{20... | collective-permute-start | bytes 245768 | tf_op jit(solution)/shard_map/ppermute | solution.py:24
  95.8 17.4 %all-to-all-start.1 = ((bf16[16,216,128]{2,1,0:T(8,128)(2,1)}), bf16[16,216,128]{2,1,0:T(8,128)(2,1)S(1)}, u32[]{:S(2)}, u32[]{:S(2)}) async-start(bf16[16,216,128]{2,1,0:T(8,128)(2,1)} %broadcast_in_dim.2), calls=%async_computation.1 | async-start | bytes 1769472 | tf_op jit(solution)/shard_map/all_to_all | solution.py:440
  113.2 9.3 %collective-permute-start.14 = (bf16[27,128,128]{2,1,0:T(8,128)(2,1)S(1)}, bf16[27,128,128]{2,1,0:T(8,128)(2,1)S(1)}, u32[]{:S(2)}, u32[]{:S(2)}) collective-permute-start(bf16[27,128,128]{2,1,0:T(8,128)(2,1)S(1)} %bitcast.21), channel_id=1, source_target_pairs={{0,1},{1,0},{2,3},{3,2},{4,5},{5,4},{6,7},{7,6},{8,9},{9,8},{10,11... | collective-permute-start | bytes 2654216 | tf_op jit(solution)/shard_map/ppermute | solution.py:418

commit v6 on v5

--- a/solution.py
+++ b/solution.py
@@ -227,19 +227,19 @@
 
 
 def main_kernel(scale, core, *refs):
-    far, own, refs = refs[:10], refs[10], refs[11:]
+    far, (xm, xp, ym, yp, qm, qp, own), refs = refs[:4], refs[4:11], refs[11:]
     out, b2o, b1o, elow, ehigh, gr = refs[:6]
-    near, (w2f, sems, field, hid, back, p1, p2, px, py, pc, slope1, turned, wide, staged, tab, sem) = refs[6:16], refs[16:]
-    x, cot, xm, xp, ym, yp, qm, qp, w1, w2 = near
-    copies = [pltpu.make_async_copy(far[i], near[i], sems.at[i]) for i in range(10)]
-    order = [8, 0, 2, 3, 4, 5, 6, 7, 9, 1]
+    near, (w2f, sems, field, hid, back, p1, p2, px, py, pc, slope1, turned, wide, staged, tab, sem) = refs[6:10], refs[10:]
+    x, cot, w1, w2 = near
+    copies = [pltpu.make_async_copy(far[i], near[i], sems.at[i]) for i in range(4)]
+    order = [2, 0, 3, 1]
     for i in order:
         copies[i].start()
     for ref in (field, hid, back):
         zero_slot(ref)
     clear_turned(turned)
     clear_band(wide)
-    copies[8].wait()
+    copies[2].wait()
     band(w1, wide)
     for i in order[1:]:
         copies[i].wait()
@@ -472,10 +472,8 @@
         [block, block, block, edge, edge, shape_of(2, 27 * C, C)],
         [
             *[pltpu.VMEM((BE, BE, ROWS, C), BF16)] * 2,
-            *[pltpu.VMEM((33, ROWS, C), BF16)] * 4,
-            *[pltpu.VMEM((22, ROWS, C), BF16)] * 2,
             *[pltpu.VMEM((27 * C, C), BF16)] * 3,
-            pltpu.SemaphoreType.DMA((10,)),
+            pltpu.SemaphoreType.DMA((4,)),
             pltpu.VMEM((14, 14, ROWS + BE, C), F32),
             pltpu.VMEM((12, 12, ROWS + BE, C), F32),
             pltpu.VMEM((10, 10, ROWS + BE, C), F32),
@@ -489,8 +487,8 @@
             pltpu.VMEM((36 * C, 2 * C), BF16),
             *tables,
         ],
-        (7 * unit, 10 * 2**20), 40, 1, 10,
-        core.reshape(1), x, cot, xm, xp, ym, yp, qm, qp, w1, w2, own,
+        (7 * unit, 10 * 2**20), 36, 1, 4,
+        core.reshape(1), x, cot, w1, w2, xm, xp, ym, yp, qm, qp, own,
     )
 
     received = swap_cores(grads[1])

time: 125 us -> 124 us (level)
  no operation moved by 1% of the time
where the time goes in v6:
time: 124 us; the launch traced here: 123 us
  starting transfers between devices  52.3 us (42%)
  waiting for transfers between devices  32.8 us (26%)
  Pallas kernels  31.6 us (25%)
  other arithmetic  3.34 us (3%)
  local copies, waits for them, and re-layouts  1.77 us (1%)
  between operations  1.42 us (1%)
    pallas_call x5, Pallas kernels, call(): pl.pallas_call(kernel, out_shape=outs, in_specs=[smem] * scalars + [anywh...  31.6 us
    ppermute x5, starting transfers between devices, shift_pair(): from_high = lax.ppermute(low, axis, [((i + 1) % n, i) for i in range(n)])  18.8 us
    all_to_all x1, waiting for transfers between devices, sum_scatter(): lax.all_to_all(part.reshape(n, part.shape[0] // n, C), axis, 0, 0, tiled=...  11.8 us
    ppermute x2, starting transfers between devices, swap_cores(): return lax.ppermute(part, 'dp', [(0, 1), (1, 0)])  9.31 us
    all_to_all x1, starting transfers between devices, sum_scatter(): lax.all_to_all(part.reshape(n, part.shape[0] // n, C), axis, 0, 0, tiled=...  6.43 us
    ppermute x5, waiting for transfers between devices, shift_pair(): from_low = lax.ppermute(high, axis, [(i, (i + 1) % n) for i in range(n)])  6.21 us
    all_to_all x1, starting transfers between devices, gather_axis(): lax.all_to_all(copies, axis, 0, 0, tiled=True).reshape(n * part.shape[0], C)  6.16 us
    all_to_all x1, waiting for transfers between devices, gather_axis(): lax.all_to_all(copies, axis, 0, 0, tiled=True).reshape(n * part.shape[0], C)  6.13 us
  transfers between devices with their start and end apart: 17, of which 9 were waited for; matrix products, arithmetic and copies ran while one was open for 0% of the time, Pallas kernels for 4%

profile of v6, /device:TPU:1, one launch (start us, length us, event | category | flops | bytes accessed | tf_op | source)
XLA Modules:
  0.0 123.2 jit_solution(12977325069203659393)
XLA Ops:
  1.3 0.0 copy-start
  1.3 0.7 copy-done
  2.0 1.9 %shard_map.93 = (bf16[33,32,128]{2,1,0:T(8,128)(2,1)S(1)}, bf16[33,32,128]{2,1,0:T(8,128)(2,1)S(1)}, bf16[33,32,128]{2,1,0:T(8,128)(2,1)S(1)}, bf16[33,32,128]{2,1,0:T(8,128)(2,1)S(1)}, bf16[1,32,128]{2,1,0:T(8,128)(2,1)S(1)}) custom-call(s32[4,26]{1,0:T(4,128)S(1)} %bitcast.18, s32[1]{0:T(128)} %bitcast.17.count, bf16[8,8,32,128]{3,2,1,0:T(8,128)(2,1)} %bitcast.23, ...), custom_call_target="tpu_custom_call" | custom-call | bytes 2097152 | tf_op jit(solution)/shard_map/pallas_call | solution.py:406
  3.8 2.5 %collective-permute-start = (bf16[33,32,128]{2,1,0:T(8,128)(2,1)S(1)}, bf16[33,32,128]{2,1,0:T(8,128)(2,1)S(1)}, u32[]{:S(2)}, u32[]{:S(2)}) collective-permute-start(bf16[33,32,128]{2,1,0:T(8,128)(2,1)S(1)} %get-tuple-element.28), channel_id=1, source_target_pairs={{0,32},{32,64},{64,96},{96,128},{128,160},{160,192},{192,224},{224... | collective-permute-start | bytes 811016 | tf_op jit(solution)/shard_map/ppermute | solution.py:23
  6.4 4.0 %collective-permute-start.1 = (bf16[33,32,128]{2,1,0:T(8,128)(2,1)S(1)}, bf16[33,32,128]{2,1,0:T(8,128)(2,1)S(1)}, u32[]{:S(2)}, u32[]{:S(2)}) collective-permute-start(bf16[33,32,128]{2,1,0:T(8,128)(2,1)S(1)} %get-tuple-element.29), channel_id=1, source_target_pairs={{32,0},{64,32},{96,64},{128,96},{160,128},{192,160},{224,192},{0,2... | collective-permute-start | bytes 811016 | tf_op jit(solution)/shard_map/ppermute | solution.py:24
  10.4 1.2 collective-permute-start.2
  11.6 3.7 %collective-permute-start.3 = (bf16[33,32,128]{2,1,0:T(8,128)(2,1)S(1)}, bf16[33,32,128]{2,1,0:T(8,128)(2,1)S(1)}, u32[]{:S(2)}, u32[]{:S(2)}) collective-permute-start(bf16[33,32,128]{2,1,0:T(8,128)(2,1)S(1)} %get-tuple-element.31), channel_id=1, source_target_pairs={{2,0},{4,2},{6,4},{8,6},{10,8},{12,10},{14,12},{16,14},{18,16},{20... | collective-permute-start | bytes 811016 | tf_op jit(solution)/shard_map/ppermute | solution.py:24
  15.3 1.2 collective-permute-done.xm.refs_4_
  16.5 0.0 collective-permute-done.1.xp.refs_5_
  16.6 1.3 %collective-permute-start.4 = (bf16[22,32,128]{2,1,0:T(8,128)(2,1)S(1)}, bf16[22,32,128]{2,1,0:T(8,128)(2,1)S(1)}, u32[]{:S(2)}, u32[]{:S(2)}) collective-permute-start(bf16[22,32,128]{2,1,0:T(8,128)(2,1)S(1)} %get-tuple-element.32), channel_id=1, source_target_pairs={{0,2},{2,4},{4,6},{6,8},{8,10},{10,12},{12,14},{14,16},{16,18},{18... | collective-permute-start | bytes 540680 | tf_op jit(solution)/shard_map/ppermute | solution.py:23
  17.9 4.0 %collective-permute-start.5 = (bf16[22,32,128]{2,1,0:T(8,128)(2,1)S(1)}, bf16[22,32,128]{2,1,0:T(8,128)(2,1)S(1)}, u32[]{:S(2)}, u32[]{:S(2)}) collective-permute-start(bf16[22,32,128]{2,1,0:T(8,128)(2,1)S(1)} %get-tuple-element.33), channel_id=1, source_target_pairs={{2,0},{4,2},{6,4},{8,6},{10,8},{12,10},{14,12},{16,14},{18,16},{20... | collective-permute-start | bytes 540680 | tf_op jit(solution)/shard_map/ppermute | solution.py:24
  21.8 0.0 collective-permute-done.2.refs_6_
  21.8 0.0 collective-permute-done.3.refs_7_
  21.9 3.2 %collective-permute-done.4.refs_8_ = bf16[22,32,128]{2,1,0:T(8,128)(2,1)S(1)} collective-permute-done((bf16[22,32,128]{2,1,0:T(8,128)(2,1)S(1)}, bf16[22,32,128]{2,1,0:T(8,128)(2,1)S(1)}, u32[]{:S(2)}, u32[]{:S(2)}) %collective-permute-start.4) | collective-permute-done | bytes 180256 | tf_op jit(solution)/shard_map/ppermute | solution.py:23
  25.1 0.0 collective-permute-done.5.refs_9_
  25.1 24.6 %shard_map.95 = (bf16[8,8,32,128]{3,2,1,0:T(8,128)(2,1)}, bf16[8,8,32,128]{3,2,1,0:T(8,128)(2,1)S(1)}, bf16[8,8,32,128]{3,2,1,0:T(8,128)(2,1)S(1)}, bf16[8,32,12...) custom-call(s32[1]{0:T(128)} %bitcast.core, ...), custom_call_target="tpu_custom_call" | custom-call | flops 12683575296 | bytes 10485760 | tf_op jit(solution)/shard_map/pallas_call | solution.py:406
  49.7 0.1 slice_bitcast_fusion
  49.8 2.1 %collective-permute-start.6 = (bf16[3456,128]{1,0:T(8,128)(2,1)S(1)}, bf16[3456,128]{1,0:T(8,128)(2,1)S(1)}, u32[]{:S(2)}, u32[]{:S(2)}) collective-permute-start(bf16[3456,128]{1,0:T(8,128)(2,1)S(1)} %slice_bitcast_fusion), channel_id=1, source_target_pairs={{0,1},{1,0},{2,3},{3,2},{4,5},{5,4},{6,7},{7,6},{8,9},{9,8},{10,11... | collective-permute-start | bytes 2654216 | tf_op jit(solution)/shard_map/ppermute | solution.py:418
  51.9 2.1 %collective-permute-done.6 = bf16[3456,128]{1,0:T(8,128)(2,1)S(1)} collective-permute-done((bf16[3456,128]{1,0:T(8,128)(2,1)S(1)}, bf16[3456,128]{1,0:T(8,128)(2,1)S(1)}, u32[]{:S(2)}, u32[]{:S(2)}) %collective-permute-start.6) | collective-permute-done | bytes 884768 | tf_op jit(solution)/shard_map/ppermute | solution.py:418
  53.9 1.1 fusion
  55.0 6.4 %all-to-all-start = ((bf16[16,216,128]{2,1,0:T(8,128)(2,1)}), bf16[16,216,128]{2,1,0:T(8,128)(2,1)S(1)}, u32[]{:S(2)}, u32[]{:S(2)}) async-start(bf16[16,216,128]{2,1,0:T(8,128)(2,1)} %bitcast.10), calls=%async_computation | async-start | bytes 1769472 | tf_op jit(solution)/shard_map/all_to_all | solution.py:423
  61.5 0.1 collective-permute-start.7
  61.6 2.7 %collective-permute-start.8 = (bf16[8,32,128]{2,1,0:T(8,128)(2,1)S(1)}, bf16[8,32,128]{2,1,0:T(8,128)(2,1)S(1)}, u32[]{:S(2)}, u32[]{:S(2)}) collective-permute-start(bf16[8,32,128]{2,1,0:T(8,128)(2,1)S(1)} %get-tuple-element.38), channel_id=1, source_target_pairs={{32,0},{64,32},{96,64},{128,96},{160,128},{192,160},{224,192},{0,2... | collective-permute-start | bytes 196616 | tf_op jit(solution)/shard_map/ppermute | solution.py:24
  64.2 11.8 %all-to-all-done = bf16[16,216,128]{2,1,0:T(8,128)(2,1)S(1)} async-done(((bf16[16,216,128]{2,1,0:T(8,128)(2,1)}), bf16[16,216,128]{2,1,0:T(8,128)(2,1)S(1)}, u32[]{:S(2)}, u32[]{:S(2)}) %all-to-all-start) | async-done | bytes 884768 | tf_op jit(solution)/shard_map/all_to_all | solution.py:423
  76.1 0.1 reduce_sum.12
  76.2 0.0 collective-permute-done.7.xm
  76.2 0.0 collective-permute-done.8.xp
  76.2 0.1 collective-permute-start.9
  76.3 3.0 %collective-permute-done.9 = bf16[216,128]{1,0:T(8,128)(2,1)S(1)} collective-permute-done((bf16[216,128]{1,0:T(8,128)(2,1)S(1)}, bf16[216,128]{1,0:T(8,128)(2,1)S(1)}, u32[]{:S(2)}, u32[]{:S(2)}) %collective-permute-start.9) | collective-permute-done | bytes 55328 | tf_op jit(solution)/shard_map/ppermute | solution.py:431
  79.3 4.2 %collective-permute-start.10 = (bf16[216,128]{1,0:T(8,128)(2,1)S(1)}, bf16[216,128]{1,0:T(8,128)(2,1)S(1)}, u32[]{:S(2)}, u32[]{:S(2)}) collective-permute-start(bf16[216,128]{1,0:T(8,128)(2,1)S(1)} %add_convert_fusion.2), channel_id=1, source_target_pairs={{0,96},{32,64},{64,32},{96,0},{128,224},{160,192},{192,160},{224,1... | collective-permute-start | bytes 165896 | tf_op jit(solution)/shard_map/ppermute | solution.py:431
  83.5 1.5 %collective-permute-done.10 = bf16[216,128]{1,0:T(8,128)(2,1)S(1)} collective-permute-done((bf16[216,128]{1,0:T(8,128)(2,1)S(1)}, bf16[216,128]{1,0:T(8,128)(2,1)S(1)}, u32[]{:S(2)}, u32[]{:S(2)}) %collective-permute-start.10) | collective-permute-done | bytes 55328 | tf_op jit(solution)/shard_map/ppermute | solution.py:431
  85.1 0.0 copy-start.1
  85.1 1.8 %collective-permute-start.11 = (bf16[216,128]{1,0:T(8,128)(2,1)S(1)}, bf16[216,128]{1,0:T(8,128)(2,1)S(1)}, u32[]{:S(2)}, u32[]{:S(2)}) collective-permute-start(bf16[216,128]{1,0:T(8,128)(2,1)S(1)} %add_convert_fusion.1), channel_id=1, source_target_pairs={{0,224},{32,192},{64,160},{96,128},{128,96},{160,64},{192,32},{224... | collective-permute-start | bytes 165896 | tf_op jit(solution)/shard_map/ppermute | solution.py:431
  86.8 0.4 collective-permute-start.12
  87.3 4.4 %collective-permute-start.13 = (bf16[10,32,128]{2,1,0:T(8,128)(2,1)S(1)}, bf16[10,32,128]{2,1,0:T(8,128)(2,1)S(1)}, u32[]{:S(2)}, u32[]{:S(2)}) collective-permute-start(bf16[10,32,128]{2,1,0:T(8,128)(2,1)S(1)} %get-tuple-element.44), channel_id=1, source_target_pairs={{2,0},{4,2},{6,4},{8,6},{10,8},{12,10},{14,12},{16,14},{18,16},{20... | collective-permute-start | bytes 245768 | tf_op jit(solution)/shard_map/ppermute | solution.py:24
  91.7 0.0 collective-permute-done.11
  91.7 1.8 %collective-permute-done.12.ym = bf16[10,32,128]{2,1,0:T(8,128)(2,1)S(1)} collective-permute-done((bf16[10,32,128]{2,1,0:T(8,128)(2,1)S(1)}, bf16[10,32,128]{2,1,0:T(8,128)(2,1)S(1)}, u32[]{:S(2)}, u32[]{:S(2)}) %collective-permute-start.12) | collective-permute-done | bytes 81952 | tf_op jit(solution)/shard_map/ppermute | solution.py:23
  93.5 0.0 collective-permute-done.13.yp
  93.5 1.0 broadcast_in_dim.2
  94.6 6.2 %all-to-all-start.1 = ((bf16[16,216,128]{2,1,0:T(8,128)(2,1)}), bf16[16,216,128]{2,1,0:T(8,128)(2,1)S(1)}, u32[]{:S(2)}, u32[]{:S(2)}) async-start(bf16[16,216,128]{2,1,0:T(8,128)(2,1)} %broadcast_in_dim.2), calls=%async_computation.1 | async-start | bytes 1769472 | tf_op jit(solution)/shard_map/all_to_all | solution.py:440
  100.7 0.0 copy-done.1
  100.7 5.1 %shard_map.97 = bf16[8,8,32,128]{3,2,1,0:T(8,128)(2,1)} custom-call(bf16[1,32,128]{2,1,0:T(8,128)(2,1)S(1)} %get-tuple-element.34.refs_10_.own, bf16[8,8,32,128]{3,2,1,0:T(8,128)(2,1)S(1)} %get-tuple-element.42.b1, bf16[8,8,32,128]{3,2,1,0:T(8,128)(2,1)S(1)} %get-tuple-element.47.b2, bf16[8,32,128]{2,1,0:T(8,128)(2,1)S(1)} %collective-permute-done.7.xm, ...), custom_call_target="tpu_custom_call" | custom-call | flops 1811939328 | bytes 4194304 | tf_op jit(solution)/shard_map/pallas_call | solution.py:406
  105.8 6.1 %all-to-all-done.1 = bf16[16,216,128]{2,1,0:T(8,128)(2,1)S(1)} async-done(((bf16[16,216,128]{2,1,0:T(8,128)(2,1)}), bf16[16,216,128]{2,1,0:T(8,128)(2,1)S(1)}, u32[]{:S(2)}, u32[]{:S(2)}) %all-to-all-start.1) | async-done | bytes 884768 | tf_op jit(solution)/shard_map/all_to_all | solution.py:440
  111.9 7.2 %collective-permute-start.14 = (bf16[27,128,128]{2,1,0:T(8,128)(2,1)S(1)}, bf16[27,128,128]{2,1,0:T(8,128)(2,1)S(1)}, u32[]{:S(2)}, u32[]{:S(2)}) collective-permute-start(bf16[27,128,128]{2,1,0:T(8,128)(2,1)S(1)} %bitcast.21), channel_id=1, source_target_pairs={{0,1},{1,0},{2,3},{3,2},{4,5},{5,4},{6,7},{7,6},{8,9},{9,8},{10,11... | collective-permute-start | bytes 2654216 | tf_op jit(solution)/shard_map/ppermute | solution.py:418
  119.2 2.1 %collective-permute-done.14 = bf16[27,128,128]{2,1,0:T(8,128)(2,1)S(1)} collective-permute-done((bf16[27,128,128]{2,1,0:T(8,128)(2,1)S(1)}, bf16[27,128,128]{2,1,0:T(8,128)(2,1)S(1)}, u32[]{:S(2)}, u32[]{:S(2)}) %collective-permute-start.14) | collective-permute-done | bytes 884768 | tf_op jit(solution)/shard_map/ppermute | solution.py:418
  121.2 2.0 %select_convert_fusion = (f32[27,128,128]{2,1,0:T(8,128)}, f32[27,128,128]{2,1,0:T(8,128)}) fusion(bf16[27,128,128]{2,1,0:T(8,128)(2,1)S(1)} %collective-permute-done.14, bf16[27,128,128]{2,1,0:T(8,128)(2,1)S(1)} %bitcast.22, pred[]{:T(512)S(6)} %eq.4), kind=kLoop, calls=%fused_computation.2 | loop fusion | flops 1769472 | bytes 5308417 | tf_op jit(solution)/shard_map/convert_element_type | solution.py:519
  (5 shorter events, 0.1 us)
Async XLA Ops:
  1.3 0.7 copy-start
  3.8 12.7 %collective-permute-start = (bf16[33,32,128]{2,1,0:T(8,128)(2,1)S(1)}, bf16[33,32,128]{2,1,0:T(8,128)(2,1)S(1)}, u32[]{:S(2)}, u32[]{:S(2)}) collective-permute-start(bf16[33,32,128]{2,1,0:T(8,128)(2,1)S(1)} %get-tuple-element.28), channel_id=1, source_target_pairs={{0,32},{32,64},{64,96},{96,128},{128,160},{160,192},{192,224},{224... | collective-permute-start | bytes 811016 | tf_op jit(solution)/shard_map/ppermute | solution.py:23
  6.4 10.1 %collective-permute-start.1 = (bf16[33,32,128]{2,1,0:T(8,128)(2,1)S(1)}, bf16[33,32,128]{2,1,0:T(8,128)(2,1)S(1)}, u32[]{:S(2)}, u32[]{:S(2)}) collective-permute-start(bf16[33,32,128]{2,1,0:T(8,128)(2,1)S(1)} %get-tuple-element.29), channel_id=1, source_target_pairs={{32,0},{64,32},{96,64},{128,96},{160,128},{192,160},{224,192},{0,2... | collective-permute-start | bytes 811016 | tf_op jit(solution)/shard_map/ppermute | solution.py:24
  10.4 11.4 %collective-permute-start.2 = (bf16[33,32,128]{2,1,0:T(8,128)(2,1)S(1)}, bf16[33,32,128]{2,1,0:T(8,128)(2,1)S(1)}, u32[]{:S(2)}, u32[]{:S(2)}) collective-permute-start(bf16[33,32,128]{2,1,0:T(8,128)(2,1)S(1)} %get-tuple-element.30), channel_id=1, source_target_pairs={{0,2},{2,4},{4,6},{6,8},{8,10},{10,12},{12,14},{14,16},{16,18},{18... | collective-permute-start | bytes 811016 | tf_op jit(solution)/shard_map/ppermute | solution.py:23
  11.6 10.2 %collective-permute-start.3 = (bf16[33,32,128]{2,1,0:T(8,128)(2,1)S(1)}, bf16[33,32,128]{2,1,0:T(8,128)(2,1)S(1)}, u32[]{:S(2)}, u32[]{:S(2)}) collective-permute-start(bf16[33,32,128]{2,1,0:T(8,128)(2,1)S(1)} %get-tuple-element.31), channel_id=1, source_target_pairs={{2,0},{4,2},{6,4},{8,6},{10,8},{12,10},{14,12},{16,14},{18,16},{20... | collective-permute-start | bytes 811016 | tf_op jit(solution)/shard_map/ppermute | solution.py:24
  16.6 8.5 %collective-permute-start.4 = (bf16[22,32,128]{2,1,0:T(8,128)(2,1)S(1)}, bf16[22,32,128]{2,1,0:T(8,128)(2,1)S(1)}, u32[]{:S(2)}, u32[]{:S(2)}) collective-permute-start(bf16[22,32,128]{2,1,0:T(8,128)(2,1)S(1)} %get-tuple-element.32), channel_id=1, source_target_pairs={{0,2},{2,4},{4,6},{6,8},{8,10},{10,12},{12,14},{14,16},{16,18},{18... | collective-permute-start | bytes 540680 | tf_op jit(solution)/shard_map/ppermute | solution.py:23
  17.9 7.2 %collective-permute-start.5 = (bf16[22,32,128]{2,1,0:T(8,128)(2,1)S(1)}, bf16[22,32,128]{2,1,0:T(8,128)(2,1)S(1)}, u32[]{:S(2)}, u32[]{:S(2)}) collective-permute-start(bf16[22,32,128]{2,1,0:T(8,128)(2,1)S(1)} %get-tuple-element.33), channel_id=1, source_target_pairs={{2,0},{4,2},{6,4},{8,6},{10,8},{12,10},{14,12},{16,14},{18,16},{20... | collective-permute-start | bytes 540680 | tf_op jit(solution)/shard_map/ppermute | solution.py:24
  49.8 4.1 %collective-permute-start.6 = (bf16[3456,128]{1,0:T(8,128)(2,1)S(1)}, bf16[3456,128]{1,0:T(8,128)(2,1)S(1)}, u32[]{:S(2)}, u32[]{:S(2)}) collective-permute-start(bf16[3456,128]{1,0:T(8,128)(2,1)S(1)} %slice_bitcast_fusion), channel_id=1, source_target_pairs={{0,1},{1,0},{2,3},{3,2},{4,5},{5,4},{6,7},{7,6},{8,9},{9,8},{10,11... | collective-permute-start | bytes 2654216 | tf_op jit(solution)/shard_map/ppermute | solution.py:418
  55.0 21.0 %all-to-all-start = ((bf16[16,216,128]{2,1,0:T(8,128)(2,1)}), bf16[16,216,128]{2,1,0:T(8,128)(2,1)S(1)}, u32[]{:S(2)}, u32[]{:S(2)}) async-start(bf16[16,216,128]{2,1,0:T(8,128)(2,1)} %bitcast.10), calls=%async_computation | async-start | bytes 1769472 | tf_op jit(solution)/shard_map/all_to_all | solution.py:423
  61.5 14.7 %collective-permute-start.7 = (bf16[8,32,128]{2,1,0:T(8,128)(2,1)S(1)}, bf16[8,32,128]{2,1,0:T(8,128)(2,1)S(1)}, u32[]{:S(2)}, u32[]{:S(2)}) collective-permute-start(bf16[8,32,128]{2,1,0:T(8,128)(2,1)S(1)} %get-tuple-element.37), channel_id=1, source_target_pairs={{0,32},{32,64},{64,96},{96,128},{128,160},{160,192},{192,224},{224... | collective-permute-start | bytes 196616 | tf_op jit(solution)/shard_map/ppermute | solution.py:23
  61.6 14.6 %collective-permute-start.8 = (bf16[8,32,128]{2,1,0:T(8,128)(2,1)S(1)}, bf16[8,32,128]{2,1,0:T(8,128)(2,1)S(1)}, u32[]{:S(2)}, u32[]{:S(2)}) collective-permute-start(bf16[8,32,128]{2,1,0:T(8,128)(2,1)S(1)} %get-tuple-element.38), channel_id=1, source_target_pairs={{32,0},{64,32},{96,64},{128,96},{160,128},{192,160},{224,192},{0,2... | collective-permute-start | bytes 196616 | tf_op jit(solution)/shard_map/ppermute | solution.py:24
  76.2 3.1 %collective-permute-start.9 = (bf16[216,128]{1,0:T(8,128)(2,1)S(1)}, bf16[216,128]{1,0:T(8,128)(2,1)S(1)}, u32[]{:S(2)}, u32[]{:S(2)}) collective-permute-start(bf16[216,128]{1,0:T(8,128)(2,1)S(1)} %reduce_sum.12), channel_id=1, source_target_pairs={{0,32},{32,0},{64,96},{96,64},{128,160},{160,128},{192,224},{224,1... | collective-permute-start | bytes 165896 | tf_op jit(solution)/shard_map/ppermute | solution.py:431
  79.3 5.7 %collective-permute-start.10 = (bf16[216,128]{1,0:T(8,128)(2,1)S(1)}, bf16[216,128]{1,0:T(8,128)(2,1)S(1)}, u32[]{:S(2)}, u32[]{:S(2)}) collective-permute-start(bf16[216,128]{1,0:T(8,128)(2,1)S(1)} %add_convert_fusion.2), channel_id=1, source_target_pairs={{0,96},{32,64},{64,32},{96,0},{128,224},{160,192},{192,160},{224,1... | collective-permute-start | bytes 165896 | tf_op jit(solution)/shard_map/ppermute | solution.py:431
  85.1 15.7 %copy-start.1 = (bf16[27,128,128]{2,1,0:T(8,128)(2,1)S(1)}, bf16[27,128,128]{2,1,0:T(8,128)(2,1)}, u32[]{:S(2)}) copy-start(bf16[27,128,128]{2,1,0:T(8,128)(2,1)} %param.8) | copy-start | bytes 2654212
  85.1 6.6 %collective-permute-start.11 = (bf16[216,128]{1,0:T(8,128)(2,1)S(1)}, bf16[216,128]{1,0:T(8,128)(2,1)S(1)}, u32[]{:S(2)}, u32[]{:S(2)}) collective-permute-start(bf16[216,128]{1,0:T(8,128)(2,1)S(1)} %add_convert_fusion.1), channel_id=1, source_target_pairs={{0,224},{32,192},{64,160},{96,128},{128,96},{160,64},{192,32},{224... | collective-permute-start | bytes 165896 | tf_op jit(solution)/shard_map/ppermute | solution.py:431
  86.8 6.7 %collective-permute-start.12 = (bf16[10,32,128]{2,1,0:T(8,128)(2,1)S(1)}, bf16[10,32,128]{2,1,0:T(8,128)(2,1)S(1)}, u32[]{:S(2)}, u32[]{:S(2)}) collective-permute-start(bf16[10,32,128]{2,1,0:T(8,128)(2,1)S(1)} %get-tuple-element.43), channel_id=1, source_target_pairs={{0,2},{2,4},{4,6},{6,8},{8,10},{10,12},{12,14},{14,16},{16,18},{18... | collective-permute-start | bytes 245768 | tf_op jit(solution)/shard_map/ppermute | solution.py:23
  87.3 6.3 %collective-permute-start.13 = (bf16[10,32,128]{2,1,0:T(8,128)(2,1)S(1)}, bf16[10,32,128]{2,1,0:T(8,128)(2,1)S(1)}, u32[]{:S(2)}, u32[]{:S(2)}) collective-permute-start(bf16[10,32,128]{2,1,0:T(8,128)(2,1)S(1)} %get-tuple-element.44), channel_id=1, source_target_pairs={{2,0},{4,2},{6,4},{8,6},{10,8},{12,10},{14,12},{16,14},{18,16},{20... | collective-permute-start | bytes 245768 | tf_op jit(solution)/shard_map/ppermute | solution.py:24
  94.6 17.4 %all-to-all-start.1 = ((bf16[16,216,128]{2,1,0:T(8,128)(2,1)}), bf16[16,216,128]{2,1,0:T(8,128)(2,1)S(1)}, u32[]{:S(2)}, u32[]{:S(2)}) async-start(bf16[16,216,128]{2,1,0:T(8,128)(2,1)} %broadcast_in_dim.2), calls=%async_computation.1 | async-start | bytes 1769472 | tf_op jit(solution)/shard_map/all_to_all | solution.py:440
  111.9 9.3 %collective-permute-start.14 = (bf16[27,128,128]{2,1,0:T(8,128)(2,1)S(1)}, bf16[27,128,128]{2,1,0:T(8,128)(2,1)S(1)}, u32[]{:S(2)}, u32[]{:S(2)}) collective-permute-start(bf16[27,128,128]{2,1,0:T(8,128)(2,1)S(1)} %bitcast.21), channel_id=1, source_target_pairs={{0,1},{1,0},{2,3},{3,2},{4,5},{5,4},{6,7},{7,6},{8,9},{9,8},{10,11... | collective-permute-start | bytes 2654216 | tf_op jit(solution)/shard_map/ppermute | solution.py:418
